TPU v7x, 32 devices: a whole 2x2x4 slice. The times are simulated.
32 devices in a mesh: rep: 4 (over z), shard: 8 (over y, x, core).
Axes of the slice: x: 2, y: 2, z: 4, core: 2. Of those that a mesh axis runs over, the one named last changes fastest.
Arguments:
- block_input: bfloat16 [32, 128, 2048], P(('rep', 'shard')), may hold values from -6 to 6
- lengths: int32 [32], P(('rep', 'shard')), may hold values from 32 to 128, as said below
- first_gain: bfloat16 [2048], P('shard'), may hold values from 0.5 to 1.5
- first_shift: bfloat16 [2048], P('shard'), may hold values from -1 to 1
- query_weight: bfloat16 [2048, 2048], P('shard'), may hold values from -0.25 to 0.25
- query_bias: bfloat16 [2048], P('shard'), may hold values from -1.5 to 1.5
- key_weight: bfloat16 [2048, 2048], P('shard'), may hold values from -0.125 to 0.125
- value_weight: bfloat16 [2048, 2048], P('shard'), may hold values from -0.125 to 0.125
- value_bias: bfloat16 [2048], P('shard'), may hold values from -1.5 to 1.5
- out_weight: bfloat16 [2048, 2048], P('shard'), may hold values from -0.75 to 0.75
- out_bias: bfloat16 [2048], P('shard'), may hold values from -1.5 to 1.5
- second_gain: bfloat16 [2048], P('shard'), may hold values from 0.5 to 1.5
- second_shift: bfloat16 [2048], P('shard'), may hold values from -1 to 1
- up_weight: bfloat16 [2048, 8192], P('shard'), may hold values from -0.125 to 0.125
- up_bias: bfloat16 [8192], P('shard'), may hold values from -1.5 to 1.5
- down_weight: bfloat16 [8192, 2048], P('shard'), may hold values from -0.125 to 0.125
- down_bias: bfloat16 [2048], P('shard'), may hold values from -1.5 to 1.5
- cotangent: bfloat16 [32, 128, 2048], P(('rep', 'shard')), may hold values from -6 to 6
Outputs:
- block_output: bfloat16 [32, 128, 2048], P(('rep', 'shard'))
- input_grad: bfloat16 [32, 128, 2048], P(('rep', 'shard'))
- first_gain_grad: float32 [2048], P('shard')
- first_shift_grad: float32 [2048], P('shard')
- query_weight_grad: float32 [2048, 2048], P('shard')
- query_bias_grad: float32 [2048], P('shard')
- key_weight_grad: float32 [2048, 2048], P('shard')
- value_weight_grad: float32 [2048, 2048], P('shard')
- value_bias_grad: float32 [2048], P('shard')
- out_weight_grad: float32 [2048, 2048], P('shard')
- out_bias_grad: float32 [2048], P('shard')
- second_gain_grad: float32 [2048], P('shard')
- second_shift_grad: float32 [2048], P('shard')
- up_weight_grad: float32 [2048, 8192], P('shard')
- up_bias_grad: float32 [8192], P('shard')
- down_weight_grad: float32 [8192, 2048], P('shard')
- down_bias_grad: float32 [2048], P('shard')
Inputs may be any that keep to these rules, and one draw needn't show every extreme that they name: `lengths`: one sequence has exactly 128 live slots and one exactly 32.
All inputs are finite; a program needn't handle non-finite values.
Results may differ from a plain program's by a relative error of at most 0.019.
Values may be sent and summed in bfloat16 or wider, within the bound.
A program may use at most 768 MiB of HBM per device.

v0:
```python
import math

import jax
import jax.numpy as jnp
from jax import lax
from jax.sharding import PartitionSpec as P

HEADS = 16


def layer_norm(values, gain, shift):
    center = values - jnp.mean(values, axis=-1, keepdims=True)
    spread = jnp.mean(center * center, axis=-1, keepdims=True)
    return center * lax.rsqrt(spread + 1e-05) * gain + shift


def exact_gelu(values):
    return jax.nn.gelu(values, approximate=False)


def masked_scores(query_block, key_heads, start, length, scale):
    rows_here = query_block.shape[0]
    scores = (
        jnp.einsum("qhd,khd->hqk", query_block, key_heads, preferred_element_type=jnp.float32)
        * scale
    )
    query_pos = start + jnp.arange(rows_here, dtype=jnp.int32)
    key_pos = jnp.arange(key_heads.shape[0], dtype=jnp.int32)
    valid = (key_pos[None, :] <= query_pos[:, None]) & (key_pos[None, :] < length)
    return jnp.where(valid[None], scores, -1e30)


def attend_forward(query_heads, key_heads, value_heads, length, scale, block_rows):
    count = query_heads.shape[0] // block_rows
    blocks = query_heads.reshape(count, block_rows, query_heads.shape[1], query_heads.shape[2])
    starts = jnp.arange(count, dtype=jnp.int32) * block_rows

    def one_block(item):
        query_block, start = item
        scores = masked_scores(query_block, key_heads, start, length, scale)
        top = jnp.max(scores, axis=-1, keepdims=True)
        expo = jnp.exp(scores - top)
        total = jnp.sum(expo, axis=-1, keepdims=True)
        weights = (expo / total).astype(jnp.bfloat16)
        context = jnp.einsum(
            "hqk,khd->qhd", weights, value_heads, preferred_element_type=jnp.float32
        )
        return (context, (top + jnp.log(total))[..., 0])

    contexts, logsum = lax.map(one_block, (blocks, starts))
    return (contexts.reshape(query_heads.shape), logsum)


def attend_backward(
    query_heads, key_heads, value_heads, grad_heads, logsum, length, scale, block_rows
):
    count = query_heads.shape[0] // block_rows
    shape_block = (count, block_rows, query_heads.shape[1], query_heads.shape[2])
    blocks = query_heads.reshape(shape_block)
    grad_blocks = grad_heads.reshape(shape_block)
    starts = jnp.arange(count, dtype=jnp.int32) * block_rows

    def one_block(carry, item):
        key_total, value_total = carry
        query_block, grad_block, block_logsum, start = item
        scores = masked_scores(query_block, key_heads, start, length, scale)
        weights = jnp.exp(scores - block_logsum[..., None])
        weights_low = weights.astype(jnp.bfloat16)
        grad_weights = jnp.einsum(
            "qhd,khd->hqk", grad_block, value_heads, preferred_element_type=jnp.float32
        )
        inner = jnp.sum(weights * grad_weights, axis=-1, keepdims=True)
        grad_scores = (weights * (grad_weights - inner)).astype(jnp.bfloat16)
        grad_query = (
            jnp.einsum("hqk,khd->qhd", grad_scores, key_heads, preferred_element_type=jnp.float32)
            * scale
        )
        key_total = (
            key_total
            + jnp.einsum(
                "hqk,qhd->khd", grad_scores, query_block, preferred_element_type=jnp.float32
            )
            * scale
        )
        value_total = value_total + jnp.einsum(
            "hqk,qhd->khd", weights_low, grad_block, preferred_element_type=jnp.float32
        )
        return ((key_total, value_total), grad_query)

    zero_heads = jnp.zeros(key_heads.shape, jnp.float32)
    (key_total, value_total), grad_queries = lax.scan(
        one_block, (zero_heads, zero_heads), (blocks, grad_blocks, logsum, starts)
    )
    return (grad_queries.reshape(query_heads.shape), key_total, value_total)


def small_block(columns, extra, width):
    stacked = jnp.stack(columns, axis=1)
    filler = jnp.zeros((width, 128 - stacked.shape[1] - extra.shape[1]), jnp.float32)
    return jnp.concatenate([stacked, extra, filler], axis=1)


def column_grad(left, right):
    return jnp.einsum("tr,tc->rc", left, right, preferred_element_type=jnp.float32)


def local(
    block_input,
    lengths,
    first_gain,
    first_shift,
    query_weight,
    query_bias,
    key_weight,
    value_weight,
    value_bias,
    out_weight,
    out_bias,
    second_gain,
    second_shift,
    up_weight,
    up_bias,
    down_weight,
    down_bias,
    cotangent,
):
    seq_len = block_input.shape[1]
    width = block_input.shape[2]
    hidden = up_weight.shape[1]
    head_size = width // HEADS
    block_rows = min(seq_len, 512)
    scale = 1.0 / math.sqrt(head_size)
    groups = lax.axis_size("shard")
    rows_dev = width // groups
    attn_set = (
        lax.all_gather(first_gain, "shard", axis=0, tiled=True),
        lax.all_gather(first_shift, "shard", axis=0, tiled=True),
        lax.all_gather(query_weight, "shard", axis=0, tiled=True),
        lax.all_gather(query_bias, "shard", axis=0, tiled=True),
        lax.all_gather(key_weight, "shard", axis=0, tiled=True),
        lax.all_gather(value_weight, "shard", axis=0, tiled=True),
        lax.all_gather(value_bias, "shard", axis=0, tiled=True),
    )
    gain_one, shift_one, query_full, query_shift, key_full, value_full, value_shift = attn_set
    block = block_input[0].astype(jnp.float32)
    length = lengths[0]
    positions = jnp.arange(seq_len, dtype=jnp.int32)
    live = (positions < length).astype(jnp.float32)[:, None]
    normed_low = layer_norm(
        block, gain_one.astype(jnp.float32), shift_one.astype(jnp.float32)
    ).astype(jnp.bfloat16)
    queries = (
        jnp.dot(normed_low, query_full, preferred_element_type=jnp.float32)
        + query_shift.astype(jnp.float32)
    ).astype(jnp.bfloat16)
    keys_low = jnp.dot(normed_low, key_full, preferred_element_type=jnp.float32).astype(
        jnp.bfloat16
    )
    values_low = (
        jnp.dot(normed_low, value_full, preferred_element_type=jnp.float32)
        + value_shift.astype(jnp.float32)
    ).astype(jnp.bfloat16)
    head_shape = (seq_len, HEADS, head_size)
    query_heads = queries.reshape(head_shape)
    key_heads = keys_low.reshape(head_shape)
    value_heads = values_low.reshape(head_shape)
    contexts, logsum = attend_forward(
        query_heads, key_heads, value_heads, length, scale, block_rows
    )
    context_low = contexts.reshape(seq_len, width).astype(jnp.bfloat16)
    ffn_set = (
        lax.all_gather(out_weight, "shard", axis=0, tiled=True),
        lax.all_gather(out_bias, "shard", axis=0, tiled=True),
        lax.all_gather(second_gain, "shard", axis=0, tiled=True),
        lax.all_gather(second_shift, "shard", axis=0, tiled=True),
        lax.all_gather(up_weight, "shard", axis=0, tiled=True),
        lax.all_gather(up_bias, "shard", axis=0, tiled=True),
        lax.all_gather(down_weight, "shard", axis=0, tiled=True),
        lax.all_gather(down_bias, "shard", axis=0, tiled=True),
    )
    out_full, out_shift, gain_two, shift_two, up_full, up_shift, down_full, down_shift = ffn_set
    branch = jnp.dot(context_low, out_full, preferred_element_type=jnp.float32) + out_shift.astype(
        jnp.float32
    )
    middle = block + branch
    second_low = layer_norm(
        middle, gain_two.astype(jnp.float32), shift_two.astype(jnp.float32)
    ).astype(jnp.bfloat16)
    upper = jnp.dot(second_low, up_full, preferred_element_type=jnp.float32) + up_shift.astype(
        jnp.float32
    )
    active_low = exact_gelu(upper).astype(jnp.bfloat16)
    mixed = jnp.dot(active_low, down_full, preferred_element_type=jnp.float32) + down_shift.astype(
        jnp.float32
    )
    block_output = ((middle + mixed) * live).astype(jnp.bfloat16)[None]
    ffn_back = (
        lax.all_gather(out_weight, "shard", axis=0, tiled=True),
        lax.all_gather(out_bias, "shard", axis=0, tiled=True),
        lax.all_gather(second_gain, "shard", axis=0, tiled=True),
        lax.all_gather(second_shift, "shard", axis=0, tiled=True),
        lax.all_gather(up_weight, "shard", axis=0, tiled=True),
        lax.all_gather(up_bias, "shard", axis=0, tiled=True),
        lax.all_gather(down_weight, "shard", axis=0, tiled=True),
        lax.all_gather(down_bias, "shard", axis=0, tiled=True),
    )
    out_full, out_shift, gain_two, shift_two, up_full, up_shift, down_full, down_shift = ffn_back
    grad_out = cotangent[0].astype(jnp.float32) * live
    grad_mixed = grad_out.astype(jnp.bfloat16)
    grad_active = jnp.einsum("tc,fc->tf", grad_mixed, down_full, preferred_element_type=jnp.float32)
    unused_gelu, gelu_pull = jax.vjp(exact_gelu, upper)
    grad_upper = gelu_pull(grad_active)[0].astype(jnp.bfloat16)
    grad_second = jnp.einsum("tf,cf->tc", grad_upper, up_full, preferred_element_type=jnp.float32)
    unused_norm, norm_pull = jax.vjp(
        layer_norm, middle, gain_two.astype(jnp.float32), shift_two.astype(jnp.float32)
    )
    grad_middle_norm, second_gain_total, second_shift_total = norm_pull(grad_second)
    grad_middle = grad_out + grad_middle_norm
    grad_branch = grad_middle.astype(jnp.bfloat16)
    ffn_small = small_block(
        [
            jnp.sum(grad_branch.astype(jnp.float32), axis=0),
            second_gain_total,
            second_shift_total,
            jnp.sum(grad_mixed.astype(jnp.float32), axis=0),
        ],
        jnp.sum(grad_upper.astype(jnp.float32), axis=0).reshape(width, 4),
        width,
    )
    out_part = column_grad(context_low, grad_branch)
    up_part = column_grad(second_low, grad_upper)
    down_part = column_grad(active_low, grad_mixed).reshape(
        rows_dev * lax.axis_size("shard"), 4 * width
    )
    small_part = ffn_small
    ffn_shard = lax.psum_scatter(
        jnp.concatenate([out_part, up_part, down_part, small_part], axis=1).astype(jnp.bfloat16),
        "shard",
        scatter_dimension=0,
        tiled=True,
    ).astype(jnp.float32)
    grad_context = jnp.einsum(
        "tc,rc->tr", grad_branch, out_full, preferred_element_type=jnp.float32
    ).astype(jnp.bfloat16)
    grad_queries, key_total, value_total = attend_backward(
        query_heads,
        key_heads,
        value_heads,
        grad_context.reshape(head_shape),
        logsum,
        length,
        scale,
        block_rows,
    )
    grad_query = grad_queries.reshape(seq_len, width).astype(jnp.bfloat16)
    grad_key = key_total.reshape(seq_len, width).astype(jnp.bfloat16)
    grad_value = value_total.reshape(seq_len, width).astype(jnp.bfloat16)
    attn_back = (
        lax.all_gather(first_gain, "shard", axis=0, tiled=True),
        lax.all_gather(first_shift, "shard", axis=0, tiled=True),
        lax.all_gather(query_weight, "shard", axis=0, tiled=True),
        lax.all_gather(query_bias, "shard", axis=0, tiled=True),
        lax.all_gather(key_weight, "shard", axis=0, tiled=True),
        lax.all_gather(value_weight, "shard", axis=0, tiled=True),
        lax.all_gather(value_bias, "shard", axis=0, tiled=True),
    )
    gain_one, shift_one, query_full, query_shift, key_full, value_full, value_shift = attn_back
    grad_normed = jnp.einsum(
        "tr,cr->tc", grad_query, query_full, preferred_element_type=jnp.float32
    )
    grad_normed = grad_normed + jnp.einsum(
        "tr,cr->tc", grad_key, key_full, preferred_element_type=jnp.float32
    )
    grad_normed = grad_normed + jnp.einsum(
        "tr,cr->tc", grad_value, value_full, preferred_element_type=jnp.float32
    )
    unused_first, first_pull = jax.vjp(
        layer_norm, block, gain_one.astype(jnp.float32), shift_one.astype(jnp.float32)
    )
    grad_block_norm, first_gain_total, first_shift_total = first_pull(grad_normed)
    input_grad = (grad_middle + grad_block_norm).astype(jnp.bfloat16)[None]
    attn_small = small_block(
        [
            first_gain_total,
            first_shift_total,
            jnp.sum(grad_query.astype(jnp.float32), axis=0),
            jnp.sum(grad_value.astype(jnp.float32), axis=0),
        ],
        jnp.zeros((width, 0), jnp.float32),
        width,
    )
    query_part = column_grad(normed_low, grad_query)
    key_part = column_grad(normed_low, grad_key)
    value_part = column_grad(normed_low, grad_value)
    small_part = attn_small
    attn_shard = lax.psum_scatter(
        jnp.concatenate([query_part, key_part, value_part, small_part], axis=1).astype(
            jnp.bfloat16
        ),
        "shard",
        scatter_dimension=0,
        tiled=True,
    ).astype(jnp.float32)
    ffn_shard, attn_shard = (
        lax.psum(ffn_shard.astype(jnp.bfloat16), "rep").astype(jnp.float32),
        lax.psum(attn_shard.astype(jnp.bfloat16), "rep").astype(jnp.float32),
    )
    out_weight_grad = ffn_shard[:, :width]
    up_weight_grad = ffn_shard[:, width : width + hidden]
    down_weight_grad = ffn_shard[:, width + hidden : width + 2 * hidden].reshape(-1, width)
    ffn_tail = ffn_shard[:, width + 2 * hidden :]
    query_weight_grad = attn_shard[:, :width]
    key_weight_grad = attn_shard[:, width : 2 * width]
    value_weight_grad = attn_shard[:, 2 * width : 3 * width]
    attn_tail = attn_shard[:, 3 * width :]
    return (
        block_output,
        input_grad,
        attn_tail[:, 0],
        attn_tail[:, 1],
        query_weight_grad,
        attn_tail[:, 2],
        key_weight_grad,
        value_weight_grad,
        attn_tail[:, 3],
        out_weight_grad,
        ffn_tail[:, 0],
        ffn_tail[:, 1],
        ffn_tail[:, 2],
        up_weight_grad,
        ffn_tail[:, 4:8].reshape(-1),
        down_weight_grad,
        ffn_tail[:, 3],
    )


def solution(mesh):
    return jax.shard_map(
        local,
        mesh=mesh,
        in_specs=(
            P(("rep", "shard"), None, None),
            P(("rep", "shard")),
            P("shard"),
            P("shard"),
            P("shard", None),
            P("shard"),
            P("shard", None),
            P("shard", None),
            P("shard"),
            P("shard", None),
            P("shard"),
            P("shard"),
            P("shard"),
            P("shard", None),
            P("shard"),
            P("shard", None),
            P("shard"),
            P(("rep", "shard"), None, None),
        ),
        out_specs=(
            P(("rep", "shard"), None, None),
            P(("rep", "shard"), None, None),
            P("shard"),
            P("shard"),
            P("shard", None),
            P("shard"),
            P("shard", None),
            P("shard", None),
            P("shard"),
            P("shard", None),
            P("shard"),
            P("shard"),
            P("shard"),
            P("shard", None),
            P("shard"),
            P("shard", None),
            P("shard"),
        ),
        check_vma=False,
    )
```

profile of v0, /device:TPU:0, one launch (start us, length us, event | category | flops | bytes accessed | tf_op | source)
XLA Modules:
  0.0 1951.0 jit_solution(7732753283931812263)
XLA Ops:
  12.1 10.3 all-gather.6
  22.4 8.9 all-gather.5
  39.3 8.9 all-gather.2
  73.0 8.9 all_gather.65
  87.5 36.0 %all-gather.19.cloned.1.call-done = bf16[2048,2048]{1,0:T(8,128)(2,1)} async-done(((bf16[256,2048]{1,0:T(8,128)(2,1)}), bf16[2048,2048]{1,0:T(8,128)(2,1)}) %all-gather.19.cloned.1.call-update) | async-done | bytes 8388624 | tf_op jit(solution)/shard_map/all_gather | solution.py:140
  129.0 50.8 %all-gather.15.cloned.1.call-done = bf16[2048,2048]{1,0:T(8,128)(2,1)} async-done(((bf16[256,2048]{1,0:T(8,128)(2,1)}), bf16[2048,2048]{1,0:T(8,128)(2,1)}) %all-gather.15.cloned.1.call-update) | async-done | bytes 8388624 | tf_op jit(solution)/shard_map/all_gather | solution.py:141
  185.0 51.0 %all-gather.21.cloned.1.call-done = bf16[2048,2048]{1,0:T(8,128)(2,1)} async-done(((bf16[256,2048]{1,0:T(8,128)(2,1)}), bf16[2048,2048]{1,0:T(8,128)(2,1)}) %all-gather.21.cloned.1.call-update) | async-done | bytes 8388624 | tf_op jit(solution)/shard_map/all_gather | solution.py:172
  241.0 157.5 %all-gather.23.cloned.1.call-done = bf16[2048,8192]{1,0:T(8,128)(2,1)} async-done(((bf16[256,8192]{1,0:T(8,128)(2,1)}), bf16[2048,8192]{1,0:T(8,128)(2,1)}) %all-gather.23.cloned.1.call-update) | async-done | bytes 33554448 | tf_op jit(solution)/shard_map/all_gather | solution.py:176
  398.5 22.5 %multiply_convert_fusion = (bf16[128,8192]{1,0:T(8,128)(2,1)}, f32[128,8192]{1,0:T(8,128)}, f32[128,8192]{1,0:T(8,128)}) fusion(f32[8192]{0:T(1024)S(1)} %convert_element_type.197, bf16[2048,8192]{1,0:T(8,128)(2,1)} %all-gather.23.cloned.1.call-done, f32[128,2048]{1,0:T(8,128)S(1)} %get-tuple-element.151, f32[2048]{0:T(1024)S(1)} %bitcast.177, ...), kind=kOutput, calls=%fused_computation.10 | convolution fusion | flops 4365484032 | bytes 45138944 | tf_op jit(solution)/shard_map/dot_general | solution.py:189
  421.0 140.1 %all-gather.25.cloned.1.call-done = bf16[8192,2048]{1,0:T(8,128)(2,1)} async-done(((bf16[1024,2048]{1,0:T(8,128)(2,1)}), bf16[8192,2048]{1,0:T(8,128)(2,1)}) %all-gather.25.cloned.1.call-update) | async-done | bytes 33554448 | tf_op jit(solution)/shard_map/all_gather | solution.py:178
  561.1 19.3 fusion.79
  580.4 19.5 multiply_reduce_fusion
  645.2 108.5 %concatenate.8 = bf16[2048,6272]{0,1:T(8,128)(2,1)} concatenate(bf16[2048,2048]{0,1:T(8,128)(2,1)} %convolution_convert_fusion.4, bf16[2048,2048]{0,1:T(8,128)(2,1)} %convolution_convert_fusion.3, bf16[2048,2048]{0,1:T(8,128)(2,1)} %convolution_convert_fusion.2, bf16[2048,1]{0,1:T(2,128)(2,1)S(1)} %stack.32, bf16[2048,1]{0,1:T(2,128)(2,1)S(1)} %stack.33, ...), dimensions={1} | concatenate | bytes 51380224 | tf_op jit(solution)/shard_map/concatenate | solution.py:297
  768.7 13.4 copy.93
  782.1 16.3 convolution_convert_fusion.1
  798.4 55.9 %reshape.282 = bf16[2048,8192]{1,0:T(8,128)(2,1)} reshape(bf16[8192,2048]{1,0:T(8,128)(2,1)} %convolution_convert_fusion.1) | data formatting | bytes 67108864 | tf_op jit(solution)/shard_map/reshape | solution.py:232
  854.3 15.6 convolution_convert_fusion
  870.7 162.6 %concatenate.9 = bf16[2048,18560]{1,0:T(8,128)(2,1)} concatenate(bf16[2048,2048]{1,0:T(8,128)(2,1)} %copy.93, bf16[2048,8192]{1,0:T(8,128)(2,1)} %convolution_convert_fusion, bf16[2048,8192]{1,0:T(8,128)(2,1)} %reshape.282, bf16[2048,1]{1,0:T(8,128)(2,1)} %stack.40, bf16[2048,1]{1,0:T(8,128)(2,1)} %stack.41, bf16[2048,1]{1,0:T(8,128)(2,1)} %stack.42, bf16[2048,1]{1,0:T(8,128)(2,1)} %stack.43, ...), dimensions={1} | concatenate | bytes 152043520 | tf_op jit(solution)/shard_map/concatenate | solution.py:237
  1033.4 426.6 %reduce-scatter.5.cloned.1.call-done = bf16[256,18560]{1,0:T(8,128)(2,1)} async-done(((bf16[2048,18560]{1,0:T(8,128)(2,1)}), bf16[256,18560]{1,0:T(8,128)(2,1)}) %reduce-scatter.5.cloned.1.call-update) | async-done | bytes 9502736 | tf_op jit(solution)/shard_map/reduce_scatter | solution.py:236
  1472.2 14.3 fusion.12
  1486.5 407.2 %all-reduce.3.cloned.1.call-done = (bf16[256,6272]{0,1:T(8,128)(2,1)}, bf16[256,18560]{1,0:T(8,128)(2,1)}) async-done(((bf16[256,6272]{0,1:T(8,128)(2,1)}, bf16[256,18560]{1,0:T(8,128)(2,1)}), (bf16[256,6272]{0,1:T(8,128)(2,1)}, bf16[256,18560]{1,0:T(8,128)(2,1)})) %all-reduce.3.cloned.1.call-update) | async-done | bytes 12714000 | tf_op jit(solution)/shard_map/psum | solution.py:306
  1900.7 11.8 fusion.73
  1912.5 11.5 convert_element_type.228
  1932.3 9.8 reshape.285
  (170 shorter events, 148.5 us)
Async XLA Ops:
  7.2 75.3 %all-gather.17.cloned.1.call-start = ((), (), s32[]{:S(2)}) async-start(), calls=%async_computation.3 | async-start | bytes 9437184 | tf_op jit(solution)/shard_map/all_gather | solution.py:138
  7.9 115.5 %all-gather.19.cloned.1.call-start = ((), (), s32[]{:S(2)}) async-start(), calls=%async_computation.4 | async-start | bytes 9437184 | tf_op jit(solution)/shard_map/all_gather | solution.py:140
  8.7 171.1 %all-gather.15.cloned.1.call-start = ((), (), s32[]{:S(2)}) async-start(), calls=%async_computation.2 | async-start | bytes 9437184 | tf_op jit(solution)/shard_map/all_gather | solution.py:141
  9.4 226.5 %all-gather.21.cloned.1.call-start = ((), (), s32[]{:S(2)}) async-start(), calls=%async_computation.5 | async-start | bytes 9437184 | tf_op jit(solution)/shard_map/all_gather | solution.py:172
  10.1 62.9 %copy-start.14 = (bf16[1024]{0:T(1024)(128)(2,1)S(1)}, bf16[1024]{0:T(1024)(128)(2,1)}, u32[]{:S(2)}) copy-start(bf16[1024]{0:T(1024)(128)(2,1)} %param.32) | copy-start | bytes 6148
  10.1 71.8 %copy-start = (bf16[1,128,2048]{2,1,0:T(8,128)(2,1)S(1)}, bf16[1,128,2048]{2,1,0:T(8,128)(2,1)}, u32[]{:S(2)}) copy-start(bf16[1,128,2048]{2,1,0:T(8,128)(2,1)} %param.18) | copy-start | bytes 1572868
  10.1 388.4 %all-gather.23.cloned.1.call-start = ((), (), s32[]{:S(2)}) async-start(), calls=%async_computation.6 | async-start | bytes 37748736 | tf_op jit(solution)/shard_map/all_gather | solution.py:176
  10.7 550.4 %all-gather.25.cloned.1.call-start = ((), (), s32[]{:S(2)}) async-start(), calls=%async_computation.7 | async-start | bytes 37748736 | tf_op jit(solution)/shard_map/all_gather | solution.py:178
  11.2 1022.2 %reduce-scatter.3.cloned.1.call-start = ((), (), s32[]{:S(2)}) async-start(), calls=%async_computation.8 | async-start | bytes 28901376 | tf_op jit(solution)/shard_map/reduce_scatter | solution.py:296
  87.5 41.0 %copy-start.9 = (bf16[128,2048]{0,1:T(8,128)(2,1)}, bf16[128,2048]{0,1:T(8,128)(2,1)S(1)}, u32[]{:S(2)}) copy-start(bf16[128,2048]{0,1:T(8,128)(2,1)S(1)} %copy.107) | copy-start | bytes 1572868
  128.4 56.1 %copy-start.11 = (bf16[128,2048]{0,1:T(8,128)(2,1)}, bf16[128,2048]{0,1:T(8,128)(2,1)S(1)}, u32[]{:S(2)}) copy-start(bf16[128,2048]{0,1:T(8,128)(2,1)S(1)} %copy.108) | copy-start | bytes 1572868
  184.5 51.4 %copy-start.13 = (bf16[16,16,8,128]{3,2,1,0:T(8,128)(2,1)}, bf16[16,16,8,128]{3,2,1,0:T(8,128)(2,1)S(1)}, u32[]{:S(2)}) copy-start(bf16[16,16,8,128]{3,2,1,0:T(8,128)(2,1)S(1)} %fusion.21) | copy-start | bytes 1572868
  185.0 55.7 %copy-start.4 = (bf16[16,128,128]{2,1,0:T(8,128)(2,1)}, bf16[16,128,128]{2,1,0:T(8,128)(2,1)S(1)}, u32[]{:S(2)}) copy-start(bf16[16,128,128]{2,1,0:T(8,128)(2,1)S(1)} %convolution_convert_fusion.9) | copy-start | bytes 1572868
  398.5 162.6 %copy-start.6 = (bf16[1,128,2048]{2,1,0:T(8,128)(2,1)S(1)}, bf16[1,128,2048]{2,1,0:T(8,128)(2,1)}, u32[]{:S(2)}) copy-start(bf16[1,128,2048]{2,1,0:T(8,128)(2,1)} %param.35) | copy-start | bytes 1572868
  601.5 8.4 copy-start.15
  623.6 11.9 slice-start
  623.6 14.8 slice-start.4
  629.4 9.0 slice-start.5
  753.7 6.5 copy-start.5
  753.7 706.3 %reduce-scatter.5.cloned.1.call-start = ((), (), s32[]{:S(2)}) async-start(), calls=%async_computation.9 | async-start | bytes 85524480 | tf_op jit(solution)/shard_map/reduce_scatter | solution.py:236
  768.7 13.4 copy-start.7
  1033.4 860.3 %all-reduce.3.cloned.1.call-start = ((), (), s32[]{:S(2)}) async-start(), calls=%async_computation.10 | async-start | bytes 25427968 | tf_op jit(solution)/shard_map/psum | solution.py:306
  1460.0 9.6 copy-start.16
  1460.7 11.5 copy-start.2
  (16 other events, 41.0 us)
Sparse Core Ops, SparseCore 0:
  9.9 57.1 all-gather.16
  69.0 54.3 all-gather.18
  125.3 54.3 all-gather.14
  181.5 54.3 all-gather.20
  237.7 160.7 all-gather.22
  400.2 160.7 all-gather.24
  753.8 159.6 reduce-scatter.2
  1033.5 426.5 reduce-scatter.4
  1462.6 430.9 all-reduce.2
where the time goes:
time: 1970 us; the launch traced here: 1950 us
  waiting for transfers between devices  1270 us (64%)
  local copies, waits for them, and re-layouts  393 us (20%)
  matrix products  173 us (9%)
  blocking collectives  78.5 us (4%)
    reduce_scatter x1, waiting for transfers between devices, local(): lax.psum_scatter(jnp.concatenate([out_part, up_part, down_part, small_par...  427 us
    psum x1, waiting for transfers between devices, local(): lax.psum(attn_shard.astype(jnp.bfloat16), 'rep').astype(jnp.float32)  407 us
    concatenate x1, local copies, waits for them, and re-layouts, local(): jnp.concatenate([out_part, up_part, down_part, small_part], axis=1)  163 us
    all_gather x1, waiting for transfers between devices, local(): lax.all_gather(up_weight, 'shard', axis=0, tiled=True)  158 us
    all_gather x1, waiting for transfers between devices, local(): lax.all_gather(down_weight, 'shard', axis=0, tiled=True)  140 us
    concatenate x1, local copies, waits for them, and re-layouts, local(): jnp.concatenate([query_part, key_part, value_part, small_part], axis=1)  109 us
    dot_general x6, matrix products, column_grad(): jnp.einsum('tr,tc->rc', left, right, preferred_element_type=jnp.float32)  57.9 us
    reshape x1, local copies, waits for them, and re-layouts, local(): column_grad(active_low, grad_mixed)  55.9 us
  transfers between devices with their start and end apart: 9, of which 7 were waited for; matrix products, arithmetic and copies ran while one was open for 17% of the time, Pallas kernels for 0%

commit v1 on v0

v1 whole, which is shorter than its diff:
```python
import functools
import math

import jax
import jax.numpy as jnp
from jax import lax
from jax.experimental import pallas as pl
from jax.experimental.pallas import tpu as pltpu
from jax.sharding import PartitionSpec as P

HEADS = 16
MESH = pl.DeviceIdType.MESH
BF = jnp.bfloat16
F32 = jnp.float32
VM = pl.BlockSpec(memory_space=pltpu.VMEM)
LIMIT = 60 * 2**20
SIZE = None


def flip(index, mask):
    bit = 1
    while bit <= mask:
        if mask & bit:
            index = index + bit - 2 * bit * ((index // bit) % 2)
        bit *= 2
    return index


def span(masks):
    out = [0]
    for m in masks:
        out = out + [h ^ m for h in out]
    return out


def pair_masks(size):
    masks, bit = [], 1
    while bit < size:
        masks.append(bit + bit // 2 if len(masks) % 2 and size >= 2 * bit else bit)
        bit *= 2
    return masks


def shard_masks(size):
    masks, bit = [], 2
    while bit < size:
        masks.append(bit if len(masks) < 2 else bit + bit // 2)
        bit *= 2
    return masks


def orders(masks):
    return [list(masks), list(masks[1:]) + list(masks[:1])]


class Net:
    def __init__(self, send, recv):
        self.send, self.recv, self.used, self.open = send, recv, 0, []

    def to(self, axis, mask, src, dst):
        k = self.used
        self.used += 1
        copy = pltpu.make_async_remote_copy(
            src_ref=src,
            dst_ref=dst,
            send_sem=self.send.at[k],
            recv_sem=self.recv.at[k],
            device_id={axis: flip(lax.axis_index(axis), mask)},
            device_id_type=MESH,
        )
        copy.start()
        self.open.append(copy)
        return copy

    def own(self, src, dst):
        k = self.used
        self.used += 1
        copy = pltpu.make_async_copy(src, dst, self.send.at[k])
        copy.start()
        return copy

    def finish(self):
        for copy in self.open:
            copy.wait_send()


def meet(shard_set, rep_set):
    barrier = pltpu.get_barrier_semaphore()
    for axis, masks in (("shard", shard_set), ("rep", rep_set)):
        for m in masks:
            pl.semaphore_signal(
                barrier,
                inc=1,
                device_id={axis: flip(lax.axis_index(axis), m)},
                device_id_type=MESH,
            )
    pl.semaphore_wait(barrier, len(shard_set) + len(rep_set))


class Gather:
    def __init__(self, net, buf, masks):
        self.net, self.buf = net, buf
        rows = buf.shape[1] // 2
        self.parts = [
            dict(rows=pl.ds(i * rows, rows), order=o, held=[0], wait=[])
            for i, o in enumerate(orders(masks))
        ]
        self.cores = []
        self.step = 0
        self.steps = len(masks)

    def start(self):
        net, buf = self.net, self.buf
        for part in self.parts:
            fresh = part["held"] if self.step == 0 else part["new"]
            if self.step < self.steps:
                m = part["order"][self.step]
                part["new"] = [h ^ m for h in part["held"]]
                part["wait"] = [
                    net.to("shard", m, buf.at[h, part["rows"]], buf.at[h ^ m, part["rows"]])
                    for h in part["held"]
                ]
                part["held"] = part["held"] + part["new"]
            self.cores += [
                net.to("shard", 1, buf.at[h, part["rows"]], buf.at[h ^ 1, part["rows"]])
                for h in fresh
            ]
        self.step += 1

    def arrive(self):
        for part in self.parts:
            for copy in part["wait"]:
                copy.wait_recv()
            part["wait"] = []

    def run(self):
        for _ in range(self.steps):
            self.start()
            self.arrive()
        self.start()
        self.end()

    def end(self):
        for copy in self.cores:
            copy.wait_recv()


def reduce_shapes(group, rows, width, masks):
    half = [pltpu.VMEM((group // 2, rows, width), BF)] * 2
    count = 0
    for i in range(len(masks)):
        count += 2 ** (len(masks) - 1 - i)
    return half + [pltpu.VMEM((count, rows, width), BF)]


class Reduce:
    def __init__(self, net, part, work, masks):
        self.net, self.part, self.masks = net, part, masks
        self.core_land, self.sums, self.land = work
        self.group, self.rows = part.shape[0], part.shape[1]
        self.cores = {}

    def begin(self):
        for j in range(1, self.group, 2):
            self.cores[j ^ 1] = self.net.to(
                "shard", 1, self.part.at[j], self.core_land.at[(j ^ 1) // 2]
            )

    def fold(self, h, rows, landed):
        step = 32

        @pl.loop(0, rows.size // step)
        def _(i):
            at = pl.ds(pl.multiple_of(rows.start + i * step, step), step)
            self.sums[h // 2, at] = (
                self.sums[h // 2, at].astype(F32) + landed[at].astype(F32)
            ).astype(BF)

    def first(self, h):
        step = 32
        self.cores[h].wait_recv()

        @pl.loop(0, self.rows // step)
        def _(i):
            at = pl.ds(pl.multiple_of(i * step, step), step)
            self.sums[h // 2, at] = (
                self.part[h, at].astype(F32) + self.core_land[h // 2, at].astype(F32)
            ).astype(BF)

    def launch(self, k):
        half = self.rows // 2
        self.flight = []
        base = 0
        for i in range(k):
            base += 2 ** (len(self.masks) - 1 - i)
        for n, order in enumerate(orders(self.masks)):
            rows = pl.ds(n * half, half)
            rest = span(order[k + 1 :])
            for at, h in enumerate(rest):
                copy = self.net.to(
                    "shard",
                    order[k],
                    self.sums.at[(h ^ order[k]) // 2, rows],
                    self.land.at[base + at, rows],
                )
                self.flight.append((copy, h, rows, base + at))

    def prepare(self):
        both = orders(self.masks)
        sent = set()
        for order in both:
            sent |= {h ^ order[0] for h in span(order[1:])}
        every = span(self.masks)
        for h in sorted(sent):
            self.first(h)
        self.launch(0)
        for h in every:
            if h not in sent:
                self.first(h)

    def advance(self, k):
        flight = self.flight
        for copy, h, rows, at in flight:
            copy.wait_recv()
            if k < len(self.masks) - 1:
                self.fold(h, rows, self.land.at[at])
        if k < len(self.masks) - 1:
            self.launch(k + 1)

    def run(self):
        self.begin()
        self.prepare()
        for k in range(len(self.masks)):
            self.advance(k)

    def total(self, at):
        [(_, _, rows, slot)] = [f for f in self.flight if f[2].start == at[0]]
        return (self.sums[0, at[1]].astype(F32) + self.land[slot, at[1]].astype(F32))


def norm_rows(v):
    center = v - jnp.mean(v, axis=-1, keepdims=True)
    spread = jnp.mean(center * center, axis=-1, keepdims=True)
    inv = lax.rsqrt(spread + 1e-05)
    return center * inv, inv


def norm_back(grad, gain, n, inv):
    scaled = grad * gain
    return inv * (
        scaled
        - jnp.mean(scaled, axis=-1, keepdims=True)
        - n * jnp.mean(scaled * n, axis=-1, keepdims=True)
    )


FG, FS, OB, SG, SS, DB, LN = range(7)


def live_rows(length, start, rows):
    at = start + lax.broadcasted_iota(jnp.int32, (rows, 1), 0)
    return (at.astype(F32) < length).astype(F32)


def rep_gather(net, views, order):
    held = [0]
    for m in order:
        copies = [net.to("rep", m, views(h), views(h)) for h in held]
        held = held + [h ^ m for h in held]
        yield copies


def gather_kernel(
    sizes,
    x_ref,
    cot_ref,
    small_ref,
    q_ref,
    k_ref,
    v_ref,
    u_ref,
    nrm,
    mix,
    small_all,
    wq,
    wk,
    wv,
    wu,
    send,
    recv,
):
    group, reps = sizes
    me, rep = lax.axis_index("shard"), lax.axis_index("rep")
    net = Net(send, recv)
    masks, rmasks = shard_masks(group), pair_masks(reps)
    meet(range(1, group), rmasks)
    width = small_ref.shape[1]
    mine = pl.ds(pl.multiple_of(me * width, width), width)
    small = [
        net.to("shard", j, small_ref, small_all.at[:, mine]) for j in range(1, group)
    ]
    own_small = net.own(small_ref, small_all.at[:, mine])
    arrays = ((q_ref, wq), (k_ref, wk), (v_ref, wv), (u_ref, wu))
    chunk = q_ref.shape[0] // reps

    def piece(mask):
        return pl.ds(pl.multiple_of(flip(rep, mask) * chunk, chunk), chunk)

    moved = []
    for src, dst in arrays:
        n = dst.shape[2]

        def columns(j):
            return pl.ds(pl.multiple_of(flip(me, j) * n, n), n)

        moved.append(
            [
                net.to("shard", j, src.at[piece(0), columns(j)], dst.at[me, piece(0)])
                for j in range(1, group)
            ]
            + [net.own(src.at[piece(0), columns(0)], dst.at[me, piece(0)])]
        )
    for copy in small:
        copy.wait_recv()
    own_small.wait()
    length = small_all[LN : LN + 1, pl.ds(pl.multiple_of(me * width, width), 128)][:, :1]
    step = 16

    @pl.loop(0, x_ref.shape[0] // step)
    def _(i):
        at = pl.ds(pl.multiple_of(i * step, step), step)
        n, _ = norm_rows(x_ref[at].astype(F32))
        nrm[0, at] = (n * small_all[FG : FG + 1] + small_all[FS : FS + 1]).astype(BF)
        mix[0, at] = (cot_ref[at].astype(F32) * live_rows(length, i * step, step)).astype(BF)

    gathers = [Gather(net, nrm, masks), Gather(net, mix, masks)]
    for g in gathers:
        g.start()
    streams = []
    for i, ((_, dst), copies) in enumerate(zip(arrays, moved)):
        for copy in copies[:-1]:
            copy.wait_recv()
        copies[-1].wait()
        both = (rmasks, rmasks[::-1])
        lanes = dst.shape[2] // 2
        if lanes % 128:
            lanes, both = dst.shape[2], both[i % 2 :][:1]
        for n, order in enumerate(both):
            cols = pl.ds(n * lanes, lanes)
            streams.append(
                rep_gather(net, lambda h, d=dst, c=cols: d.at[:, piece(h), c], order)
            )
    flights = [next(s) for s in streams]
    for _ in range(len(masks)):
        for g in gathers:
            g.arrive()
            g.start()
    for _ in range(len(rmasks)):
        for i, s in enumerate(streams):
            for copy in flights[i]:
                copy.wait_recv()
            flights[i] = next(s, [])
    for g in gathers:
        g.end()
    net.finish()


def middle_kernel(sizes, part, x_ref, small, mid, second, *work):
    group, _ = sizes
    net = Net(*work[-2:])
    masks = shard_masks(group)
    meet([1] + masks, [])
    red = Reduce(net, part, work[:3], masks)
    red.run()
    step, half = 16, x_ref.shape[0] // 2
    for n in range(2):

        @pl.loop(0, half // step)
        def _(i):
            at = pl.ds(pl.multiple_of(n * half + i * step, step), step)
            m = x_ref[at].astype(F32) + (red.total((n * half, at)) + small[OB : OB + 1])
            mid[at] = m
            v, _ = norm_rows(m)
            second[0, at] = (v * small[SG : SG + 1] + small[SS : SS + 1]).astype(BF)

    Gather(net, second, masks).run()
    net.finish()


def branch_kernel(sizes, down, grad, mid, cot, small, out, gmid, sums, branch, *work):
    group, _ = sizes
    net = Net(*work[-2:])
    masks = shard_masks(group)
    meet([1] + masks, [])
    me = lax.axis_index("shard")
    width = small.shape[1] // group
    length = small[LN : LN + 1, pl.ds(pl.multiple_of(me * width, width), 128)][:, :1]
    red = Reduce(net, grad, work[:3], masks)
    late = Reduce(net, down, work[3:6], masks)
    red.begin()
    late.begin()
    red.prepare()
    for k in range(len(masks)):
        red.advance(k)
    step, half = 16, mid.shape[0] // 2
    sums[...] = jnp.zeros_like(sums)
    for n in range(2):

        @pl.loop(0, half // step)
        def _(i):
            at = pl.ds(pl.multiple_of(n * half + i * step, step), step)
            g = red.total((n * half, at))
            v, inv = norm_rows(mid[at])
            gout = cot[at].astype(F32) * live_rows(length, n * half + i * step, step)
            res = gout + norm_back(g, small[SG : SG + 1], v, inv)
            gmid[at] = res
            low = res.astype(BF)
            branch[0, at] = low
            sums[SG : SG + 1] += jnp.sum(g * v, axis=0, keepdims=True)
            sums[SS : SS + 1] += jnp.sum(g, axis=0, keepdims=True)
            sums[OB : OB + 1] += jnp.sum(low.astype(F32), axis=0, keepdims=True)
            sums[DB : DB + 1] += jnp.sum(gout, axis=0, keepdims=True)

    gather = Gather(net, branch, masks)
    gather.start()
    late.prepare()
    for k in range(len(masks)):
        gather.arrive()
        gather.start()
        late.advance(k)
    gather.end()
    for n in range(2):

        @pl.loop(0, half // step)
        def _(i):
            at = pl.ds(pl.multiple_of(n * half + i * step, step), step)
            v = mid[at] + (late.total((n * half, at)) + small[DB : DB + 1])
            out[at] = (v * live_rows(length, n * half + i * step, step)).astype(BF)

    net.finish()


class RepSum:
    def __init__(self, net, arr, order, sums, land, reps):
        self.net, self.arr, self.order = net, arr, order
        self.sums, self.land = sums, land
        self.chunk = arr.shape[1] // reps
        self.slots = {h: i for i, h in enumerate(span(order[1:]))}

    def view(self, mask):
        at = flip(lax.axis_index("rep"), mask) * self.chunk
        return self.arr.at[:, pl.ds(pl.multiple_of(at, self.chunk), self.chunk)]

    def launch(self, k):
        rest = span(self.order[k + 1 :])
        base = 0
        for i in range(k):
            base += 2 ** (len(self.order) - 1 - i)
        m = self.order[k]
        self.flight = []
        for at, h in enumerate(rest):
            src = self.view(h ^ m) if k == 0 else self.sums.at[self.slots[h ^ m]]
            copy = self.net.to("rep", m, src, self.land.at[base + at])
            self.flight.append((copy, h, base + at))

    def fold(self, k):
        flight = self.flight
        for copy, h, at in reversed(flight):
            copy.wait_recv()
            left = self.view(h) if k == 0 else self.sums.at[self.slots[h]]
            right, dst = self.land.at[at], self.sums.at[self.slots[h]]
            add_into(dst, left, right)


def add_into(dst, left, right):
    a, c, n = dst.shape
    step = 16 if n >= 1024 else min(c, 64)

    @pl.loop(0, a)
    def _(i):
        @pl.loop(0, c // step)
        def _(j):
            at = pl.ds(pl.multiple_of(j * step, step), step)
            dst[i, at] = (left[i, at].astype(F32) + right[i, at].astype(F32)).astype(BF)


def sum_shapes(shape, reps):
    a, rows, n = shape
    masks = pair_masks(reps)
    count = 2 ** len(masks)
    return [
        pltpu.VMEM((count // 2, a, rows // reps, n), BF),
        pltpu.VMEM((count - 1, a, rows // reps, n), BF),
    ]


def final_kernel(sizes, *refs):
    group, reps = sizes
    grad, x_ref, gmid, small, sums3, cols = refs[:6]
    arrays = refs[6:12]
    gin, smalls = refs[12:14]
    outs = refs[14:20]
    work = refs[20:]
    red_work = work[:3]
    pairs = [work[3 + 2 * i : 5 + 2 * i] for i in range(6)]
    sums, land, both, zland = work[15:19]
    net = Net(*work[-2:])
    masks, rmasks = shard_masks(group), pair_masks(reps)
    me, rep = lax.axis_index("shard"), lax.axis_index("rep")
    meet(range(1, group), range(1, reps))
    width = smalls.shape[1]
    flips = [rmasks, rmasks[::-1]]
    reds = [
        RepSum(net, a, flips[f], *p, reps)
        for a, p, f in zip(arrays, pairs, (0, 0, 1, 0, 1, 1))
    ]
    q, k, v, up, out, down = reds
    turn = [down, up, out, q, k, v]
    for red in turn:
        red.launch(0)
    first = Reduce(net, grad, red_work, masks)
    first.run()
    step, half = 16, x_ref.shape[0] // 2
    sums[...] = sums3[...]
    for n in range(2):

        @pl.loop(0, half // step)
        def _(i):
            at = pl.ds(pl.multiple_of(n * half + i * step, step), step)
            g = first.total((n * half, at))
            w, inv = norm_rows(x_ref[at].astype(F32))
            gin[at] = (gmid[at] + norm_back(g, small[FG : FG + 1], w, inv)).astype(BF)
            sums[FG : FG + 1] += jnp.sum(g * w, axis=0, keepdims=True)
            sums[FS : FS + 1] += jnp.sum(g, axis=0, keepdims=True)

    def mine(j):
        return pl.ds(pl.multiple_of(flip(me, j) * width, width), width)

    tiny = [net.to("shard", j, sums.at[:, mine(j)], land.at[me]) for j in range(1, group)]
    own = net.own(sums.at[:, mine(0)], land.at[me])
    for copy in tiny:
        copy.wait_recv()
    own.wait()
    total = land[0]
    for j in range(1, group):
        total = total + land[j]
    both[0:8] = total
    both[8:16] = cols[...]
    tiny = [net.to("rep", h, both, zland.at[rep]) for h in range(1, reps)]
    own = net.own(both, zland.at[rep])
    for step_at in range(len(rmasks)):
        for red in turn:
            red.fold(step_at)
            if step_at < len(rmasks) - 1:
                red.launch(step_at + 1)

    def rows(o, mask):
        c = o.shape[0] // reps
        return pl.ds(pl.multiple_of(flip(rep, mask) * c, c), c)

    moved = {}
    for i in (3, 4, 5, 0, 1, 2):
        red, o = reds[i], outs[i]
        done = red.sums.at[0]
        if i in (4, 5):
            moved[i] = [net.own(done.at[0], o.at[rows(o, 0)])]
            continue
        n = done.shape[2]

        def place(n=n):
            return pl.ds(pl.multiple_of(me * n, n), n)

        moved[i] = [
            net.to("shard", j, done.at[flip(me, j)], o.at[rows(o, 0), place()])
            for j in range(1, group)
        ] + [net.own(done.at[me], o.at[rows(o, 0), place()])]
    streams, flights = [], []
    for i in (5, 3, 4, 0, 1, 2):
        for copy in moved[i][:-1]:
            copy.wait_recv()
        moved[i][-1].wait()
        o = outs[i]
        lanes = o.shape[1] // 2
        for n, order in enumerate(flips):
            c = pl.ds(n * lanes, lanes)
            s = rep_gather(net, lambda h, o=o, c=c: o.at[rows(o, h), c], order)
            streams.append(s)
            flights.append(next(s))
    for copy in tiny:
        copy.wait_recv()
    own.wait()
    total = zland[0]
    for h in range(1, reps):
        total = total + zland[h]
    smalls[...] = total
    for _ in range(len(rmasks)):
        for i, s in enumerate(streams):
            for copy in flights[i]:
                copy.wait_recv()
            flights[i] = next(s, [])
    net.finish()


def call(body, number, sizes, outs, scratch, copies, args):
    return pl.pallas_call(
        functools.partial(body, sizes),
        out_shape=[jax.ShapeDtypeStruct(s, d) for s, d in outs],
        in_specs=[VM] * len(args),
        out_specs=[VM] * len(outs),
        scratch_shapes=list(scratch)
        + [pltpu.SemaphoreType.DMA((copies,)), pltpu.SemaphoreType.DMA((copies,))],
        compiler_params=pltpu.CompilerParams(
            collective_id=number, has_side_effects=True, vmem_limit_bytes=LIMIT
        ),
        name=body.__name__,
    )(*args)


def dot(a, b):
    return jnp.dot(a, b, preferred_element_type=F32)


def dot_nt(a, b):
    return jnp.einsum("tc,rc->tr", a, b, preferred_element_type=F32)


def dot_tn(a, b):
    return jnp.einsum("tr,tc->rc", a, b, preferred_element_type=F32)


def local(
    block_input,
    lengths,
    first_gain,
    first_shift,
    query_weight,
    query_bias,
    key_weight,
    value_weight,
    value_bias,
    out_weight,
    out_bias,
    second_gain,
    second_shift,
    up_weight,
    up_bias,
    down_weight,
    down_bias,
    cotangent,
):
    rows, width = block_input.shape[1], block_input.shape[2]
    hidden = up_weight.shape[1]
    group, reps = lax.axis_size("shard"), lax.axis_size("rep")
    sizes = (group, reps)
    g, f = width // group, hidden // group
    head = width // HEADS
    scale = 1.0 / math.sqrt(head)
    me = lax.axis_index("shard")
    small = jnp.stack(
        [
            first_gain.astype(F32),
            first_shift.astype(F32),
            out_bias.astype(F32),
            second_gain.astype(F32),
            second_shift.astype(F32),
            down_bias.astype(F32),
            jnp.full((g,), 1.0, F32) * lengths[0].astype(F32),
            jnp.zeros((g,), F32),
        ]
    )
    x, cot = block_input[0], cotangent[0]
    blocks = (group, rows, width)
    nrm, mix, small_all, wq, wk, wv, wu = call(
        gather_kernel,
        1,
        sizes,
        [
            (blocks, BF),
            (blocks, BF),
            ((8, width), F32),
            ((group, g, g), BF),
            ((group, g, g), BF),
            ((group, g, g), BF),
            ((group, g, f), BF),
        ],
        [],
        320,
        (x, cot, small, query_weight, key_weight, value_weight, up_weight),
    )
    flat = lambda a: a.reshape(-1, a.shape[-1])
    normed = flat(nrm)
    wq, wk, wv, wu = flat(wq), flat(wk), flat(wv), flat(wu)
    queries = (dot(normed, wq) + query_bias.astype(F32)).astype(BF)
    keys = dot(normed, wk).astype(BF)
    values = (dot(normed, wv) + value_bias.astype(F32)).astype(BF)
    shape = (group, rows, g // head, head)
    qh, kh, vh = (a.reshape(shape) for a in (queries, keys, values))
    lens = small_all[LN].reshape(group, g)[:, 0]
    order = jnp.bitwise_xor(jnp.arange(group, dtype=jnp.int32), me)
    lens = jnp.take(lens, order).astype(jnp.int32)
    pos = jnp.arange(rows, dtype=jnp.int32)
    valid = (pos[None, None, :] <= pos[None, :, None]) & (pos[None, None, :] < lens[:, None, None])
    scores = jnp.einsum("bqhd,bkhd->bhqk", qh, kh, preferred_element_type=F32) * scale
    scores = jnp.where(valid[:, None], scores, -1e30)
    top = jnp.max(scores, axis=-1, keepdims=True)
    expo = jnp.exp(scores - top)
    p = expo / jnp.sum(expo, axis=-1, keepdims=True)
    p_low = p.astype(BF)
    ctx = (
        jnp.einsum("bhqk,bkhd->bqhd", p_low, vh, preferred_element_type=F32)
        .astype(BF)
        .reshape(group * rows, g)
    )
    part = dot(ctx, out_weight).astype(BF).reshape(blocks)
    masks = shard_masks(group)
    work = reduce_shapes(group, rows, width, masks)
    mid, second = call(
        middle_kernel,
        2,
        sizes,
        [((rows, width), F32), (blocks, BF)],
        work,
        96,
        (part, x, small_all),
    )
    second = flat(second)
    mixed = flat(mix)
    upper = dot(second, wu) + up_bias.astype(F32)
    cdf = 0.5 * (1.0 + lax.erf(upper * (1.0 / math.sqrt(2.0))))
    pdf = jnp.exp(-0.5 * upper * upper) * (1.0 / math.sqrt(2.0 * math.pi))
    active = (upper * cdf).astype(BF)
    gup = (dot_nt(mixed, down_weight) * (cdf + upper * pdf)).astype(BF)
    gpart = dot_nt(gup, wu).astype(BF).reshape(blocks)
    dpart = dot(active, down_weight).astype(BF).reshape(blocks)
    out, gmid, sums3, branch = call(
        branch_kernel,
        3,
        sizes,
        [((rows, width), BF), ((rows, width), F32), ((8, width), F32), (blocks, BF)],
        work + work,
        160,
        (dpart, gpart, mid, cot, small_all),
    )
    branch = flat(branch)
    gctx = dot_nt(branch, out_weight).astype(BF).reshape(shape)
    gw = jnp.einsum("bqhd,bkhd->bhqk", gctx, vh, preferred_element_type=F32)
    inner = jnp.sum(p * gw, axis=-1, keepdims=True)
    gs = (p * (gw - inner)).astype(BF)
    join = lambda a: a.astype(BF).reshape(group * rows, g)
    gq = join(jnp.einsum("bhqk,bkhd->bqhd", gs, kh, preferred_element_type=F32) * scale)
    gk = join(jnp.einsum("bhqk,bqhd->bkhd", gs, qh, preferred_element_type=F32) * scale)
    gv = join(jnp.einsum("bhqk,bqhd->bkhd", p_low, gctx, preferred_element_type=F32))
    npart = (dot_nt(gq, wq) + dot_nt(gk, wk) + dot_nt(gv, wv)).astype(BF).reshape(blocks)
    total = lambda a: jnp.sum(a.astype(F32), axis=0)
    cols = jnp.concatenate(
        [
            total(gq)[None],
            total(gv)[None],
            total(gup).reshape(4, g),
            jnp.zeros((2, g), F32),
        ]
    )
    grads = (
        dot_tn(normed, gq).astype(BF).reshape(group, g, g),
        dot_tn(normed, gk).astype(BF).reshape(group, g, g),
        dot_tn(normed, gv).astype(BF).reshape(group, g, g),
        dot_tn(second, gup).astype(BF).reshape(group, g, f),
        dot_tn(ctx, branch).astype(BF).reshape(1, g, width),
        dot_tn(active, mixed).astype(BF).reshape(1, f, width),
    )
    scratch = list(work)
    for a in grads:
        scratch += sum_shapes(a.shape, reps)
    scratch += [
        pltpu.VMEM((8, width), F32),
        pltpu.VMEM((group, 8, g), F32),
        pltpu.VMEM((16, g), F32),
        pltpu.VMEM((reps, 16, g), F32),
    ]
    gin, smalls, *weights = call(
        final_kernel,
        4,
        sizes,
        [
            ((rows, width), BF),
            ((16, g), F32),
            ((g, width), BF),
            ((g, width), BF),
            ((g, width), BF),
            ((g, hidden), BF),
            ((g, width), BF),
            ((f, width), BF),
        ],
        scratch,
        320,
        (npart, x, gmid, small_all, sums3, cols) + grads,
    )
    dq, dk, dv, du, do, dd = (w.astype(F32) for w in weights)
    return (
        out[None],
        gin[None],
        smalls[FG],
        smalls[FS],
        dq,
        smalls[8],
        dk,
        dv,
        smalls[9],
        do,
        smalls[OB],
        smalls[SG],
        smalls[SS],
        du,
        smalls[10:14].reshape(-1),
        dd,
        smalls[DB],
    )


def solution(mesh):
    tokens = P(("rep", "shard"), None, None)
    vec, mat = P("shard"), P("shard", None)
    return jax.shard_map(
        local,
        mesh=mesh,
        in_specs=(
            tokens,
            P(("rep", "shard")),
            vec,
            vec,
            mat,
            vec,
            mat,
            mat,
            vec,
            mat,
            vec,
            vec,
            vec,
            mat,
            vec,
            mat,
            vec,
            tokens,
        ),
        out_specs=(
            tokens,
            tokens,
            vec,
            vec,
            mat,
            vec,
            mat,
            mat,
            vec,
            mat,
            vec,
            vec,
            vec,
            mat,
            vec,
            mat,
            vec,
        ),
        check_vma=False,
    )
```

time: 1970 us -> 866 us (0.44)
  waiting for transfers between devices: 1270 us -> 0 us
  Pallas kernels: 0 us -> 722 us
  local copies, waits for them, and re-layouts: 393 us -> 16.7 us
  matrix products: 173 us -> 92.1 us
  blocking collectives: 78.5 us -> 0 us
    pallas_call x0 -> x4, Pallas kernels: none -> 722 us  [call(): pl.pallas_call(functools.partial(body, sizes), out_shape=[jax.ShapeDtypeS...]
    all_gather x6 -> x0, waiting for transfers between devices: 435 us -> none  [the longest x1 158 us: local(): lax.all_gather(up_weight, 'shard', axis=0, tiled=True)]
    reduce_scatter x2 -> x0, waiting for transfers between devices: 427 us -> none  [the longest x1 427 us: local(): lax.psum_scatter(jnp.concatenate([out_part, up_part, down_part, small_par...]
    psum x1 -> x0, waiting for transfers between devices: 407 us -> none  [local(): lax.psum(attn_shard.astype(jnp.bfloat16), 'rep').astype(jnp.float32)]
    concatenate x2 -> x1, local copies, waits for them, and re-layouts: 271 us -> 0.07 us  [local(): jnp.concatenate([total(gq)[None], total(gv)[None], total(gup).reshape(4,...]
    dot_general x24, matrix products: 173 us -> 92.1 us  [the longest x6 31.5 us: dot(): return jnp.dot(a, b, preferred_element_type=F32)]
    all_gather x9 -> x0, blocking collectives: 78.5 us -> none  [the longest x1 10.3 us: local(): lax.all_gather(second_shift, 'shard', axis=0, tiled=True)]
    reshape x5 -> x6, local copies, waits for them, and re-layouts: 68.5 us -> 5.77 us  [the longest x4 3.75 us: local(): qh, kh, vh = (a.reshape(shape) for a in (queries, keys, values))]
  transfers between devices with their start and end apart: 9 -> 0, of which waited for: 7 -> 0; matrix products, arithmetic and copies ran while one was open for 17% -> 0% of each run, Pallas kernels for 0% -> 0%
where the time goes in v1:
time: 866 us; the launch traced here: 858 us
  Pallas kernels  722 us (83%)
  matrix products  92.1 us (11%)
  other arithmetic  25.9 us (3%)
  local copies, waits for them, and re-layouts  16.7 us (2%)
    pallas_call x4, Pallas kernels, call(): pl.pallas_call(functools.partial(body, sizes), out_shape=[jax.ShapeDtypeS...  722 us
    dot_general x6, matrix products, dot(): return jnp.dot(a, b, preferred_element_type=F32)  31.5 us
    dot_general x6, matrix products, dot_tn(): return jnp.einsum('tr,tc->rc', a, b, preferred_element_type=F32)  29.7 us
    dot_general x6, matrix products, dot_nt(): return jnp.einsum('tc,rc->tr', a, b, preferred_element_type=F32)  22 us
    convert_element_type x6, other arithmetic, local(): dq, dk, dv, du, do, dd = (w.astype(F32) for w in weights)  17.8 us

profile of v1, /device:TPU:0, one launch (start us, length us, event | category | flops | bytes accessed | tf_op | source)
XLA Modules:
  0.0 858.5 jit_solution(5417014853623975840)
XLA Ops:
  8.1 163.5 %gather_kernel.1 = (bf16[8,128,2048]{2,1,0:T(8,128)(2,1)}, bf16[8,128,2048]{2,1,0:T(8,128)(2,1)}, f32[8,2048]{1,0:T(8,128)}, bf16[8,256,256]{2,1,0:T(8,128)(2,1)...) custom-call(bf16[128,2048]{1,0:T(8,128)(2,1)} %bitcast.129, ...), custom_call_target="tpu_custom_call" | custom-call | tf_op jit(solution)/shard_map/gather_kernel/pallas_call | solution.py:605
  173.5 3.8 fusion.11
  178.3 4.3 fusion.12
  184.2 4.2 convolution_convert_fusion.11
  192.8 3.0 fusion.17
  197.2 3.3 convolution_convert_fusion
  200.5 56.7 %middle_kernel.1 = (f32[128,2048]{1,0:T(8,128)}, bf16[8,128,2048]{2,1,0:T(8,128)(2,1)}) custom-call(bf16[8,128,2048]{2,1,0:T(8,128)(2,1)} %bitcast.127, bf16[128,2048]{1,0:T(8,128)(2,1)} %bitcast.130, f32[8,2048]{1,0:T(8,128)} %get-tuple-element.40.small.refs_3_), custom_call_target="tpu_custom_call" | custom-call | tf_op jit(solution)/shard_map/middle_kernel/pallas_call | solution.py:605
  257.3 9.7 %multiply_convert_fusion = (bf16[1024,1024]{1,0:T(8,128)(2,1)}, f32[1024,1024]{1,0:T(8,128)S(1)}) fusion(f32[1024]{0:T(1024)S(1)} %convert_element_type.147, bf16[1024,2048]{1,0:T(8,128)(2,1)} %bitcast.183, bf16[2048,1024]{1,0:T(8,128)(2,1)} %bitcast.181), kind=kOutput, calls=%fused_computation.12 | convolution fusion | flops 4301258752 | bytes 14684160 | tf_op jit(solution)/shard_map/dot_general | solution.py:620
  267.0 7.0 convert_reduce_fusion
  274.1 9.5 %convolution_convert_fusion.1 = bf16[2048,1024]{1,0:T(8,128)(2,1)} fusion(bf16[1024,2048]{1,0:T(8,128)(2,1)} %bitcast.184, bf16[1024,1024]{1,0:T(8,128)(2,1)} %get-tuple-element.74), kind=kOutput, calls=%fused_computation.15 | convolution fusion | flops 4297064448 | bytes 10485760 | tf_op jit(solution)/shard_map/tr,tc->rc/dot_general | solution.py:628
  283.6 6.6 convolution_convert_fusion.2
  290.3 6.3 convert_bitcast_fusion.refs_11_
  296.6 6.0 convolution_convert_fusion.3
  302.6 73.6 %branch_kernel.1 = (bf16[128,2048]{1,0:T(8,128)(2,1)}, f32[128,2048]{1,0:T(8,128)}, f32[8,2048]{1,0:T(8,128)}, bf16[8,128,2048]{2,1,0:T(8,128)(2,1)}) custom-call(bf16[8,128,2048]{2,1,0:T(8,128)(2,1)} %bitcast.133, bf16[8,128,2048]{2,1,0:T(8,128)(2,1)} %bitcast.132, f32[128,2048]{1,0:T(8,128)} %get-tuple-element.46.mid, bf16[128,2048]{1,0:T(8,128)(2,1)} %bitcast.142, ...), custom_call_target="tpu_custom_call" | custom-call | tf_op jit(solution)/shard_map/branch_kernel/pallas_call | solution.py:605
  376.2 4.6 fusion.7.refs_10_
  384.9 3.1 convert_reduce_fusion.1
  392.3 4.7 convolution_convert_fusion.5
  397.0 2.4 convolution_convert_fusion.7
  404.6 3.4 add_convert_fusion
  408.0 427.9 %final_kernel.1 = (bf16[128,2048]{1,0:T(8,128)(2,1)}, f32[16,256]{1,0:T(8,128)}, bf16[256,2048]{1,0:T(8,128)(2,1)}, bf16[256,2048]{1,0:T(8,128)(2,1)}, bf16[256,...) custom-call(bf16[8,128,2048]{2,1,0:T(8,128)(2,1)} %bitcast.128, ...), custom_call_target="tpu_custom_call" | custom-call | tf_op jit(solution)/shard_map/final_kernel/pallas_call | solution.py:605
  838.9 2.9 convert_element_type.170
  841.8 2.9 convert_element_type.171
  847.8 4.4 convert_element_type.174
  852.2 4.4 convert_element_type.175
  (107 shorter events, 38.1 us)
Async XLA Ops:
  0.7 196.6 %copy-start = (bf16[256,2048]{1,0:T(8,128)(2,1)S(1)}, bf16[256,2048]{1,0:T(8,128)(2,1)}, u32[]{:S(2)}) copy-start(bf16[256,2048]{1,0:T(8,128)(2,1)} %param.27) | copy-start | bytes 3145732
  173.5 4.8 copy-start.7
  178.3 5.9 copy-start.9
  188.5 4.4 copy-start.14
  257.2 9.8 %copy-start.18 = (bf16[1024,2048]{1,0:T(8,128)(2,1)S(1)}, bf16[1024,2048]{1,0:T(8,128)(2,1)}, u32[]{:S(2)}) copy-start(bf16[1024,2048]{1,0:T(8,128)(2,1)} %param.33) | copy-start | bytes 12582916
  257.3 9.8 %copy-start.21 = (bf16[8,128,2048]{2,1,0:T(8,128)(2,1)S(1)}, bf16[8,128,2048]{2,1,0:T(8,128)(2,1)}, u32[]{:S(2)}) copy-start(bf16[8,128,2048]{2,1,0:T(8,128)(2,1)} %get-tuple-element.45) | copy-start | bytes 12582916
  274.1 9.5 %copy-start.23 = (bf16[8,256,1024]{2,1,0:T(8,128)(2,1)S(1)}, bf16[8,256,1024]{2,1,0:T(8,128)(2,1)}, u32[]{:S(2)}) copy-start(bf16[8,256,1024]{2,1,0:T(8,128)(2,1)} %get-tuple-element.44) | copy-start | bytes 12582916
  274.1 9.5 %copy-start.26 = (bf16[1024,1024]{1,0:T(8,128)(2,1)S(1)}, bf16[1024,1024]{1,0:T(8,128)(2,1)}, u32[]{:S(2)}) copy-start(bf16[1024,1024]{1,0:T(8,128)(2,1)} %get-tuple-element.74) | copy-start | bytes 6291460
  283.6 6.7 copy-start.22
  283.6 6.6 copy-start.25
  290.3 6.3 copy-start.19
  376.2 4.6 copy-start.24
  382.9 5.1 copy-start.15
  388.0 2.3 copy-start.5
  389.6 2.4 copy-start.17
  392.3 4.7 copy-start.20
  399.3 2.4 copy-start.10
  403.0 1.6 copy-start.6
  836.0 8.7 %copy-start.12 = (bf16[256,2048]{1,0:T(8,128)(2,1)S(1)}, bf16[256,2048]{1,0:T(8,128)(2,1)}, u32[]{:S(2)}) copy-start(bf16[256,2048]{1,0:T(8,128)(2,1)} %get-tuple-element.55) | copy-start | bytes 3145732
  838.9 7.4 copy-start.11
  841.8 6.1 copy-start.2
  847.8 4.4 copy-start.1
  852.2 4.5 copy-start.13
  852.2 5.2 copy-start.16
  (3 other events, 3.1 us)

commit v2 on v1

v2 whole, which is shorter than its diff:
```python
import functools
import math

import jax
import jax.numpy as jnp
from jax import lax
from jax.experimental import pallas as pl
from jax.experimental.pallas import tpu as pltpu
from jax.sharding import PartitionSpec as P

HEADS = 16
MESH = pl.DeviceIdType.MESH
BF = jnp.bfloat16
F32 = jnp.float32
VM = pl.BlockSpec(memory_space=pltpu.VMEM)
LIMIT = 60 * 2**20
SIZE = None


def flip(index, mask):
    bit = 1
    while bit <= mask:
        if mask & bit:
            index = index + bit - 2 * bit * ((index // bit) % 2)
        bit *= 2
    return index


def span(masks):
    out = [0]
    for m in masks:
        out = out + [h ^ m for h in out]
    return out


def pair_masks(size):
    masks, bit = [], 1
    while bit < size:
        masks.append(bit + bit // 2 if len(masks) % 2 and size >= 2 * bit else bit)
        bit *= 2
    return masks


def shard_masks(size):
    masks, bit = [], 2
    while bit < size:
        masks.append(bit if len(masks) < 2 else bit + bit // 2)
        bit *= 2
    return masks


def orders(masks):
    return [list(masks), list(masks[1:]) + list(masks[:1])]


class Net:
    def __init__(self, send, recv):
        self.send, self.recv, self.used, self.open = send, recv, 0, []

    def to(self, axis, mask, src, dst):
        k = self.used
        self.used += 1
        copy = pltpu.make_async_remote_copy(
            src_ref=src,
            dst_ref=dst,
            send_sem=self.send.at[k],
            recv_sem=self.recv.at[k],
            device_id={axis: flip(lax.axis_index(axis), mask)},
            device_id_type=MESH,
        )
        copy.start()
        self.open.append(copy)
        return copy

    def own(self, src, dst):
        k = self.used
        self.used += 1
        copy = pltpu.make_async_copy(src, dst, self.send.at[k])
        copy.start()
        return copy

    def finish(self):
        for copy in self.open:
            copy.wait_send()


def meet(shard_set, rep_set):
    barrier = pltpu.get_barrier_semaphore()
    for axis, masks in (("shard", shard_set), ("rep", rep_set)):
        for m in masks:
            pl.semaphore_signal(
                barrier,
                inc=1,
                device_id={axis: flip(lax.axis_index(axis), m)},
                device_id_type=MESH,
            )
    pl.semaphore_wait(barrier, len(shard_set) + len(rep_set))


class Gather:
    def __init__(self, net, buf, masks):
        self.net, self.buf = net, buf
        rows = buf.shape[1] // 2
        self.parts = [
            dict(rows=pl.ds(i * rows, rows), order=o, held=[0], new=[0], wait=[], step=0)
            for i, o in enumerate(orders(masks))
        ]
        self.cores = []
        self.steps = len(masks)

    def start(self, n):
        net, buf, part = self.net, self.buf, self.parts[n]
        fresh, rows = part["new"], part["rows"]
        if part["step"] < self.steps:
            m = part["order"][part["step"]]
            part["new"] = [h ^ m for h in part["held"]]
            part["wait"] = [
                net.to("shard", m, buf.at[h, rows], buf.at[h ^ m, rows]) for h in part["held"]
            ]
            part["held"] = part["held"] + part["new"]
        self.cores += [net.to("shard", 1, buf.at[h, rows], buf.at[h ^ 1, rows]) for h in fresh]
        part["step"] += 1

    def arrive(self, n):
        for copy in self.parts[n]["wait"]:
            copy.wait_recv()
        self.parts[n]["wait"] = []

    def both(self):
        for n in range(2):
            self.arrive(n)
            self.start(n)

    def end(self):
        for copy in self.cores:
            copy.wait_recv()

    def finish(self):
        for _ in range(self.steps):
            self.both()
        self.end()


def reduce_shapes(group, rows, width, masks):
    count = 2 ** len(masks) - 1
    return [
        pltpu.VMEM((group // 2, rows, width), BF),
        pltpu.VMEM((count, rows, width), BF),
    ]


class Reduce:
    def __init__(self, net, part, work, masks):
        self.net, self.part = net, part
        self.sums, self.land = work
        self.group, self.rows = part.shape[0], part.shape[1]
        self.cores = {}
        self.half = self.rows // 2
        self.steps = len(masks)
        self.orders = orders(masks)
        self.flight = [[], []]
        first = [o[0] for o in self.orders]
        self.sequence = sorted(
            span(masks), key=lambda h: -sum(self.sends(n, h) for n in range(2))
        )

    def sends(self, n, h):
        order = self.orders[n]
        return h not in span(order[1:])

    def begin(self):
        for h in self.sequence:
            self.cores[h] = self.net.to(
                "shard", 1, self.part.at[h ^ 1], self.sums.at[h // 2]
            )

    def add(self, h, start, count, other):
        step = min(count, 32)

        @pl.loop(0, count // step)
        def _(i):
            at = pl.ds(pl.multiple_of(start + i * step, step), step)
            self.sums[h // 2, at] = (
                self.sums[h // 2, at].astype(F32) + other[at].astype(F32)
            ).astype(BF)

    def send(self, n, k, h):
        order = self.orders[n]
        rest = span(order[k + 1 :])
        base = sum(2 ** (self.steps - 1 - i) for i in range(k))
        to = h ^ order[k]
        rows = pl.ds(n * self.half, self.half)
        slot = base + rest.index(to)
        copy = self.net.to(
            "shard", order[k], self.sums.at[h // 2, rows], self.land.at[slot, rows]
        )
        self.flight[n].append((copy, to, slot))

    def prepare(self):
        for h in self.sequence:
            self.cores[h].wait_recv()
            self.add(h, 0, self.rows, self.part.at[h])
            for n in range(2):
                if self.sends(n, h):
                    self.send(n, 0, h)

    def advance(self, n, k):
        flight, self.flight[n] = self.flight[n], []
        rest = span(self.orders[n][k + 2 :])
        flight.sort(key=lambda f: f[1] in rest)
        for copy, h, slot in flight:
            copy.wait_recv()
            if k < self.steps - 1:
                self.add(h, n * self.half, self.half, self.land.at[slot])
                if h not in rest:
                    self.send(n, k + 1, h)
            else:
                self.last = slot

    def run(self):
        self.begin()
        self.prepare()
        for k in range(self.steps - 1):
            for n in range(2):
                self.advance(n, k)

    def total(self, at):
        return self.sums[0, at].astype(F32) + self.land[self.last, at].astype(F32)


def norm_rows(v):
    center = v - jnp.mean(v, axis=-1, keepdims=True)
    spread = jnp.mean(center * center, axis=-1, keepdims=True)
    inv = lax.rsqrt(spread + 1e-05)
    return center * inv, inv


def norm_back(grad, gain, n, inv):
    scaled = grad * gain
    return inv * (
        scaled
        - jnp.mean(scaled, axis=-1, keepdims=True)
        - n * jnp.mean(scaled * n, axis=-1, keepdims=True)
    )


FG, FS, OB, SG, SS, DB, LN = range(7)


def live_rows(length, start, rows):
    at = start + lax.broadcasted_iota(jnp.int32, (rows, 1), 0)
    return (at.astype(F32) < length).astype(F32)


def by_rows(n, count, body):
    step = 16

    @pl.loop(0, count // 2 // step)
    def _(i):
        start = pl.multiple_of(n * (count // 2) + i * step, step)
        body(pl.ds(start, step), start)


def gather_kernel(
    sizes,
    x_ref,
    small_ref,
    q_ref,
    k_ref,
    v_ref,
    u_ref,
    nrm,
    small_all,
    wq,
    wk,
    wv,
    wu,
    send,
    recv,
):
    group, reps = sizes
    me, rep = lax.axis_index("shard"), lax.axis_index("rep")
    net = Net(send, recv)
    masks = shard_masks(group)
    meet(range(1, group), [])
    width = small_ref.shape[1]
    mine = pl.ds(pl.multiple_of(me * width, width), width)
    small = [
        net.to("shard", j, small_ref, small_all.at[:, mine]) for j in range(1, group)
    ]
    own_small = net.own(small_ref, small_all.at[:, mine])

    def scatter(src, dst, first, n):
        part = src.shape[1] // group

        def columns(j):
            return pl.ds(pl.multiple_of(flip(me, j) * part + first, n), n)

        return [
            net.to("shard", j, src.at[:, columns(j)], dst.at[me]) for j in range(1, group)
        ] + [net.own(src.at[:, columns(0)], dst.at[me])]

    moved = scatter(q_ref, wq, 0, width) + scatter(k_ref, wk, 0, width)
    for copy in small:
        copy.wait_recv()
    own_small.wait()
    gather = Gather(net, nrm, masks)
    for n in range(2):

        def one(at, start):
            v, _ = norm_rows(x_ref[at].astype(F32))
            nrm[0, at] = (v * small_all[FG : FG + 1] + small_all[FS : FS + 1]).astype(BF)

        by_rows(n, x_ref.shape[0], one)
        gather.start(n)
    moved += scatter(v_ref, wv, 0, width)
    quarter = wu.shape[2]
    moved += scatter(u_ref, wu, rep * quarter, quarter)
    gather.finish()
    for i, copy in enumerate(moved):
        if i % group == group - 1:
            copy.wait()
        else:
            copy.wait_recv()
    net.finish()


def middle_kernel(sizes, part, x_ref, cot_ref, small, mid, second, mix, *work):
    group, _ = sizes
    net = Net(*work[-2:])
    masks = shard_masks(group)
    meet([1] + masks, [])
    me = lax.axis_index("shard")
    width = small.shape[1] // group
    length = small[LN : LN + 1, pl.ds(pl.multiple_of(me * width, width), 128)][:, :1]
    rows = x_ref.shape[0]
    red = Reduce(net, part, work[:2], masks)
    red.begin()
    gmix = Gather(net, mix, masks)
    for n in range(2):

        def live(at, start):
            mix[0, at] = (cot_ref[at].astype(F32) * live_rows(length, start, 16)).astype(BF)

        by_rows(n, rows, live)
        gmix.start(n)
    red.prepare()
    for k in range(red.steps - 1):
        for n in range(2):
            red.advance(n, k)
    gather = Gather(net, second, masks)
    gmix.both()
    for n in range(2):
        red.advance(n, red.steps - 1)

        def norm(at, start):
            m = x_ref[at].astype(F32) + (red.total(at) + small[OB : OB + 1])
            mid[at] = m
            v, _ = norm_rows(m)
            second[0, at] = (v * small[SG : SG + 1] + small[SS : SS + 1]).astype(BF)

        by_rows(n, rows, norm)
        gather.start(n)
    for _ in range(gather.steps - 1):
        gmix.both()
        gather.both()
    gather.both()
    gmix.end()
    gather.end()
    net.finish()


def branch_kernel(
    sizes, down, grad, up, mid, cot, small, out, gmid, sums, branch, up_rows, *work
):
    group, _ = sizes
    net = Net(*work[-2:])
    masks = shard_masks(group)
    meet(range(1, group), [])
    me = lax.axis_index("shard")
    width = small.shape[1] // group
    rows = mid.shape[0]
    length = small[LN : LN + 1, pl.ds(pl.multiple_of(me * width, width), 128)][:, :1]
    red = Reduce(net, grad, work[:2], masks)
    red.run()
    late = Reduce(net, down, work[2:4], masks)
    late.begin()
    sums[...] = jnp.zeros_like(sums)
    gather = Gather(net, branch, masks)
    for n in range(2):
        red.advance(n, red.steps - 1)

        def back(at, start):
            g = red.total(at)
            v, inv = norm_rows(mid[at])
            gout = cot[at].astype(F32) * live_rows(length, start, 16)
            res = gout + norm_back(g, small[SG : SG + 1], v, inv)
            gmid[at] = res
            low = res.astype(BF)
            branch[0, at] = low
            sums[SG : SG + 1] += jnp.sum(g * v, axis=0, keepdims=True)
            sums[SS : SS + 1] += jnp.sum(g, axis=0, keepdims=True)
            sums[OB : OB + 1] += jnp.sum(low.astype(F32), axis=0, keepdims=True)
            sums[DB : DB + 1] += jnp.sum(gout, axis=0, keepdims=True)

        by_rows(n, rows, back)
        gather.start(n)
    wide = up.shape[2]
    each = mid.shape[1] // wide
    place = pl.ds(pl.multiple_of((me % each) * wide, wide), wide)
    tall = up.shape[1]
    down_to = pl.ds(pl.multiple_of((me // each) * tall, tall), tall)
    target = up_rows.at[down_to, place]
    moved = [net.to("shard", j, up.at[flip(me, j)], target) for j in range(1, group)]
    own = net.own(up.at[me], target)
    late.prepare()
    for k in range(gather.steps):
        gather.both()
        for n in range(2):
            late.advance(n, k)
    gather.end()
    for n in range(2):

        def close(at, start):
            v = mid[at] + (late.total(at) + small[DB : DB + 1])
            out[at] = (v * live_rows(length, start, 16)).astype(BF)

        by_rows(n, rows, close)
    for copy in moved:
        copy.wait_recv()
    own.wait()
    net.finish()


class Line:
    def __init__(self, own, land, out, tall, reps, sems):
        self.own, self.land, self.out = own, land, out
        self.rep, self.reps, self.sems = lax.axis_index("rep"), reps, sems
        self.count, self.size = land.shape[1], land.shape[2]
        self.tall, self.each = tall, tall // 2 // self.size
        self.skew = 2
        self.steps = self.count + 2 * self.skew * (reps - 1)

    def rows(self, way, i):
        row = (i // self.each) * self.tall + way * (self.tall // 2) + (i % self.each) * self.size
        return pl.ds(pl.multiple_of(row, self.size), self.size)

    def copy(self, src, dst, way, back, i, up):
        s, r = self.sems
        at = (2 * way + back) * self.count + i
        return pltpu.make_async_remote_copy(
            src_ref=src,
            dst_ref=dst,
            send_sem=s.at[at],
            recv_sem=r.at[at],
            device_id={"rep": self.rep + (1 if up else -1)},
            device_id_type=MESH,
        )

    def place(self, way):
        return self.rep if way == 0 else self.reps - 1 - self.rep

    def forth(self, way, t):
        at = self.place(way)
        i, last = t - self.skew * at, self.reps - 1

        @pl.when((i >= 0) & (i < self.count))
        def _():
            rows, land = self.rows(way, i), self.land.at[way, i]

            @pl.when(at == 0)
            def _():
                self.copy(self.own.at[rows], land, way, 0, i, way == 0).start()

            @pl.when(at != 0)
            def _():
                self.copy(self.own.at[rows], land, way, 0, i, way == 0).wait_recv()

            @pl.when((at != 0) & (at != last))
            def _():
                self.add(land, rows, land)
                self.copy(land, land, way, 0, i, way == 0).start()

            @pl.when(at == last)
            def _():
                out = self.out.at[rows]
                self.add(land, rows, out)
                self.copy(out, out, way, 1, i, way != 0).start()

    def add(self, land, rows, to):
        own, step = self.own.at[rows], 16

        @pl.loop(0, self.size // step)
        def _(n):
            at = pl.ds(pl.multiple_of(n * step, step), step)
            to[at] = (land[at].astype(F32) + own[at].astype(F32)).astype(BF)

    def back(self, way, t):
        at, last = self.place(way), self.reps - 1
        i = t - self.skew * (last + last - at)

        @pl.when((at != last) & (i >= 0) & (i < self.count))
        def _():
            out = self.out.at[self.rows(way, i)]
            self.copy(out, out, way, 1, i, way != 0).wait_recv()

            @pl.when(at != 0)
            def _():
                self.copy(out, out, way, 1, i, way != 0).start()

    def step(self, t):
        for way in (0, 1):
            self.forth(way, t)
        for way in (0, 1):
            self.back(way, t)

    def finish(self):
        last = self.reps - 1
        for way in (0, 1):
            at = self.place(way)

            @pl.loop(0, self.count)
            def _(i):
                out = self.out.at[self.rows(way, i)]

                @pl.when(at != last)
                def _():
                    self.copy(out, out, way, 0, i, way == 0).wait_send()

                @pl.when(at != 0)
                def _():
                    self.copy(out, out, way, 1, i, way != 0).wait_send()


def final_kernel(sizes, *refs):
    group, reps = sizes
    grad, x_ref, gmid, small, sums3, cols = refs[:6]
    arrays = refs[6:10]
    up_rows = refs[10]
    gin, smalls = refs[11:13]
    whole = refs[13]
    work = refs[14:]
    sums, land, both, zland, mine_all, line_land = work[2:8]
    net = Net(*work[-2:])
    masks = shard_masks(group)
    me, rep = lax.axis_index("shard"), lax.axis_index("rep")
    meet(range(1, group), range(1, reps))
    width, rows = smalls.shape[1], x_ref.shape[0]
    place = pl.ds(pl.multiple_of(me * width, width), width)
    tall = arrays[3].shape[0]
    wide = up_rows.shape[0]
    moved = [[net.own(up_rows, mine_all.at[0:wide]), net.own(arrays[3], mine_all.at[pl.ds(wide, tall)])]]
    for i, src in enumerate(arrays[:3]):
        dst = mine_all.at[pl.ds(wide + (i + 1) * tall, tall)]
        moved.append(
            [
                net.to("shard", j, src.at[flip(me, j)], dst.at[:, place])
                for j in range(1, group)
            ]
            + [net.own(src.at[me], dst.at[:, place])]
        )
    line = Line(mine_all, line_land, whole, tall, reps, work[-4:-2])
    red = Reduce(net, grad, work[:2], masks)

    def tasks():
        red.begin()
        yield
        red.prepare()
        for k in range(red.steps - 1):
            for n in range(2):
                yield
                red.advance(n, k)
        sums[...] = sums3[...]
        for n in range(2):
            yield
            red.advance(n, red.steps - 1)

            def back(at, start):
                g = red.total(at)
                w, inv = norm_rows(x_ref[at].astype(F32))
                gin[at] = (gmid[at] + norm_back(g, small[FG : FG + 1], w, inv)).astype(BF)
                sums[FG : FG + 1] += jnp.sum(g * w, axis=0, keepdims=True)
                sums[FS : FS + 1] += jnp.sum(g, axis=0, keepdims=True)

            by_rows(n, rows, back)

        def mine(j):
            return pl.ds(pl.multiple_of(flip(me, j) * width, width), width)

        tiny = [net.to("shard", j, sums.at[:, mine(j)], land.at[me]) for j in range(1, group)]
        own = net.own(sums.at[:, mine(0)], land.at[me])
        yield
        yield
        for copy in tiny:
            copy.wait_recv()
        own.wait()
        total = land[0]
        for j in range(1, group):
            total = total + land[j]
        both[0:8] = total
        both[8:16] = cols[...]
        tiny = [net.to("rep", h, both, zland.at[rep]) for h in range(1, reps)]
        own = net.own(both, zland.at[rep])
        yield
        yield
        yield
        for copy in tiny:
            copy.wait_recv()
        own.wait()
        total = zland[0]
        for h in range(1, reps):
            total = total + zland[h]
        smalls[...] = total

    todo = tasks()
    next(todo)
    for t in range(line.steps):
        i = t // line.each - wide // tall
        if t == 0:
            for copy in moved[0]:
                copy.wait()
        elif t < line.count and t % line.each == 0 and i > 0:
            for copy in moved[i][:-1]:
                copy.wait_recv()
            moved[i][-1].wait()
        line.step(t)
        if t >= 15 and t % 4 == 3:
            next(todo, None)
    for _ in todo:
        pass
    line.finish()
    net.finish()


def call(body, number, sizes, outs, scratch, copies, args):
    return pl.pallas_call(
        functools.partial(body, sizes),
        out_shape=[jax.ShapeDtypeStruct(s, d) for s, d in outs],
        in_specs=[VM] * len(args),
        out_specs=[VM] * len(outs),
        scratch_shapes=list(scratch)
        + [pltpu.SemaphoreType.DMA((copies,)), pltpu.SemaphoreType.DMA((copies,))],
        compiler_params=pltpu.CompilerParams(
            collective_id=number, has_side_effects=True, vmem_limit_bytes=LIMIT
        ),
        name=body.__name__,
    )(*args)


def dot(a, b):
    return jnp.dot(a, b, preferred_element_type=F32)


def dot_nt(a, b):
    return jnp.einsum("tc,rc->tr", a, b, preferred_element_type=F32)


def dot_tn(a, b):
    return jnp.einsum("tr,tc->rc", a, b, preferred_element_type=F32)


def local(
    block_input,
    lengths,
    first_gain,
    first_shift,
    query_weight,
    query_bias,
    key_weight,
    value_weight,
    value_bias,
    out_weight,
    out_bias,
    second_gain,
    second_shift,
    up_weight,
    up_bias,
    down_weight,
    down_bias,
    cotangent,
):
    rows, width = block_input.shape[1], block_input.shape[2]
    hidden = up_weight.shape[1]
    group, reps = lax.axis_size("shard"), lax.axis_size("rep")
    sizes = (group, reps)
    g, f = width // group, hidden // group
    head = width // HEADS
    scale = 1.0 / math.sqrt(head)
    me = lax.axis_index("shard")
    small = jnp.stack(
        [
            first_gain.astype(F32),
            first_shift.astype(F32),
            out_bias.astype(F32),
            second_gain.astype(F32),
            second_shift.astype(F32),
            down_bias.astype(F32),
            jnp.full((g,), 1.0, F32) * lengths[0].astype(F32),
            jnp.zeros((g,), F32),
        ]
    )
    x, cot = block_input[0], cotangent[0]
    blocks = (group, rows, width)
    parts = reps if f // reps % 128 == 0 else 1
    nrm, small_all, wq, wk, wv, wu = call(
        gather_kernel,
        1,
        sizes,
        [
            (blocks, BF),
            ((8, width), F32),
            ((group, g, g), BF),
            ((group, g, g), BF),
            ((group, g, g), BF),
            ((group, g, f // parts), BF),
        ],
        [],
        200,
        (x, small, query_weight, key_weight, value_weight, up_weight),
    )
    flat = lambda a: a.reshape(-1, a.shape[-1])
    normed = flat(nrm)
    wq, wk, wv, wu = flat(wq), flat(wk), flat(wv), flat(wu)
    if parts > 1:
        wu = lax.all_gather(wu, "rep", axis=0).transpose(1, 0, 2).reshape(width, f)
    queries = (dot(normed, wq) + query_bias.astype(F32)).astype(BF)
    keys = dot(normed, wk).astype(BF)
    values = (dot(normed, wv) + value_bias.astype(F32)).astype(BF)
    shape = (group, rows, g // head, head)
    qh, kh, vh = (a.reshape(shape) for a in (queries, keys, values))
    lens = small_all[LN].reshape(group, g)[:, 0]
    order = jnp.bitwise_xor(jnp.arange(group, dtype=jnp.int32), me)
    lens = jnp.take(lens, order).astype(jnp.int32)
    pos = jnp.arange(rows, dtype=jnp.int32)
    valid = (pos[None, None, :] <= pos[None, :, None]) & (pos[None, None, :] < lens[:, None, None])
    scores = jnp.einsum("bqhd,bkhd->bhqk", qh, kh, preferred_element_type=F32) * scale
    scores = jnp.where(valid[:, None], scores, -1e30)
    top = jnp.max(scores, axis=-1, keepdims=True)
    expo = jnp.exp(scores - top)
    p = expo / jnp.sum(expo, axis=-1, keepdims=True)
    p_low = p.astype(BF)
    ctx = (
        jnp.einsum("bhqk,bkhd->bqhd", p_low, vh, preferred_element_type=F32)
        .astype(BF)
        .reshape(group * rows, g)
    )
    part = dot(ctx, out_weight).astype(BF).reshape(blocks)
    masks = shard_masks(group)
    work = reduce_shapes(group, rows, width, masks)
    mid, second, mix = call(
        middle_kernel,
        2,
        sizes,
        [((rows, width), F32), (blocks, BF), (blocks, BF)],
        work,
        160,
        (part, x, cot, small_all),
    )
    second = flat(second)
    mixed = flat(mix)
    upper = dot(second, wu) + up_bias.astype(F32)
    cdf = 0.5 * (1.0 + lax.erf(upper * (1.0 / math.sqrt(2.0))))
    pdf = jnp.exp(-0.5 * upper * upper) * (1.0 / math.sqrt(2.0 * math.pi))
    active = (upper * cdf).astype(BF)
    gup = (dot_nt(mixed, down_weight) * (cdf + upper * pdf)).astype(BF)
    gpart = dot_nt(gup, wu).astype(BF).reshape(blocks)
    dpart = dot(active, down_weight).astype(BF).reshape(blocks)
    down_grad = lax.psum(dot_tn(active, mixed).astype(BF), "rep")
    up_part = dot_tn(second, gup).astype(BF).reshape(group, g, f)
    out, gmid, sums3, branch, up_rows = call(
        branch_kernel,
        3,
        sizes,
        [
            ((rows, width), BF),
            ((rows, width), F32),
            ((8, width), F32),
            (blocks, BF),
            ((hidden // width * g, width), BF),
        ],
        work + work,
        200,
        (dpart, gpart, up_part, mid, cot, small_all),
    )
    up_rows, down_grad = lax.optimization_barrier((up_rows, down_grad))
    branch = flat(branch)
    gctx = dot_nt(branch, out_weight).astype(BF).reshape(shape)
    gw = jnp.einsum("bqhd,bkhd->bhqk", gctx, vh, preferred_element_type=F32)
    inner = jnp.sum(p * gw, axis=-1, keepdims=True)
    gs = (p * (gw - inner)).astype(BF)
    join = lambda a: a.astype(BF).reshape(group * rows, g)
    gq = join(jnp.einsum("bhqk,bkhd->bqhd", gs, kh, preferred_element_type=F32) * scale)
    gk = join(jnp.einsum("bhqk,bqhd->bkhd", gs, qh, preferred_element_type=F32) * scale)
    gv = join(jnp.einsum("bhqk,bqhd->bkhd", p_low, gctx, preferred_element_type=F32))
    npart = (dot_nt(gq, wq) + dot_nt(gk, wk) + dot_nt(gv, wv)).astype(BF).reshape(blocks)
    total = lambda a: jnp.sum(a.astype(F32), axis=0)
    cols = jnp.concatenate(
        [
            total(gq)[None],
            total(gv)[None],
            total(gup).reshape(4, g),
            jnp.zeros((2, g), F32),
        ]
    )
    grads = (
        dot_tn(normed, gq).astype(BF).reshape(group, g, g),
        dot_tn(normed, gk).astype(BF).reshape(group, g, g),
        dot_tn(normed, gv).astype(BF).reshape(group, g, g),
        dot_tn(ctx, branch).astype(BF),
    )
    piece = 16
    blocks_up = hidden // width
    tall_all = (4 + blocks_up) * g
    count = (4 + blocks_up) * (g // 2 // piece)
    scratch = (
        list(work)
        + [
            pltpu.VMEM((8, width), F32),
            pltpu.VMEM((group, 8, g), F32),
            pltpu.VMEM((16, g), F32),
            pltpu.VMEM((reps, 16, g), F32),
            pltpu.VMEM((tall_all, width), BF),
            pltpu.VMEM((2, count, piece, width), BF),
        ]
        + [pltpu.SemaphoreType.DMA((4 * count,))] * 2
    )
    gin, smalls, whole = call(
        final_kernel,
        4,
        sizes,
        [((rows, width), BF), ((16, g), F32), ((tall_all, width), BF)],
        scratch,
        200,
        (npart, x, gmid, small_all, sums3, cols) + grads + (up_rows,),
    )
    do, dq, dk, dv = (
        whole[(i + blocks_up) * g : (i + blocks_up + 1) * g].astype(F32) for i in range(4)
    )
    du = whole[: blocks_up * g].reshape(blocks_up, g, width).transpose(1, 0, 2)
    du = du.reshape(g, hidden).astype(F32)
    dd = down_grad.astype(F32)
    return (
        out[None],
        gin[None],
        smalls[FG],
        smalls[FS],
        dq,
        smalls[8],
        dk,
        dv,
        smalls[9],
        do,
        smalls[OB],
        smalls[SG],
        smalls[SS],
        du,
        smalls[10:14].reshape(-1),
        dd,
        smalls[DB],
    )


def solution(mesh):
    tokens = P(("rep", "shard"), None, None)
    vec, mat = P("shard"), P("shard", None)
    return jax.shard_map(
        local,
        mesh=mesh,
        in_specs=(
            tokens,
            P(("rep", "shard")),
            vec,
            vec,
            mat,
            vec,
            mat,
            mat,
            vec,
            mat,
            vec,
            vec,
            vec,
            mat,
            vec,
            mat,
            vec,
            tokens,
        ),
        out_specs=(
            tokens,
            tokens,
            vec,
            vec,
            mat,
            vec,
            mat,
            mat,
            vec,
            mat,
            vec,
            vec,
            vec,
            mat,
            vec,
            mat,
            vec,
        ),
        check_vma=False,
    )
```

time: 866 us -> 640 us (0.74)
  Pallas kernels: 722 us -> 485 us
  between operations: 1.96 us -> 15.4 us
  local copies, waits for them, and re-layouts: 16.7 us -> 30.1 us
  other arithmetic: 25.9 us -> 15.6 us
    pallas_call x4, Pallas kernels: 722 us -> 485 us  [call(): pl.pallas_call(functools.partial(body, sizes), out_shape=[jax.ShapeDtypeS...]
    convert_element_type x6 -> x2, other arithmetic: 17.8 us -> 8.24 us  [the longest x1 4.47 us: local(): dd = down_grad.astype(F32)]
  transfers between devices with their start and end apart: 0 -> 2, of which waited for: 0 -> 1; matrix products, arithmetic and copies ran while one was open for 0% -> 9% of each run, Pallas kernels for 0% -> 30%
where the time goes in v2:
time: 640 us; the launch traced here: 636 us
  Pallas kernels  485 us (76%)
  matrix products  88.6 us (14%)
  local copies, waits for them, and re-layouts  30.1 us (5%)
  other arithmetic  15.6 us (2%)
  between operations  15.4 us (2%)
    pallas_call x4, Pallas kernels, call(): pl.pallas_call(functools.partial(body, sizes), out_shape=[jax.ShapeDtypeS...  485 us
    dot_general x6, matrix products, dot(): return jnp.dot(a, b, preferred_element_type=F32)  32.1 us
    dot_general x6, matrix products, dot_tn(): return jnp.einsum('tr,tc->rc', a, b, preferred_element_type=F32)  24.4 us
    dot_general x6, matrix products, dot_nt(): return jnp.einsum('tc,rc->tr', a, b, preferred_element_type=F32)  22.9 us
  transfers between devices with their start and end apart: 2, of which 1 were waited for; matrix products, arithmetic and copies ran while one was open for 9% of the time, Pallas kernels for 30%

profile of v2, /device:TPU:0, one launch (start us, length us, event | category | flops | bytes accessed | tf_op | source)
XLA Modules:
  0.0 636.3 jit_solution(467902596222665941)
XLA Ops:
  12.6 80.4 %gather_kernel.1 = (bf16[8,128,2048]{2,1,0:T(8,128)(2,1)}, f32[8,2048]{1,0:T(8,128)}, bf16[8,256,256]{2,1,0:T(8,128)(2,1)}, bf16[8,256,256]{2,1,0:T(8,128)(2,1)}...) custom-call(bf16[128,2048]{1,0:T(8,128)(2,1)} %bitcast.136, f32[8,256]{1,0:T(8,128)} %stack.55.small_ref, ...), custom_call_target="tpu_custom_call" | custom-call | tf_op jit(solution)/shard_map/gather_kernel/pallas_call | solution.py:636
  94.1 3.8 fusion.10
  98.8 3.8 fusion.11
  103.8 3.7 convolution_convert_fusion.12
  110.1 2.4 fusion.16
  114.0 3.3 convolution_convert_fusion
  117.3 68.5 %middle_kernel.1 = (f32[128,2048]{1,0:T(8,128)}, bf16[8,128,2048]{2,1,0:T(8,128)(2,1)}, bf16[8,128,2048]{2,1,0:T(8,128)(2,1)}) custom-call(bf16[8,128,2048]{2,1,0:T(8,128)(2,1)} %bitcast.132, bf16[128,2048]{1,0:T(8,128)(2,1)} %bitcast.137, bf16[128,2048]{1,0:T(8,128)(2,1)} %bitcast.150, f32[8,2048]{1,0:T(8,128)} %get-tuple-element.38.small.refs_3_), custom_call_target="tpu_custom_call" | custom-call | tf_op jit(solution)/shard_map/middle_kernel/pallas_call | solution.py:636
  185.8 6.2 copy.74
  192.1 8.1 %multiply_convert_fusion = (bf16[1024,1024]{1,0:T(8,128)(2,1)S(1)}, f32[1024,1024]{1,0:T(8,128)S(1)}) fusion(f32[1024]{0:T(1024)S(1)} %convert_element_type.156, bf16[1024,2048]{1,0:T(8,128)(2,1)} %bitcast.193, bf16[2048,1024]{0,1:T(8,128)(2,1)} %bitcast.142), kind=kOutput, calls=%fused_computation.12 | convolution fusion | flops 4301258752 | bytes 14684160 | tf_op jit(solution)/shard_map/dot_general | solution.py:651
  200.2 6.1 convert_reduce_fusion
  206.4 6.4 %convolution_convert_fusion.2 = bf16[2048,1024]{1,0:T(8,128)(2,1)} fusion(bf16[1024,2048]{1,0:T(8,128)(2,1)S(1)} %bitcast.194, bf16[1024,1024]{1,0:T(8,128)(2,1)S(1)} %get-tuple-element.74), kind=kOutput, calls=%fused_computation.16 | convolution fusion | flops 4297064448 | bytes 10485760 | tf_op jit(solution)/shard_map/tr,tc->rc/dot_general | solution.py:659
  212.8 6.1 convolution_convert_fusion.3
  218.8 6.2 convolution_convert_fusion.1
  225.1 9.3 %convolution_convert_fusion.4 = bf16[1024,2048]{1,0:T(8,128)(2,1)} fusion(bf16[1024,1024]{1,0:T(8,128)(2,1)} %copy-done.21, bf16[1024,2048]{1,0:T(8,128)(2,1)} %param.33), kind=kOutput, calls=%fused_computation.18 | convolution fusion | flops 4297064448 | bytes 10485760 | tf_op jit(solution)/shard_map/dot_general | solution.py:651
  234.4 119.5 %branch_kernel.1 = (bf16[128,2048]{1,0:T(8,128)(2,1)}, f32[128,2048]{1,0:T(8,128)}, f32[8,2048]{1,0:T(8,128)}, bf16[8,128,2048]{2,1,0:T(8,128)(2,1)}, bf16[1024,2048]{1,0:T(8,128)(2,1)}) custom-call(bf16[8,128,2048]{2,1,0:T(8,128)(2,1)} %bitcast.141, bf16[8,128,2048]{2,1,0:T(8,128)(2,1)} %bitcast.140, bf16[8,256,1024]{2,1,0:T(8,128)(2,1)} %bitcast.139, ...), custom_call_target="tpu_custom_call" | custom-call | tf_op jit(solution)/shard_map/branch_kernel/pallas_call | solution.py:636
  354.0 4.3 convolution_convert_fusion.11
  370.4 4.7 convolution_convert_fusion.5.refs_9_
  379.9 2.4 convolution_convert_fusion.7
  385.3 3.4 add_convert_fusion
  390.0 216.7 %final_kernel.1 = (bf16[128,2048]{1,0:T(8,128)(2,1)}, f32[16,256]{1,0:T(8,128)}, bf16[2048,2048]{1,0:T(8,128)(2,1)}) custom-call(bf16[8,128,2048]{2,1,0:T(8,128)(2,1)} %bitcast.134, bf16[128,2048]{1,0:T(8,128)(2,1)} %bitcast.138, f32[128,2048]{1,0:T(8,128)} %get-tuple-element.47.refs_2_, f32[8,2048]{1,0:T(8,128)} %get-tuple-element.38.small.refs_3_, ...), custom_call_target="tpu_custom_call" | custom-call | tf_op jit(solution)/shard_map/final_kernel/pallas_call | solution.py:636
  608.9 2.7 slice.61
  613.6 3.8 slice_convert_fusion
  619.0 4.2 copy.92
  623.2 4.5 convert_element_type.187
  (103 shorter events, 40.3 us)
Async XLA Ops:
  7.2 106.8 %copy-start = (bf16[256,2048]{1,0:T(8,128)(2,1)S(1)}, bf16[256,2048]{1,0:T(8,128)(2,1)}, u32[]{:S(2)}) copy-start(bf16[256,2048]{1,0:T(8,128)(2,1)} %param.27) | copy-start | bytes 3145732
  7.2 178.6 %all-gather.2.cloned.1.call-start = ((), (), s32[]{:S(2)}) async-start(), calls=%async_computation | async-start | bytes 5242880 | tf_op jit(solution)/shard_map/all_gather | solution.py:725
  12.5 80.5 %copy-start.19 = (bf16[256]{0:T(256)(128)(2,1)S(1)}, bf16[256]{0:T(256)(128)(2,1)}, u32[]{:S(2)}) copy-start(bf16[256]{0:T(256)(128)(2,1)} %param.23) | copy-start | bytes 1540
  12.5 80.5 %copy-start.20 = (bf16[256]{0:T(256)(128)(2,1)S(1)}, bf16[256]{0:T(256)(128)(2,1)}, u32[]{:S(2)}) copy-start(bf16[256]{0:T(256)(128)(2,1)} %param.26) | copy-start | bytes 1540
  12.6 80.6 %copy-start.14 = (bf16[1024]{0:T(1024)(128)(2,1)S(1)}, bf16[1024]{0:T(1024)(128)(2,1)}, u32[]{:S(2)}) copy-start(bf16[1024]{0:T(1024)(128)(2,1)} %param.32) | copy-start | bytes 6148
  93.0 297.0 %all-reduce.2.cloned.1.call-start = ((), (), s32[]{:S(2)}) async-start(), calls=%async_computation.1 | async-start | bytes 8388608 | tf_op jit(solution)/shard_map/psum | solution.py:768
  94.1 4.8 copy-start.9
  107.6 2.5 copy-start.7
  192.1 8.2 %copy-start.15 = (bf16[1024,2048]{1,0:T(8,128)(2,1)S(1)}, bf16[1024,2048]{1,0:T(8,128)(2,1)}, u32[]{:S(2)}) copy-start(bf16[1024,2048]{1,0:T(8,128)(2,1)} %param.33) | copy-start | bytes 12582916
  192.1 8.2 %copy-start.17 = (bf16[8,128,2048]{2,1,0:T(8,128)(2,1)S(1)}, bf16[8,128,2048]{2,1,0:T(8,128)(2,1)}, u32[]{:S(2)}) copy-start(bf16[8,128,2048]{2,1,0:T(8,128)(2,1)} %get-tuple-element.43) | copy-start | bytes 12582916
  200.2 18.6 %copy-start.21 = (bf16[1024,1024]{1,0:T(8,128)(2,1)}, bf16[1024,1024]{1,0:T(8,128)(2,1)S(1)}, u32[]{:S(2)}) copy-start(bf16[1024,1024]{1,0:T(8,128)(2,1)S(1)} %get-tuple-element.69) | copy-start | bytes 6291460
  200.2 6.1 copy-start.18
  206.4 6.4 %copy-start.4 = (bf16[4,2048,256]{1,2,0:T(8,128)(2,1)S(1)}, bf16[4,2048,256]{1,2,0:T(8,128)(2,1)}, u32[]{:S(2)}) copy-start(bf16[4,2048,256]{1,2,0:T(8,128)(2,1)} %copy.74) | copy-start | bytes 12582916
  358.3 4.1 copy-start.5
  362.6 0.8 copy-start.6
  369.7 5.4 copy-start.16
  379.9 2.4 copy-start.11
  382.2 1.3 copy-start.10
  383.6 1.8 copy-start.8
  608.9 4.6 copy-start.2
  619.0 4.2 copy-start.3
  623.2 4.5 copy-start.12
  623.2 5.3 copy-start.13
  623.2 6.1 copy-start.1
Sparse Core Ops, SparseCore 0:
  93.1 81.1 all-gather.1
  234.6 155.3 all-reduce.1

commit v3 on v2

--- a/solution.py
+++ b/solution.py
@@ -13,8 +13,8 @@
 BF = jnp.bfloat16
 F32 = jnp.float32
 VM = pl.BlockSpec(memory_space=pltpu.VMEM)
-LIMIT = 60 * 2**20
-SIZE = None
+ANY = pl.BlockSpec(memory_space=pl.ANY)
+LIMIT = 63 * 2**20
 
 
 def flip(index, mask):
@@ -79,9 +79,12 @@
         copy.start()
         return copy
 
-    def finish(self):
-        for copy in self.open:
+    def settle(self, count=None):
+        for copy in self.open[:count]:
             copy.wait_send()
+        self.open = self.open[len(self.open) if count is None else count :]
+
+    finish = settle
 
 
 def meet(shard_set, rep_set):
@@ -370,70 +373,9 @@
     net.finish()
 
 
-def branch_kernel(
-    sizes, down, grad, up, mid, cot, small, out, gmid, sums, branch, up_rows, *work
-):
-    group, _ = sizes
-    net = Net(*work[-2:])
-    masks = shard_masks(group)
-    meet(range(1, group), [])
-    me = lax.axis_index("shard")
-    width = small.shape[1] // group
-    rows = mid.shape[0]
-    length = small[LN : LN + 1, pl.ds(pl.multiple_of(me * width, width), 128)][:, :1]
-    red = Reduce(net, grad, work[:2], masks)
-    red.run()
-    late = Reduce(net, down, work[2:4], masks)
-    late.begin()
-    sums[...] = jnp.zeros_like(sums)
-    gather = Gather(net, branch, masks)
-    for n in range(2):
-        red.advance(n, red.steps - 1)
-
-        def back(at, start):
-            g = red.total(at)
-            v, inv = norm_rows(mid[at])
-            gout = cot[at].astype(F32) * live_rows(length, start, 16)
-            res = gout + norm_back(g, small[SG : SG + 1], v, inv)
-            gmid[at] = res
-            low = res.astype(BF)
-            branch[0, at] = low
-            sums[SG : SG + 1] += jnp.sum(g * v, axis=0, keepdims=True)
-            sums[SS : SS + 1] += jnp.sum(g, axis=0, keepdims=True)
-            sums[OB : OB + 1] += jnp.sum(low.astype(F32), axis=0, keepdims=True)
-            sums[DB : DB + 1] += jnp.sum(gout, axis=0, keepdims=True)
-
-        by_rows(n, rows, back)
-        gather.start(n)
-    wide = up.shape[2]
-    each = mid.shape[1] // wide
-    place = pl.ds(pl.multiple_of((me % each) * wide, wide), wide)
-    tall = up.shape[1]
-    down_to = pl.ds(pl.multiple_of((me // each) * tall, tall), tall)
-    target = up_rows.at[down_to, place]
-    moved = [net.to("shard", j, up.at[flip(me, j)], target) for j in range(1, group)]
-    own = net.own(up.at[me], target)
-    late.prepare()
-    for k in range(gather.steps):
-        gather.both()
-        for n in range(2):
-            late.advance(n, k)
-    gather.end()
-    for n in range(2):
-
-        def close(at, start):
-            v = mid[at] + (late.total(at) + small[DB : DB + 1])
-            out[at] = (v * live_rows(length, start, 16)).astype(BF)
-
-        by_rows(n, rows, close)
-    for copy in moved:
-        copy.wait_recv()
-    own.wait()
-    net.finish()
-
-
 class Line:
-    def __init__(self, own, land, out, tall, reps, sems):
+    def __init__(self, own, land, out, tall, reps, sems, kept):
+        self.kept = kept
         self.own, self.land, self.out = own, land, out
         self.rep, self.reps, self.sems = lax.axis_index("rep"), reps, sems
         self.count, self.size = land.shape[1], land.shape[2]
@@ -483,9 +425,9 @@
 
             @pl.when(at == last)
             def _():
-                out = self.out.at[rows]
-                self.add(land, rows, out)
-                self.copy(out, out, way, 1, i, way != 0).start()
+                self.add(land, rows, land)
+                self.copy(land, self.out.at[rows], way, 1, i, way != 0).start()
+                self.keep(way, i).start()
 
     def add(self, land, rows, to):
         own, step = self.own.at[rows], 16
@@ -494,6 +436,13 @@
         def _(n):
             at = pl.ds(pl.multiple_of(n * step, step), step)
             to[at] = (land[at].astype(F32) + own[at].astype(F32)).astype(BF)
+
+    def keep(self, way, i):
+        return pltpu.make_async_copy(
+            self.land.at[way, i],
+            self.out.at[self.rows(way, i)],
+            self.kept.at[way * self.count + i],
+        )
 
     def back(self, way, t):
         at, last = self.place(way), self.reps - 1
@@ -531,66 +480,209 @@
                 def _():
                     self.copy(out, out, way, 1, i, way != 0).wait_send()
 
-
-def final_kernel(sizes, *refs):
+                @pl.when(at == last)
+                def _():
+                    self.keep(way, i).wait()
+
+
+def final_kernel(sizes, head, *refs):
     group, reps = sizes
-    grad, x_ref, gmid, small, sums3, cols = refs[:6]
-    arrays = refs[6:10]
-    up_rows = refs[10]
-    gin, smalls = refs[11:13]
-    whole = refs[13]
-    work = refs[14:]
-    sums, land, both, zland, mine_all, line_land = work[2:8]
+    (
+        gpart,
+        dpart,
+        up_part,
+        down_grad,
+        mid,
+        cot,
+        x_ref,
+        small,
+        q,
+        k,
+        v,
+        p_ref,
+        ctx,
+        nrm,
+        wq,
+        wk,
+        wv,
+        wo,
+        cols,
+    ) = refs[:19]
+    out, gin, smalls, whole = refs[19:23]
+    work = refs[23:]
+    gmid, sums, land, both, zland, own_all, line_land = work[4:11]
+    part, branch, g3, dw, nbuf, wbuf, loads = work[11:18]
+    line_sems, kept = work[18:20], work[20]
     net = Net(*work[-2:])
     masks = shard_masks(group)
     me, rep = lax.axis_index("shard"), lax.axis_index("rep")
+    width, rows, model = smalls.shape[1], x_ref.shape[0], x_ref.shape[1]
+    heads = width // head
+    scale = 1.0 / math.sqrt(head)
+    tall = width
+    down_rows, wide = down_grad.shape[0], up_part.shape[2]
+    up_base = down_rows
+    out_base = up_base + tall * (wide * group // model)
+    loaded = [
+        net.own(gpart, part),
+        net.own(down_grad, own_all.at[pl.ds(0, down_rows)]),
+    ]
     meet(range(1, group), range(1, reps))
-    width, rows = smalls.shape[1], x_ref.shape[0]
-    place = pl.ds(pl.multiple_of(me * width, width), width)
-    tall = arrays[3].shape[0]
-    wide = up_rows.shape[0]
-    moved = [[net.own(up_rows, mine_all.at[0:wide]), net.own(arrays[3], mine_all.at[pl.ds(wide, tall)])]]
-    for i, src in enumerate(arrays[:3]):
-        dst = mine_all.at[pl.ds(wide + (i + 1) * tall, tall)]
-        moved.append(
-            [
-                net.to("shard", j, src.at[flip(me, j)], dst.at[:, place])
-                for j in range(1, group)
+    length = small[LN : LN + 1, pl.ds(pl.multiple_of(me * width, width), 128)][:, :1]
+    line = Line(own_all, line_land, whole, tall, reps, line_sems, kept)
+    for copy in loaded:
+        copy.wait()
+    arrivals = {}
+
+    def place(j):
+        return pl.ds(pl.multiple_of(flip(me, j) * width, width), width)
+
+    def tasks():
+        red = Reduce(net, part, work[:2], masks)
+        red.begin()
+        yield 3
+        red.prepare()
+        each = model // wide
+        target = own_all.at[
+            pl.ds(pl.multiple_of(up_base + (me // each) * tall, tall), tall),
+            pl.ds(pl.multiple_of((me % each) * wide, wide), wide),
+        ]
+        arrivals[up_base] = [
+            net.to("shard", j, up_part.at[flip(me, j)], target) for j in range(1, group)
+        ] + [net.own(up_part.at[me], target)]
+        yield 22
+        for s in range(red.steps - 1):
+            for n in range(2):
+                red.advance(n, s)
+        yield 28
+        for n in range(2):
+            red.advance(n, red.steps - 1)
+        net.settle()
+        sums[...] = jnp.zeros_like(sums)
+        gather = Gather(net, branch, masks)
+        for n in range(2):
+
+            def back(at, start):
+                g = red.total(at)
+                w, inv = norm_rows(mid[at])
+                gout = cot[at].astype(F32) * live_rows(length, start, 16)
+                res = gout + norm_back(g, small[SG : SG + 1], w, inv)
+                gmid[at] = res
+                low = res.astype(BF)
+                branch[0, at] = low
+                sums[SG : SG + 1] += jnp.sum(g * w, axis=0, keepdims=True)
+                sums[SS : SS + 1] += jnp.sum(g, axis=0, keepdims=True)
+                sums[OB : OB + 1] += jnp.sum(low.astype(F32), axis=0, keepdims=True)
+                sums[DB : DB + 1] += jnp.sum(gout, axis=0, keepdims=True)
+
+            by_rows(n, rows, back)
+            gather.start(n)
+        for s in range(gather.steps):
+            yield 33 + 5 * s
+            gather.both()
+        yield 33 + 5 * gather.steps
+        gather.end()
+        early = len(net.open)
+        for b in range(group):
+            at = pl.ds(b * rows, rows)
+            gc = dot_nt(branch[b], wo[...]).astype(BF)
+            for h in range(heads):
+                lane = pl.ds(h * head, head)
+                qh, kh, vh = q[at, lane], k[at, lane], v[at, lane]
+                gch = gc[:, h * head : (h + 1) * head]
+                p = p_ref[b, h]
+                gw = dot_nt(gch, vh)
+                inner = jnp.sum(p * gw, axis=-1, keepdims=True)
+                gs = (p * (gw - inner)).astype(BF)
+                g3[b, :, pl.ds(h * head, head)] = (dot(gs, kh) * scale).astype(BF)
+                g3[b, :, pl.ds(width + h * head, head)] = (dot_tn(gs, qh) * scale).astype(BF)
+                g3[b, :, pl.ds(2 * width + h * head, head)] = dot_tn(p.astype(BF), gch).astype(BF)
+            yield 0
+        n_col = 512
+        for c in range(0, model, n_col):
+            lane = pl.ds(c, n_col)
+            full = branch[:, :, lane].reshape(group * rows, n_col)
+            own_all[pl.ds(out_base, tall), lane] = dot_tn(ctx[...], full).astype(BF)
+            yield 0
+        arrivals[out_base] = []
+        grads = g3[...].reshape(group * rows, 3 * width)
+        total = jnp.sum(grads.astype(F32), axis=0, keepdims=True)
+        both[8:9] = total[:, :width]
+        both[9:10] = total[:, 2 * width :]
+        both[10:16] = cols[...]
+
+        def normed_of(j):
+            return pltpu.make_async_copy(nrm.at[:, :, place(j)], nbuf.at[j % 2], loads.at[0, j % 2])
+
+        normed_of(0).start()
+        for i in range(3):
+            arrivals[out_base + (i + 1) * tall] = []
+        for j in range(group):
+            if j + 1 < group:
+                normed_of(j + 1).start()
+            normed_of(j).wait()
+            left = nbuf[j % 2].reshape(group * rows, width)
+            right = g3[...].reshape(group * rows, 3 * width)
+            dw[j] = dot_tn(left, right).astype(BF)
+            for i in range(3):
+                src = dw.at[j, :, pl.ds(i * width, width)]
+                base = out_base + (i + 1) * tall
+                dst = own_all.at[pl.ds(base, tall), place(0)]
+                copy = net.to("shard", j, src, dst) if j else net.own(src, dst)
+                arrivals[base].insert(len(arrivals[base]) if j == 0 else 0, copy)
+            yield 0
+
+        def weight_of(a):
+            return [
+                pltpu.make_async_copy(w.at[a], wbuf.at[a % 2, i], loads.at[1 + i, a % 2])
+                for i, w in enumerate((wq, wk, wv))
             ]
-            + [net.own(src.at[me], dst.at[:, place])]
-        )
-    line = Line(mine_all, line_land, whole, tall, reps, work[-4:-2])
-    red = Reduce(net, grad, work[:2], masks)
-
-    def tasks():
+
+        for copy in weight_of(0):
+            copy.start()
+        for a in range(group):
+            if a + 1 < group:
+                for copy in weight_of(a + 1):
+                    copy.start()
+            for copy in weight_of(a):
+                copy.wait()
+            left = g3[...].reshape(group * rows, 3 * width)
+            res = dot_nt(left[:, :width], wbuf[a % 2, 0])
+            res = res + dot_nt(left[:, width : 2 * width], wbuf[a % 2, 1])
+            res = res + dot_nt(left[:, 2 * width :], wbuf[a % 2, 2])
+            part[:, :, pl.ds(a * width, width)] = res.astype(BF).reshape(group, rows, width)
+            yield 0
+        red = Reduce(net, part, work[:2], masks)
         red.begin()
-        yield
+        net.settle(early)
+        own = net.own(dpart, branch)
+        yield 62
+        own.wait()
+        late = Reduce(net, branch, work[2:4], masks)
+        late.begin()
+        yield 66
         red.prepare()
-        for k in range(red.steps - 1):
+        for s in range(red.steps - 1):
+            yield 74 + 4 * s
             for n in range(2):
-                yield
-                red.advance(n, k)
-        sums[...] = sums3[...]
+                red.advance(n, s)
+        yield 79
         for n in range(2):
-            yield
             red.advance(n, red.steps - 1)
 
-            def back(at, start):
+            def first(at, start):
                 g = red.total(at)
                 w, inv = norm_rows(x_ref[at].astype(F32))
                 gin[at] = (gmid[at] + norm_back(g, small[FG : FG + 1], w, inv)).astype(BF)
                 sums[FG : FG + 1] += jnp.sum(g * w, axis=0, keepdims=True)
                 sums[FS : FS + 1] += jnp.sum(g, axis=0, keepdims=True)
 
-            by_rows(n, rows, back)
-
-        def mine(j):
-            return pl.ds(pl.multiple_of(flip(me, j) * width, width), width)
-
-        tiny = [net.to("shard", j, sums.at[:, mine(j)], land.at[me]) for j in range(1, group)]
-        own = net.own(sums.at[:, mine(0)], land.at[me])
-        yield
-        yield
+            by_rows(n, rows, first)
+        tiny = [net.to("shard", j, sums.at[:, place(j)], land.at[me]) for j in range(1, group)]
+        own = net.own(sums.at[:, place(0)], land.at[me])
+        yield 81
+        late.prepare()
+        yield 83
         for copy in tiny:
             copy.wait_recv()
         own.wait()
@@ -598,12 +690,22 @@
         for j in range(1, group):
             total = total + land[j]
         both[0:8] = total
-        both[8:16] = cols[...]
         tiny = [net.to("rep", h, both, zland.at[rep]) for h in range(1, reps)]
         own = net.own(both, zland.at[rep])
-        yield
-        yield
-        yield
+        for s in range(late.steps - 1):
+            yield 89 + 4 * s
+            for n in range(2):
+                late.advance(n, s)
+        yield 93
+        for n in range(2):
+            late.advance(n, late.steps - 1)
+
+            def close(at, start):
+                m = mid[at] + (late.total(at) + small[DB : DB + 1])
+                out[at] = (m * live_rows(length, start, 16)).astype(BF)
+
+            by_rows(n, rows, close)
+        yield 96
         for copy in tiny:
             copy.wait_recv()
         own.wait()
@@ -613,31 +715,32 @@
         smalls[...] = total
 
     todo = tasks()
-    next(todo)
+    resume = next(todo)
     for t in range(line.steps):
-        i = t // line.each - wide // tall
-        if t == 0:
-            for copy in moved[0]:
-                copy.wait()
-        elif t < line.count and t % line.each == 0 and i > 0:
-            for copy in moved[i][:-1]:
-                copy.wait_recv()
-            moved[i][-1].wait()
+        base = t // line.each * tall
+        if t < line.count and t % line.each == 0 and (base == up_base or base >= out_base):
+            while base not in arrivals:
+                resume = next(todo, None)
+            for copy in arrivals.get(base, []):
+                if copy is arrivals[base][-1]:
+                    copy.wait()
+                else:
+                    copy.wait_recv()
         line.step(t)
-        if t >= 15 and t % 4 == 3:
-            next(todo, None)
+        if resume is not None and t >= resume:
+            resume = next(todo, None)
     for _ in todo:
         pass
     line.finish()
     net.finish()
 
 
-def call(body, number, sizes, outs, scratch, copies, args):
+def call(body, number, sizes, outs, scratch, copies, args, far=(), far_outs=()):
     return pl.pallas_call(
-        functools.partial(body, sizes),
+        functools.partial(body, *sizes),
         out_shape=[jax.ShapeDtypeStruct(s, d) for s, d in outs],
-        in_specs=[VM] * len(args),
-        out_specs=[VM] * len(outs),
+        in_specs=[ANY if i in far else VM for i in range(len(args))],
+        out_specs=[ANY if i in far_outs else VM for i in range(len(outs))],
         scratch_shapes=list(scratch)
         + [pltpu.SemaphoreType.DMA((copies,)), pltpu.SemaphoreType.DMA((copies,))],
         compiler_params=pltpu.CompilerParams(
@@ -705,7 +808,7 @@
     nrm, small_all, wq, wk, wv, wu = call(
         gather_kernel,
         1,
-        sizes,
+        (sizes,),
         [
             (blocks, BF),
             ((8, width), F32),
@@ -750,7 +853,7 @@
     mid, second, mix = call(
         middle_kernel,
         2,
-        sizes,
+        (sizes,),
         [((rows, width), F32), (blocks, BF), (blocks, BF)],
         work,
         160,
@@ -765,80 +868,78 @@
     gup = (dot_nt(mixed, down_weight) * (cdf + upper * pdf)).astype(BF)
     gpart = dot_nt(gup, wu).astype(BF).reshape(blocks)
     dpart = dot(active, down_weight).astype(BF).reshape(blocks)
-    down_grad = lax.psum(dot_tn(active, mixed).astype(BF), "rep")
+    down_grad = dot_tn(active, mixed).astype(BF)
     up_part = dot_tn(second, gup).astype(BF).reshape(group, g, f)
-    out, gmid, sums3, branch, up_rows = call(
-        branch_kernel,
-        3,
-        sizes,
-        [
-            ((rows, width), BF),
-            ((rows, width), F32),
-            ((8, width), F32),
-            (blocks, BF),
-            ((hidden // width * g, width), BF),
-        ],
-        work + work,
-        200,
-        (dpart, gpart, up_part, mid, cot, small_all),
+    cols = jnp.concatenate(
+        [jnp.sum(gup.astype(F32), axis=0).reshape(4, g), jnp.zeros((2, g), F32)]
     )
-    up_rows, down_grad = lax.optimization_barrier((up_rows, down_grad))
-    branch = flat(branch)
-    gctx = dot_nt(branch, out_weight).astype(BF).reshape(shape)
-    gw = jnp.einsum("bqhd,bkhd->bhqk", gctx, vh, preferred_element_type=F32)
-    inner = jnp.sum(p * gw, axis=-1, keepdims=True)
-    gs = (p * (gw - inner)).astype(BF)
-    join = lambda a: a.astype(BF).reshape(group * rows, g)
-    gq = join(jnp.einsum("bhqk,bkhd->bqhd", gs, kh, preferred_element_type=F32) * scale)
-    gk = join(jnp.einsum("bhqk,bqhd->bkhd", gs, qh, preferred_element_type=F32) * scale)
-    gv = join(jnp.einsum("bhqk,bqhd->bkhd", p_low, gctx, preferred_element_type=F32))
-    npart = (dot_nt(gq, wq) + dot_nt(gk, wk) + dot_nt(gv, wv)).astype(BF).reshape(blocks)
-    total = lambda a: jnp.sum(a.astype(F32), axis=0)
-    cols = jnp.concatenate(
-        [
-            total(gq)[None],
-            total(gv)[None],
-            total(gup).reshape(4, g),
-            jnp.zeros((2, g), F32),
-        ]
-    )
-    grads = (
-        dot_tn(normed, gq).astype(BF).reshape(group, g, g),
-        dot_tn(normed, gk).astype(BF).reshape(group, g, g),
-        dot_tn(normed, gv).astype(BF).reshape(group, g, g),
-        dot_tn(ctx, branch).astype(BF),
-    )
+    blocks_up = hidden // width
+    tall_all = f + (4 + blocks_up) * g
     piece = 16
-    blocks_up = hidden // width
-    tall_all = (4 + blocks_up) * g
-    count = (4 + blocks_up) * (g // 2 // piece)
+    count = tall_all // 2 // piece
     scratch = (
-        list(work)
+        work
+        + work
         + [
+            pltpu.VMEM((rows, width), F32),
             pltpu.VMEM((8, width), F32),
             pltpu.VMEM((group, 8, g), F32),
             pltpu.VMEM((16, g), F32),
             pltpu.VMEM((reps, 16, g), F32),
             pltpu.VMEM((tall_all, width), BF),
             pltpu.VMEM((2, count, piece, width), BF),
+            pltpu.VMEM(blocks, BF),
+            pltpu.VMEM(blocks, BF),
+            pltpu.VMEM((group, rows, 3 * g), BF),
+            pltpu.VMEM((group, g, 3 * g), BF),
+            pltpu.VMEM((2, group, rows, g), BF),
+            pltpu.VMEM((2, 3, g, g), BF),
+            pltpu.SemaphoreType.DMA((4, 2)),
         ]
         + [pltpu.SemaphoreType.DMA((4 * count,))] * 2
+        + [pltpu.SemaphoreType.DMA((2 * count,))]
     )
-    gin, smalls, whole = call(
+    out, gin, smalls, whole = call(
         final_kernel,
-        4,
-        sizes,
-        [((rows, width), BF), ((16, g), F32), ((tall_all, width), BF)],
+        3,
+        (sizes, head),
+        [
+            ((rows, width), BF),
+            ((rows, width), BF),
+            ((16, g), F32),
+            ((tall_all, width), BF),
+        ],
         scratch,
-        200,
-        (npart, x, gmid, small_all, sums3, cols) + grads + (up_rows,),
+        320,
+        (
+            gpart,
+            dpart,
+            up_part,
+            down_grad,
+            mid,
+            cot,
+            x,
+            small_all,
+            queries,
+            keys,
+            values,
+            p,
+            ctx,
+            nrm,
+            wq.reshape(group, g, g),
+            wk.reshape(group, g, g),
+            wv.reshape(group, g, g),
+            out_weight,
+            cols,
+        ),
+        (0, 1, 2, 3, 13, 14, 15, 16),
+        (3,),
     )
-    do, dq, dk, dv = (
-        whole[(i + blocks_up) * g : (i + blocks_up + 1) * g].astype(F32) for i in range(4)
-    )
-    du = whole[: blocks_up * g].reshape(blocks_up, g, width).transpose(1, 0, 2)
+    dd = whole[:f].astype(F32)
+    du = whole[f : f + blocks_up * g].reshape(blocks_up, g, width).transpose(1, 0, 2)
     du = du.reshape(g, hidden).astype(F32)
-    dd = down_grad.astype(F32)
+    skip = f + blocks_up * g
+    do, dq, dk, dv = (whole[skip + i * g : skip + (i + 1) * g].astype(F32) for i in range(4))
     return (
         out[None],
         gin[None],

time: 640 us -> 590 us (0.922)
  matrix products: 88.6 us -> 58.8 us
  Pallas kernels: 485 us -> 466 us
    pallas_call x4 -> x3, Pallas kernels: 485 us -> 466 us  [call(): pl.pallas_call(functools.partial(body, *sizes), out_shape=[jax.ShapeDtype...]
    dot_general x6 -> x2, matrix products: 24.4 us -> 12.5 us  [dot_tn(): return jnp.einsum('tr,tc->rc', a, b, preferred_element_type=F32)]
    dot_general x6 -> x2, matrix products: 22.9 us -> 12.2 us  [dot_nt(): return jnp.einsum('tc,rc->tr', a, b, preferred_element_type=F32)]
    dot_general x5 -> x0, matrix products: 6.7 us -> none  [the longest x1 2.31 us: local(): jnp.einsum('bhqk,bqhd->bkhd', p_low, gctx, preferred_element_type=F32)]
  transfers between devices with their start and end apart: 2 -> 1, of which waited for: 1 -> 0; matrix products, arithmetic and copies ran while one was open for 9% -> 5% of each run, Pallas kernels for 30% -> 12%
where the time goes in v3:
time: 590 us; the launch traced here: 582 us
  Pallas kernels  466 us (79%)
  matrix products  58.8 us (10%)
  local copies, waits for them, and re-layouts  24.7 us (4%)
  other arithmetic  17.7 us (3%)
  between operations  15.5 us (3%)
    pallas_call x3, Pallas kernels, call(): pl.pallas_call(functools.partial(body, *sizes), out_shape=[jax.ShapeDtype...  466 us
    dot_general x6, matrix products, dot(): return jnp.dot(a, b, preferred_element_type=F32)  29.7 us
    dot_general x2, matrix products, dot_tn(): return jnp.einsum('tr,tc->rc', a, b, preferred_element_type=F32)  12.5 us
    dot_general x2, matrix products, dot_nt(): return jnp.einsum('tc,rc->tr', a, b, preferred_element_type=F32)  12.2 us
  transfers between devices with their start and end apart: 1, of which 0 were waited for; matrix products, arithmetic and copies ran while one was open for 5% of the time, Pallas kernels for 12%

profile of v3, /device:TPU:0, one launch (start us, length us, event | category | flops | bytes accessed | tf_op | source)
XLA Modules:
  0.0 582.3 jit_solution(3977584496614752980)
XLA Ops:
  12.5 80.5 %gather_kernel.1 = (bf16[8,128,2048]{2,1,0:T(8,128)(2,1)}, f32[8,2048]{1,0:T(8,128)}, bf16[8,256,256]{2,1,0:T(8,128)(2,1)}, bf16[8,256,256]{2,1,0:T(8,128)(2,1)}...) custom-call(bf16[128,2048]{1,0:T(8,128)(2,1)} %bitcast.78, f32[8,256]{1,0:T(8,128)} %stack.55.small_ref, ...), custom_call_target="tpu_custom_call" | custom-call | tf_op jit(solution)/shard_map/gather_kernel/pallas_call | solution.py:739
  94.0 3.8 convolution_convert_fusion.6.refs_9_
  98.8 3.8 fusion.10.refs_10_
  102.8 4.0 fusion.11.refs_8_
  108.6 3.1 fusion.20
  111.7 1.6 broadcast_divide_fusion.refs_11_
  114.2 1.3 fusion.12
  115.5 1.3 copy.55
  117.7 3.3 convolution_convert_fusion
  121.0 68.2 %middle_kernel.1 = (f32[128,2048]{1,0:T(8,128)}, bf16[8,128,2048]{2,1,0:T(8,128)(2,1)}, bf16[8,128,2048]{2,1,0:T(8,128)(2,1)}) custom-call(bf16[8,128,2048]{2,1,0:T(8,128)(2,1)} %bitcast.73, bf16[128,2048]{1,0:T(8,128)(2,1)} %bitcast.79, bf16[128,2048]{1,0:T(8,128)(2,1)} %bitcast.90, f32[8,2048]{1,0:T(8,128)} %get-tuple-element.32.small.refs_7_), custom_call_target="tpu_custom_call" | custom-call | tf_op jit(solution)/shard_map/middle_kernel/pallas_call | solution.py:739
  189.2 6.2 %copy.56 = bf16[4,2048,256]{1,2,0:T(8,128)(2,1)} copy(bf16[4,2048,256]{2,1,0:T(8,128)(2,1)} %all-gather.2.cloned.1.call-done) | data formatting | bytes 8388608 | tf_op jit(solution)/shard_map/all_gather | solution.py:828
  195.4 8.7 %multiply_convert_fusion = (bf16[1024,1024]{1,0:T(8,128)(2,1)S(1)}, f32[1024,1024]{1,0:T(8,128)S(1)}) fusion(f32[1024]{0:T(1024)S(1)} %convert_element_type.109, bf16[1024,2048]{1,0:T(8,128)(2,1)} %bitcast.115, bf16[2048,1024]{0,1:T(8,128)(2,1)} %bitcast.81), kind=kOutput, calls=%fused_computation.12 | convolution fusion | flops 4301258752 | bytes 14684160 | tf_op jit(solution)/shard_map/dot_general | solution.py:754
  204.1 6.1 %convert_reduce_fusion = (f32[1024]{0:T(1024)S(1)}, bf16[1024,1024]{1,0:T(8,128)(2,1)S(1)}) fusion(f32[1024,1024]{1,0:T(8,128)S(1)} %get-tuple-element.60, f32[1024]{0:T(1024)S(1)} %convert_element_type.109, bf16[1024,2048]{1,0:T(8,128)(2,1)S(1)} %bitcast.113, bf16[1024,2048]{1,0:T(8,128)(2,1)S(1)} %copy-done.11), kind=kOutput, calls=%fused_computation.11 | convolution fusion | flops 4308597760 | bytes 14688256 | tf_op jit(solution)/shard_map/tc,rc->tr/dot_general | solution.py:758
  210.2 6.2 %convolution_convert_fusion.2 = bf16[2048,1024]{1,0:T(8,128)(2,1)} fusion(bf16[1024,2048]{1,0:T(8,128)(2,1)S(1)} %bitcast.116, bf16[1024,1024]{1,0:T(8,128)(2,1)S(1)} %get-tuple-element.62), kind=kOutput, calls=%fused_computation.16 | convolution fusion | flops 4297064448 | bytes 10485760 | tf_op jit(solution)/shard_map/tr,tc->rc/dot_general | solution.py:762
  216.5 6.1 %convolution_convert_fusion.4 = bf16[1024,2048]{1,0:T(8,128)(2,1)} fusion(bf16[1024,1024]{1,0:T(8,128)(2,1)S(1)} %get-tuple-element.62, bf16[2048,1024]{0,1:T(8,128)(2,1)S(1)} %bitcast.82), kind=kOutput, calls=%fused_computation.18 | convolution fusion | flops 4297064448 | bytes 10485760 | tf_op jit(solution)/shard_map/tc,rc->tr/dot_general | solution.py:758
  222.6 6.3 %convolution_convert_fusion.1.refs_3_ = bf16[1024,2048]{1,0:T(8,128)(2,1)} fusion(bf16[1024,1024]{1,0:T(8,128)(2,1)S(1)} %get-tuple-element.59, bf16[1024,2048]{1,0:T(8,128)(2,1)S(1)} %bitcast.114), kind=kOutput, calls=%fused_computation.15 | convolution fusion | flops 4297064448 | bytes 10485760 | tf_op jit(solution)/shard_map/tr,tc->rc/dot_general | solution.py:762
  228.8 6.2 %convolution_convert_fusion.3 = bf16[1024,2048]{1,0:T(8,128)(2,1)} fusion(bf16[1024,1024]{1,0:T(8,128)(2,1)S(1)} %get-tuple-element.59, bf16[1024,2048]{1,0:T(8,128)(2,1)S(1)} %copy-done.11), kind=kOutput, calls=%fused_computation.17 | convolution fusion | flops 4297064448 | bytes 10485760 | tf_op jit(solution)/shard_map/dot_general | solution.py:754
  235.6 316.9 %final_kernel.1 = (bf16[128,2048]{1,0:T(8,128)(2,1)}, bf16[128,2048]{1,0:T(8,128)(2,1)}, f32[16,256]{1,0:T(8,128)}, bf16[3072,2048]{1,0:T(8,128)(2,1)}) custom-call(bf16[8,128,2048]{2,1,0:T(8,128)(2,1)} %bitcast.87, bf16[8,128,2048]{2,1,0:T(8,128)(2,1)} %bitcast.88, bf16[8,256,1024]{2,1,0:T(8,128)(2,1)} %bitcast.86, ...), custom_call_target="tpu_custom_call" | custom-call | tf_op jit(solution)/shard_map/final_kernel/pallas_call | solution.py:739
  553.2 1.5 fusion.19
  554.8 6.7 %slice_convert_fusion.1 = (f32[256,2048]{1,0:T(8,128)}, f32[256,2048]{1,0:T(8,128)}, f32[256,2048]{1,0:T(8,128)}, f32[256,2048]{1,0:T(8,128)}) fusion(bf16[3072,2048]{1,0:T(8,128)(2,1)} %get-tuple-element.42), kind=kLoop, calls=%fused_computation.30 | loop fusion | flops 2097152 | bytes 12582912 | tf_op jit(solution)/shard_map/convert_element_type | solution.py:942
  561.5 2.0 copy-done
  563.5 4.2 slice_convert_fusion
  568.3 1.1 convert_bitcast_fusion
  569.4 4.0 copy.60
  (67 shorter events, 13.9 us)
Async XLA Ops:
  7.2 182.0 %all-gather.2.cloned.1.call-start = ((), (), s32[]{:S(2)}) async-start(), calls=%async_computation | async-start | bytes 5242880 | tf_op jit(solution)/shard_map/all_gather | solution.py:828
  12.4 80.5 %copy-start.14 = (bf16[256]{0:T(256)(128)(2,1)S(1)}, bf16[256]{0:T(256)(128)(2,1)}, u32[]{:S(2)}) copy-start(bf16[256]{0:T(256)(128)(2,1)} %param.23) | copy-start | bytes 1540
  12.5 80.5 %copy-start.15 = (bf16[256]{0:T(256)(128)(2,1)S(1)}, bf16[256]{0:T(256)(128)(2,1)}, u32[]{:S(2)}) copy-start(bf16[256]{0:T(256)(128)(2,1)} %param.26) | copy-start | bytes 1540
  12.5 80.5 %copy-start.10 = (bf16[1024]{0:T(1024)(128)(2,1)S(1)}, bf16[1024]{0:T(1024)(128)(2,1)}, u32[]{:S(2)}) copy-start(bf16[1024]{0:T(1024)(128)(2,1)} %param.32) | copy-start | bytes 6148
  94.0 4.8 copy-start.7
  97.8 4.8 copy-start.4
  102.6 4.2 copy-start.5
  106.8 8.7 %copy-start.6 = (bf16[1024,256]{1,0:T(8,128)(2,1)}, bf16[1024,256]{1,0:T(8,128)(2,1)S(1)}, u32[]{:S(2)}) copy-start(bf16[1024,256]{1,0:T(8,128)(2,1)S(1)} %fusion.11.refs_8_) | copy-start | bytes 1572868
  108.6 9.1 %copy-start.3 = (bf16[256,2048]{1,0:T(8,128)(2,1)S(1)}, bf16[256,2048]{1,0:T(8,128)(2,1)}, u32[]{:S(2)}) copy-start(bf16[256,2048]{1,0:T(8,128)(2,1)} %refs_17_.1) | copy-start | bytes 3145732
  113.2 1.0 copy-start.1
  195.4 8.7 %copy-start.11 = (bf16[1024,2048]{1,0:T(8,128)(2,1)S(1)}, bf16[1024,2048]{1,0:T(8,128)(2,1)}, u32[]{:S(2)}) copy-start(bf16[1024,2048]{1,0:T(8,128)(2,1)} %param.33) | copy-start | bytes 12582916
  195.4 8.7 %copy-start.12 = (bf16[8,128,2048]{2,1,0:T(8,128)(2,1)S(1)}, bf16[8,128,2048]{2,1,0:T(8,128)(2,1)}, u32[]{:S(2)}) copy-start(bf16[8,128,2048]{2,1,0:T(8,128)(2,1)} %get-tuple-element.35) | copy-start | bytes 12582916
  204.1 6.1 %copy-start.13 = (bf16[8,128,2048]{2,1,0:T(8,128)(2,1)S(1)}, bf16[8,128,2048]{2,1,0:T(8,128)(2,1)}, u32[]{:S(2)}) copy-start(bf16[8,128,2048]{2,1,0:T(8,128)(2,1)} %get-tuple-element.36) | copy-start | bytes 12582916
  210.2 6.3 %copy-start.2 = (bf16[4,2048,256]{1,2,0:T(8,128)(2,1)S(1)}, bf16[4,2048,256]{1,2,0:T(8,128)(2,1)}, u32[]{:S(2)}) copy-start(bf16[4,2048,256]{1,2,0:T(8,128)(2,1)} %copy.56) | copy-start | bytes 12582916
  554.8 8.7 %copy-start = (bf16[3072,2048]{1,0:T(8,128)(2,1)S(1)}, bf16[3072,2048]{1,0:T(8,128)(2,1)}, u32[]{:S(2)}) copy-start(bf16[3072,2048]{1,0:T(8,128)(2,1)} %get-tuple-element.42) | copy-start | bytes 37748740
  569.4 4.0 copy-start.9
  569.4 4.8 copy-start.8
Sparse Core Ops, SparseCore 0:
  93.1 81.1 all-gather.1

commit v4 on v3

--- a/solution.py
+++ b/solution.py
@@ -13,6 +13,7 @@
 BF = jnp.bfloat16
 F32 = jnp.float32
 VM = pl.BlockSpec(memory_space=pltpu.VMEM)
+SCALAR = pl.BlockSpec(memory_space=pltpu.SMEM)
 ANY = pl.BlockSpec(memory_space=pl.ANY)
 LIMIT = 63 * 2**20
 
@@ -171,11 +172,12 @@
         order = self.orders[n]
         return h not in span(order[1:])
 
+    def begin_one(self, h):
+        self.cores[h] = self.net.to("shard", 1, self.part.at[h ^ 1], self.sums.at[h // 2])
+
     def begin(self):
         for h in self.sequence:
-            self.cores[h] = self.net.to(
-                "shard", 1, self.part.at[h ^ 1], self.sums.at[h // 2]
-            )
+            self.begin_one(h)
 
     def add(self, h, start, count, other):
         step = min(count, 32)
@@ -199,13 +201,16 @@
         )
         self.flight[n].append((copy, to, slot))
 
+    def prepare_one(self, h):
+        self.cores[h].wait_recv()
+        self.add(h, 0, self.rows, self.part.at[h])
+        for n in range(2):
+            if self.sends(n, h):
+                self.send(n, 0, h)
+
     def prepare(self):
         for h in self.sequence:
-            self.cores[h].wait_recv()
-            self.add(h, 0, self.rows, self.part.at[h])
-            for n in range(2):
-                if self.sends(n, h):
-                    self.send(n, 0, h)
+            self.prepare_one(h)
 
     def advance(self, n, k):
         flight, self.flight[n] = self.flight[n], []
@@ -264,29 +269,70 @@
         body(pl.ds(start, step), start)
 
 
-def gather_kernel(
-    sizes,
-    x_ref,
-    small_ref,
-    q_ref,
-    k_ref,
-    v_ref,
-    u_ref,
-    nrm,
-    small_all,
-    wq,
-    wk,
-    wv,
-    wu,
-    send,
-    recv,
-):
+class Spread:
+    def __init__(self, buf, columns, reps, sems):
+        self.buf, self.columns, self.reps, self.sems = buf, columns, reps, sems
+        self.rep = lax.axis_index("rep")
+
+    def copy(self, hop, way, member):
+        s, r = self.sems
+        n = self.columns
+        view = self.buf.at[:, :, pl.ds(pl.multiple_of(member * n, n), n)]
+        at = 2 * (hop - 1) + way
+        return pltpu.make_async_remote_copy(
+            src_ref=view,
+            dst_ref=view,
+            send_sem=s.at[at],
+            recv_sem=r.at[at],
+            device_id={"rep": self.rep + (1 - 2 * way)},
+            device_id_type=MESH,
+        )
+
+    def each(self, hop, sent, act):
+        rep, last = self.rep, self.reps - 1
+        for way in (0, 1):
+            sign = 1 - 2 * way
+            if sent:
+                member = rep - sign * (hop - 1)
+                to = rep + sign
+                here = (to >= 0) & (to <= last)
+            else:
+                member = rep - sign * hop
+                here = True
+
+            @pl.when((member >= 0) & (member <= last) & here)
+            def _():
+                act(self.copy(hop, way, member))
+
+    def start(self, hop):
+        self.each(hop, True, lambda c: c.start())
+
+    def arrive(self, hop):
+        self.each(hop, False, lambda c: c.wait_recv())
+
+    def finish(self):
+        for hop in range(1, self.reps):
+            self.each(hop, True, lambda c: c.wait_send())
+
+
+def forward_kernel(sizes, head, *refs):
     group, reps = sizes
+    length_ref, x_ref, cot_ref, vectors, q_ref, k_ref, v_ref, u_ref, wo = refs[:9]
+    nrm, small_all, wq, wk, wv, wu, queries, keys, values, p_ref, ctx, mid, second, mix = refs[9:23]
+    work = refs[23:]
+    part, small_ref = work[2:4]
+    spread_sems = work[4:6]
     me, rep = lax.axis_index("shard"), lax.axis_index("rep")
-    net = Net(send, recv)
+    net = Net(*work[-2:])
     masks = shard_masks(group)
-    meet(range(1, group), [])
-    width = small_ref.shape[1]
+    width, rows, model = vectors.shape[1], x_ref.shape[0], x_ref.shape[1]
+    heads = width // head
+    scale = 1.0 / math.sqrt(head)
+    live = length_ref[0].astype(F32)
+    small_ref[0:6] = vectors[0:6]
+    small_ref[LN : LN + 1] = jnp.full((1, width), 1.0, F32) * live
+    small_ref[LN + 1 :] = jnp.zeros((1, width), F32)
+    meet(range(1, group), range(1, reps))
     mine = pl.ds(pl.multiple_of(me * width, width), width)
     small = [
         net.to("shard", j, small_ref, small_all.at[:, mine]) for j in range(1, group)
@@ -294,82 +340,126 @@
     own_small = net.own(small_ref, small_all.at[:, mine])
 
     def scatter(src, dst, first, n):
-        part = src.shape[1] // group
+        share = src.shape[1] // group
 
         def columns(j):
-            return pl.ds(pl.multiple_of(flip(me, j) * part + first, n), n)
-
-        return [
-            net.to("shard", j, src.at[:, columns(j)], dst.at[me]) for j in range(1, group)
-        ] + [net.own(src.at[:, columns(0)], dst.at[me])]
-
-    moved = scatter(q_ref, wq, 0, width) + scatter(k_ref, wk, 0, width)
-    for copy in small:
-        copy.wait_recv()
-    own_small.wait()
+            return pl.ds(pl.multiple_of(flip(me, j) * share + first, n), n)
+
+        return [net.to("shard", j, src.at[:, columns(j)], dst) for j in range(1, group)] + [
+            net.own(src.at[:, columns(0)], dst)
+        ]
+
+    def arrive(copies):
+        for copy in copies[:-1]:
+            copy.wait_recv()
+        copies[-1].wait()
+
+    whole = wu.shape[2]
+    share = whole // reps if whole // reps % 128 == 0 else whole
+    first = rep * share if share < whole else 0
+    lanes = pl.ds(pl.multiple_of(first, share), share)
+    ups = scatter(u_ref, wu.at[me, :, lanes], first, share)
+    spread = Spread(wu, share, reps if share < whole else 1, spread_sems)
+    moved = [scatter(s, d.at[me], 0, width) for s, d in ((q_ref, wq), (k_ref, wk), (v_ref, wv))]
+    arrive(small + [own_small])
     gather = Gather(net, nrm, masks)
     for n in range(2):
 
         def one(at, start):
             v, _ = norm_rows(x_ref[at].astype(F32))
             nrm[0, at] = (v * small_all[FG : FG + 1] + small_all[FS : FS + 1]).astype(BF)
-
-        by_rows(n, x_ref.shape[0], one)
+            mix[0, at] = (cot_ref[at].astype(F32) * live_rows(live, start, 16)).astype(BF)
+
+        by_rows(n, rows, one)
         gather.start(n)
-    moved += scatter(v_ref, wv, 0, width)
-    quarter = wu.shape[2]
-    moved += scatter(u_ref, wu, rep * quarter, quarter)
-    gather.finish()
-    for i, copy in enumerate(moved):
-        if i % group == group - 1:
-            copy.wait()
+    arrive(ups)
+    if spread.reps > 1:
+        spread.start(1)
+    for _ in range(gather.steps - 1):
+        gather.both()
+    gather.both()
+    gather.end()
+    for copies, weight, low, row in zip(
+        moved, (wq, wk, wv), (queries, keys, values), (6, None, 7)
+    ):
+        arrive(copies)
+        for b in range(0, group, 2):
+            left = nrm[b : b + 2].reshape(2 * rows, model)
+            res = dot(left, weight[...].reshape(model, width))
+            if row is not None:
+                res = res + vectors[row : row + 1]
+            low[pl.ds(b * rows, 2 * rows)] = res.astype(BF)
+    gmix = Gather(net, mix, masks)
+    red = Reduce(net, part, work[:2], masks)
+    order = [h ^ 1 for h in red.sequence] + red.sequence
+    row_at = lax.broadcasted_iota(jnp.int32, (rows, rows), 0)
+    col_at = lax.broadcasted_iota(jnp.int32, (rows, rows), 1)
+
+    def side(n):
+        if n == 0:
+            for i in range(2):
+                gmix.start(i)
+        if n == 0 and spread.reps > 1:
+            spread.arrive(1)
+            if spread.reps > 2:
+                spread.start(2)
+        if n in (3, 6) and gmix.parts[0]["step"] <= gmix.steps:
+            gmix.both()
+
+    for n, b in enumerate(order):
+        side(n)
+        at = pl.ds(b * rows, rows)
+        count = small_all[LN : LN + 1, pl.ds(pl.multiple_of(flip(me, b) * width, width), 128)]
+        valid = (col_at <= row_at) & (col_at.astype(F32) < count[:, :1])
+        for h in range(heads):
+            lane = pl.ds(h * head, head)
+            scores = dot_nt(queries[at, lane], keys[at, lane]) * scale
+            scores = jnp.where(valid, scores, -1e30)
+            expo = jnp.exp(scores - jnp.max(scores, axis=-1, keepdims=True))
+            p = expo / jnp.sum(expo, axis=-1, keepdims=True)
+            p_ref[b, h] = p
+            ctx[at, lane] = dot(p.astype(BF), values[at, lane]).astype(BF)
+        for c in range(0, model, 1024):
+            lane = pl.ds(c, 1024)
+            part[b, :, lane] = dot(ctx[at], wo[:, lane]).astype(BF)
+        if b % 2:
+            red.begin_one(b ^ 1)
         else:
-            copy.wait_recv()
-    net.finish()
-
-
-def middle_kernel(sizes, part, x_ref, cot_ref, small, mid, second, mix, *work):
-    group, _ = sizes
-    net = Net(*work[-2:])
-    masks = shard_masks(group)
-    meet([1] + masks, [])
-    me = lax.axis_index("shard")
-    width = small.shape[1] // group
-    length = small[LN : LN + 1, pl.ds(pl.multiple_of(me * width, width), 128)][:, :1]
-    rows = x_ref.shape[0]
-    red = Reduce(net, part, work[:2], masks)
-    red.begin()
-    gmix = Gather(net, mix, masks)
-    for n in range(2):
-
-        def live(at, start):
-            mix[0, at] = (cot_ref[at].astype(F32) * live_rows(length, start, 16)).astype(BF)
-
-        by_rows(n, rows, live)
-        gmix.start(n)
-    red.prepare()
+            red.prepare_one(b)
     for k in range(red.steps - 1):
         for n in range(2):
             red.advance(n, k)
     gather = Gather(net, second, masks)
-    gmix.both()
     for n in range(2):
         red.advance(n, red.steps - 1)
 
         def norm(at, start):
-            m = x_ref[at].astype(F32) + (red.total(at) + small[OB : OB + 1])
+            m = x_ref[at].astype(F32) + (red.total(at) + small_all[OB : OB + 1])
             mid[at] = m
             v, _ = norm_rows(m)
-            second[0, at] = (v * small[SG : SG + 1] + small[SS : SS + 1]).astype(BF)
+            second[0, at] = (v * small_all[SG : SG + 1] + small_all[SS : SS + 1]).astype(BF)
 
         by_rows(n, rows, norm)
         gather.start(n)
-    for _ in range(gather.steps - 1):
+    hop = 2
+    while gmix.parts[0]["step"] <= gmix.steps:
         gmix.both()
+    for _ in range(gather.steps):
+        if hop < spread.reps:
+            spread.arrive(hop)
+            hop += 1
+            if hop < spread.reps:
+                spread.start(hop)
         gather.both()
-    gather.both()
+    while hop < spread.reps:
+        spread.arrive(hop)
+        hop += 1
+        if hop < spread.reps:
+            spread.start(hop)
     gmix.end()
     gather.end()
+    if spread.reps > 1:
+        spread.finish()
     net.finish()
 
 
@@ -735,11 +825,13 @@
     net.finish()
 
 
-def call(body, number, sizes, outs, scratch, copies, args, far=(), far_outs=()):
+def call(body, number, sizes, outs, scratch, copies, args, far=(), far_outs=(), scalars=()):
     return pl.pallas_call(
         functools.partial(body, *sizes),
         out_shape=[jax.ShapeDtypeStruct(s, d) for s, d in outs],
-        in_specs=[ANY if i in far else VM for i in range(len(args))],
+        in_specs=[
+            ANY if i in far else SCALAR if i in scalars else VM for i in range(len(args))
+        ],
         out_specs=[ANY if i in far_outs else VM for i in range(len(outs))],
         scratch_shapes=list(scratch)
         + [pltpu.SemaphoreType.DMA((copies,)), pltpu.SemaphoreType.DMA((copies,))],
@@ -790,75 +882,65 @@
     head = width // HEADS
     scale = 1.0 / math.sqrt(head)
     me = lax.axis_index("shard")
-    small = jnp.stack(
+    vectors = jnp.concatenate(
         [
-            first_gain.astype(F32),
-            first_shift.astype(F32),
-            out_bias.astype(F32),
-            second_gain.astype(F32),
-            second_shift.astype(F32),
-            down_bias.astype(F32),
-            jnp.full((g,), 1.0, F32) * lengths[0].astype(F32),
-            jnp.zeros((g,), F32),
+            first_gain,
+            first_shift,
+            out_bias,
+            second_gain,
+            second_shift,
+            down_bias,
+            query_bias,
+            value_bias,
         ]
     )
+    vectors = vectors.reshape(8, g).astype(F32)
     x, cot = block_input[0], cotangent[0]
     blocks = (group, rows, width)
-    parts = reps if f // reps % 128 == 0 else 1
-    nrm, small_all, wq, wk, wv, wu = call(
-        gather_kernel,
+    masks = shard_masks(group)
+    work = reduce_shapes(group, rows, width, masks)
+    tokens, column = group * rows, ((group, g, g), BF)
+    nrm, small_all, wq, wk, wv, wu, queries, keys, values, p, ctx, mid, second, mix = call(
+        forward_kernel,
         1,
-        (sizes,),
+        (sizes, head),
         [
             (blocks, BF),
             ((8, width), F32),
-            ((group, g, g), BF),
-            ((group, g, g), BF),
-            ((group, g, g), BF),
-            ((group, g, f // parts), BF),
+            column,
+            column,
+            column,
+            ((group, g, f), BF),
+            ((tokens, g), BF),
+            ((tokens, g), BF),
+            ((tokens, g), BF),
+            ((group, g // head, rows, rows), F32),
+            ((tokens, g), BF),
+            ((rows, width), F32),
+            (blocks, BF),
+            (blocks, BF),
         ],
-        [],
-        200,
-        (x, small, query_weight, key_weight, value_weight, up_weight),
+        work
+        + [pltpu.VMEM(blocks, BF), pltpu.VMEM((8, g), F32)]
+        + [pltpu.SemaphoreType.DMA((2 * reps,))] * 2,
+        320,
+        (
+            lengths,
+            x,
+            cot,
+            vectors,
+            query_weight,
+            key_weight,
+            value_weight,
+            up_weight,
+            out_weight,
+        ),
+        (4, 5, 6, 7),
+        (),
+        (0,),
     )
     flat = lambda a: a.reshape(-1, a.shape[-1])
-    normed = flat(nrm)
-    wq, wk, wv, wu = flat(wq), flat(wk), flat(wv), flat(wu)
-    if parts > 1:
-        wu = lax.all_gather(wu, "rep", axis=0).transpose(1, 0, 2).reshape(width, f)
-    queries = (dot(normed, wq) + query_bias.astype(F32)).astype(BF)
-    keys = dot(normed, wk).astype(BF)
-    values = (dot(normed, wv) + value_bias.astype(F32)).astype(BF)
-    shape = (group, rows, g // head, head)
-    qh, kh, vh = (a.reshape(shape) for a in (queries, keys, values))
-    lens = small_all[LN].reshape(group, g)[:, 0]
-    order = jnp.bitwise_xor(jnp.arange(group, dtype=jnp.int32), me)
-    lens = jnp.take(lens, order).astype(jnp.int32)
-    pos = jnp.arange(rows, dtype=jnp.int32)
-    valid = (pos[None, None, :] <= pos[None, :, None]) & (pos[None, None, :] < lens[:, None, None])
-    scores = jnp.einsum("bqhd,bkhd->bhqk", qh, kh, preferred_element_type=F32) * scale
-    scores = jnp.where(valid[:, None], scores, -1e30)
-    top = jnp.max(scores, axis=-1, keepdims=True)
-    expo = jnp.exp(scores - top)
-    p = expo / jnp.sum(expo, axis=-1, keepdims=True)
-    p_low = p.astype(BF)
-    ctx = (
-        jnp.einsum("bhqk,bkhd->bqhd", p_low, vh, preferred_element_type=F32)
-        .astype(BF)
-        .reshape(group * rows, g)
-    )
-    part = dot(ctx, out_weight).astype(BF).reshape(blocks)
-    masks = shard_masks(group)
-    work = reduce_shapes(group, rows, width, masks)
-    mid, second, mix = call(
-        middle_kernel,
-        2,
-        (sizes,),
-        [((rows, width), F32), (blocks, BF), (blocks, BF)],
-        work,
-        160,
-        (part, x, cot, small_all),
-    )
+    wu = flat(wu)
     second = flat(second)
     mixed = flat(mix)
     upper = dot(second, wu) + up_bias.astype(F32)
@@ -901,7 +983,7 @@
     )
     out, gin, smalls, whole = call(
         final_kernel,
-        3,
+        2,
         (sizes, head),
         [
             ((rows, width), BF),
@@ -926,9 +1008,9 @@
             p,
             ctx,
             nrm,
-            wq.reshape(group, g, g),
-            wk.reshape(group, g, g),
-            wv.reshape(group, g, g),
+            wq,
+            wk,
+            wv,
             out_weight,
             cols,
         ),

time: 590 us -> 558 us (0.946)
  matrix products: 58.8 us -> 43.8 us
  between operations: 15.5 us -> 1.59 us
  Pallas kernels: 466 us -> 474 us
  local copies, waits for them, and re-layouts: 24.7 us -> 18.3 us
    dot_general x6 -> x2, matrix products: 29.7 us -> 14.8 us  [dot(): return jnp.dot(a, b, preferred_element_type=F32)]
    pallas_call x3 -> x2, Pallas kernels: 466 us -> 474 us  [call(): pl.pallas_call(functools.partial(body, *sizes), out_shape=[jax.ShapeDtype...]
    all_gather x1 -> x0, local copies, waits for them, and re-layouts: 6.2 us -> none  [local(): wu = lax.all_gather(wu, 'rep', axis=0).transpose(1, 0, 2).reshape(width, f)]
  transfers between devices with their start and end apart: 1 -> 0, of which waited for: 0 -> 0; matrix products, arithmetic and copies ran while one was open for 5% -> 0% of each run, Pallas kernels for 12% -> 0%
where the time goes in v4:
time: 558 us; the launch traced here: 551 us
  Pallas kernels  474 us (85%)
  matrix products  43.8 us (8%)
  local copies, waits for them, and re-layouts  18.3 us (3%)
  other arithmetic  12.6 us (2%)
    pallas_call x2, Pallas kernels, call(): pl.pallas_call(functools.partial(body, *sizes), out_shape=[jax.ShapeDtype...  474 us
    dot_general x2, matrix products, dot_tn(): return jnp.einsum('tr,tc->rc', a, b, preferred_element_type=F32)  15.9 us
    dot_general x2, matrix products, dot(): return jnp.dot(a, b, preferred_element_type=F32)  14.8 us
    dot_general x2, matrix products, dot_nt(): return jnp.einsum('tc,rc->tr', a, b, preferred_element_type=F32)  13.1 us

profile of v4, /device:TPU:0, one launch (start us, length us, event | category | flops | bytes accessed | tf_op | source)
XLA Modules:
  0.0 550.8 jit_solution(11975156869966779892)
XLA Ops:
  2.0 0.8 dynamic-update-slice
  2.8 0.8 dynamic-update-slice.1
  3.7 0.8 dynamic-update-slice.2
  4.5 0.8 dynamic-update-slice.3
  5.3 0.8 dynamic-update-slice.4
  6.2 0.8 dynamic-update-slice.5
  7.0 0.8 dynamic-update-slice.6
  7.8 0.8 dynamic-update-slice.7
  9.2 156.9 %forward_kernel.1 = (bf16[8,128,2048]{2,1,0:T(8,128)(2,1)}, f32[8,2048]{1,0:T(8,128)}, bf16[8,256,256]{2,1,0:T(8,128)(2,1)}, bf16[8,256,256]{2,1,0:T(8,128)(2,1)...) custom-call(s32[1]{0:T(128)S(6)} %copy.48.refs_0_, ...), custom_call_target="tpu_custom_call" | custom-call | tf_op jit(solution)/shard_map/forward_kernel/pallas_call | solution.py:829
  166.1 8.7 %multiply_convert_fusion = (bf16[1024,1024]{1,0:T(8,128)(2,1)S(1)}, f32[1024,1024]{1,0:T(8,128)S(1)}) fusion(f32[1024]{0:T(1024)S(1)} %convert_element_type.58, bf16[1024,2048]{1,0:T(8,128)(2,1)} %bitcast.63, bf16[2048,1024]{1,0:T(8,128)(2,1)} %bitcast.61), kind=kOutput, calls=%fused_computation.10 | convolution fusion | flops 4301258752 | bytes 14684160 | tf_op jit(solution)/shard_map/dot_general | solution.py:846
  174.9 7.0 %convert_reduce_fusion = (f32[1024]{0:T(1024)S(1)}, bf16[1024,1024]{1,0:T(8,128)(2,1)}) fusion(f32[1024,1024]{1,0:T(8,128)S(1)} %get-tuple-element.68, f32[1024]{0:T(1024)S(1)} %convert_element_type.58, bf16[1024,2048]{1,0:T(8,128)(2,1)S(1)} %bitcast.59, bf16[1024,2048]{1,0:T(8,128)(2,1)S(1)} %copy-done.3), kind=kOutput, calls=%fused_computation.9 | convolution fusion | flops 4308597760 | bytes 14688256 | tf_op jit(solution)/shard_map/tc,rc->tr/dot_general | solution.py:850
  182.0 9.5 %convolution_convert_fusion.1 = bf16[2048,1024]{1,0:T(8,128)(2,1)} fusion(bf16[1024,2048]{1,0:T(8,128)(2,1)} %bitcast.64, bf16[1024,1024]{1,0:T(8,128)(2,1)} %get-tuple-element.70), kind=kOutput, calls=%fused_computation.13 | convolution fusion | flops 4297064448 | bytes 10485760 | tf_op jit(solution)/shard_map/tr,tc->rc/dot_general | solution.py:854
  191.5 6.1 %convolution_convert_fusion.3 = bf16[1024,2048]{1,0:T(8,128)(2,1)} fusion(bf16[1024,1024]{1,0:T(8,128)(2,1)S(1)} %copy-done.8, bf16[2048,1024]{1,0:T(8,128)(2,1)S(1)} %bitcast.62), kind=kOutput, calls=%fused_computation.15 | convolution fusion | flops 4297064448 | bytes 10485760 | tf_op jit(solution)/shard_map/tc,rc->tr/dot_general | solution.py:850
  197.6 6.4 %convolution_convert_fusion.refs_3_ = bf16[1024,2048]{1,0:T(8,128)(2,1)} fusion(bf16[1024,1024]{1,0:T(8,128)(2,1)S(1)} %get-tuple-element.67, bf16[1024,2048]{1,0:T(8,128)(2,1)S(1)} %bitcast.60), kind=kOutput, calls=%fused_computation.12 | convolution fusion | flops 4297064448 | bytes 10485760 | tf_op jit(solution)/shard_map/tr,tc->rc/dot_general | solution.py:854
  204.6 6.1 %convolution_convert_fusion.2 = bf16[1024,2048]{1,0:T(8,128)(2,1)} fusion(bf16[1024,1024]{1,0:T(8,128)(2,1)S(1)} %get-tuple-element.67, bf16[1024,2048]{1,0:T(8,128)(2,1)S(1)} %copy-done.4), kind=kOutput, calls=%fused_computation.14 | convolution fusion | flops 4297064448 | bytes 10485760 | tf_op jit(solution)/shard_map/dot_general | solution.py:846
  210.7 317.6 %final_kernel.1 = (bf16[128,2048]{1,0:T(8,128)(2,1)}, bf16[128,2048]{1,0:T(8,128)(2,1)}, f32[16,256]{1,0:T(8,128)}, bf16[3072,2048]{1,0:T(8,128)(2,1)}) custom-call(bf16[8,128,2048]{2,1,0:T(8,128)(2,1)} %bitcast.42, bf16[8,128,2048]{2,1,0:T(8,128)(2,1)} %bitcast.43, bf16[8,256,1024]{2,1,0:T(8,128)(2,1)} %bitcast.41, ...), custom_call_target="tpu_custom_call" | custom-call | tf_op jit(solution)/shard_map/final_kernel/pallas_call | solution.py:829
  528.9 1.5 fusion.6
  531.0 6.7 %slice_convert_fusion.1 = (f32[256,2048]{1,0:T(8,128)}, f32[256,2048]{1,0:T(8,128)}, f32[256,2048]{1,0:T(8,128)}, f32[256,2048]{1,0:T(8,128)}) fusion(bf16[3072,2048]{1,0:T(8,128)(2,1)} %get-tuple-element.52), kind=kLoop, calls=%fused_computation.16 | loop fusion | flops 2097152 | bytes 12582912 | tf_op jit(solution)/shard_map/convert_element_type | solution.py:1024
  537.7 2.0 copy-done
  539.8 4.2 slice_convert_fusion
  544.0 1.1 convert_bitcast_fusion
  545.1 4.0 copy.36
  549.1 0.8 copy.49
  549.8 0.8 copy.50
  (24 shorter events, 3.2 us)
Async XLA Ops:
  166.1 8.8 %copy-start.3 = (bf16[1024,2048]{1,0:T(8,128)(2,1)S(1)}, bf16[1024,2048]{1,0:T(8,128)(2,1)}, u32[]{:S(2)}) copy-start(bf16[1024,2048]{1,0:T(8,128)(2,1)} %param.33) | copy-start | bytes 12582916
  166.1 8.8 %copy-start.5 = (bf16[8,128,2048]{2,1,0:T(8,128)(2,1)S(1)}, bf16[8,128,2048]{2,1,0:T(8,128)(2,1)}, u32[]{:S(2)}) copy-start(bf16[8,128,2048]{2,1,0:T(8,128)(2,1)} %get-tuple-element.35) | copy-start | bytes 12582916
  182.0 9.5 %copy-start.7 = (bf16[8,256,1024]{2,1,0:T(8,128)(2,1)S(1)}, bf16[8,256,1024]{2,1,0:T(8,128)(2,1)}, u32[]{:S(2)}) copy-start(bf16[8,256,1024]{2,1,0:T(8,128)(2,1)} %get-tuple-element.37) | copy-start | bytes 12582916
  182.0 9.5 %copy-start.8 = (bf16[1024,1024]{1,0:T(8,128)(2,1)S(1)}, bf16[1024,1024]{1,0:T(8,128)(2,1)}, u32[]{:S(2)}) copy-start(bf16[1024,1024]{1,0:T(8,128)(2,1)} %get-tuple-element.70) | copy-start | bytes 6291460
  191.5 6.1 %copy-start.6 = (bf16[8,128,2048]{2,1,0:T(8,128)(2,1)S(1)}, bf16[8,128,2048]{2,1,0:T(8,128)(2,1)}, u32[]{:S(2)}) copy-start(bf16[8,128,2048]{2,1,0:T(8,128)(2,1)} %get-tuple-element.35) | copy-start | bytes 12582916
  197.6 7.0 %copy-start.4 = (bf16[1024,2048]{1,0:T(8,128)(2,1)S(1)}, bf16[1024,2048]{1,0:T(8,128)(2,1)}, u32[]{:S(2)}) copy-start(bf16[1024,2048]{1,0:T(8,128)(2,1)} %param.33) | copy-start | bytes 12582916
  531.0 8.7 %copy-start = (bf16[3072,2048]{1,0:T(8,128)(2,1)S(1)}, bf16[3072,2048]{1,0:T(8,128)(2,1)}, u32[]{:S(2)}) copy-start(bf16[3072,2048]{1,0:T(8,128)(2,1)} %get-tuple-element.52) | copy-start | bytes 37748740
  545.0 4.0 copy-start.2
  545.0 4.8 copy-start.1

commit v5 on v4

--- a/solution.py
+++ b/solution.py
@@ -163,7 +163,6 @@
         self.steps = len(masks)
         self.orders = orders(masks)
         self.flight = [[], []]
-        first = [o[0] for o in self.orders]
         self.sequence = sorted(
             span(masks), key=lambda h: -sum(self.sends(n, h) for n in range(2))
         )
@@ -578,9 +577,11 @@
 def final_kernel(sizes, head, *refs):
     group, reps = sizes
     (
-        gpart,
-        dpart,
-        up_part,
+        gup,
+        active,
+        second,
+        wu,
+        wd,
         down_grad,
         mid,
         cot,
@@ -597,12 +598,12 @@
         wv,
         wo,
         cols,
-    ) = refs[:19]
-    out, gin, smalls, whole = refs[19:23]
-    work = refs[23:]
+    ) = refs[:21]
+    out, gin, smalls, whole = refs[21:25]
+    work = refs[25:]
     gmid, sums, land, both, zland, own_all, line_land = work[4:11]
-    part, branch, g3, dw, nbuf, wbuf, loads = work[11:18]
-    line_sems, kept = work[18:20], work[20]
+    part, branch, g3, dw, nbuf, wbuf, ubuf, dbuf, loads = work[11:20]
+    line_sems, kept = work[20:22], work[22]
     net = Net(*work[-2:])
     masks = shard_masks(group)
     me, rep = lax.axis_index("shard"), lax.axis_index("rep")
@@ -610,43 +611,79 @@
     heads = width // head
     scale = 1.0 / math.sqrt(head)
     tall = width
-    down_rows, wide = down_grad.shape[0], up_part.shape[2]
+    down_rows, wide = down_grad.shape[0], gup.shape[1]
     up_base = down_rows
     out_base = up_base + tall * (wide * group // model)
-    loaded = [
-        net.own(gpart, part),
-        net.own(down_grad, own_all.at[pl.ds(0, down_rows)]),
-    ]
+    loaded = [net.own(down_grad, own_all.at[pl.ds(0, down_rows)])]
     meet(range(1, group), range(1, reps))
     length = small[LN : LN + 1, pl.ds(pl.multiple_of(me * width, width), 128)][:, :1]
     line = Line(own_all, line_land, whole, tall, reps, line_sems, kept)
     for copy in loaded:
         copy.wait()
-    arrivals = {}
+    arrivals, kept_here = {}, {}
 
     def place(j):
         return pl.ds(pl.multiple_of(flip(me, j) * width, width), width)
 
+    class stream:
+        def __init__(self, source, buf, row):
+            self.source, self.buf, self.row = source, buf, row
+
+        def copy(self, a):
+            return pltpu.make_async_copy(
+                self.source(a), self.buf.at[a % 2], loads.at[self.row, a % 2]
+            )
+
+        def begin(self):
+            self.copy(0).start()
+
+        def take(self, a):
+            if a + 1 < group:
+                self.copy(a + 1).start()
+            self.copy(a).wait()
+            return self.buf[a % 2]
+
     def tasks():
-        red = Reduce(net, part, work[:2], masks)
-        red.begin()
-        yield 3
-        red.prepare()
         each = model // wide
         target = own_all.at[
             pl.ds(pl.multiple_of(up_base + (me // each) * tall, tall), tall),
             pl.ds(pl.multiple_of((me % each) * wide, wide), wide),
         ]
-        arrivals[up_base] = [
-            net.to("shard", j, up_part.at[flip(me, j)], target) for j in range(1, group)
-        ] + [net.own(up_part.at[me], target)]
-        yield 22
+        second_of = stream(lambda j: second.at[:, :, place(j)], nbuf, 0)
+        second_of.begin()
+        ups = []
+        for j in range(group):
+            left = second_of.take(j).reshape(group * rows, width)
+            at = pl.ds(out_base + j // each * tall, tall), pl.ds(j % each * wide, wide)
+            own_all[at[0], at[1]] = dot_tn(left, gup[...]).astype(BF)
+            src = own_all.at[at[0], at[1]]
+            if j:
+                ups.append(net.to("shard", j, src, target))
+            else:
+                kept_here[up_base] = [net.own(src, target)]
+            yield 0
+        arrivals[up_base] = ups
+        up_of = stream(lambda a: wu.at[a], ubuf, 4)
+        up_of.begin()
+        for a in range(group):
+            block = up_of.take(a)
+            part[:, :, pl.ds(a * width, width)] = (
+                dot_nt(gup[...], block).astype(BF).reshape(group, rows, width)
+            )
+            yield 0
+        red = Reduce(net, part, work[:2], masks)
+        red.begin()
+        yield 18
+        red.prepare()
+        yield 23
         for s in range(red.steps - 1):
             for n in range(2):
                 red.advance(n, s)
-        yield 28
+        yield 26
         for n in range(2):
             red.advance(n, red.steps - 1)
+        for copy in kept_here.pop(up_base, []):
+            copy.wait()
         net.settle()
         sums[...] = jnp.zeros_like(sums)
         gather = Gather(net, branch, masks)
@@ -668,9 +705,9 @@
             by_rows(n, rows, back)
             gather.start(n)
         for s in range(gather.steps):
-            yield 33 + 5 * s
+            yield 30 + 4 * s
             gather.both()
-        yield 33 + 5 * gather.steps
+        yield 30 + 4 * gather.steps
         gather.end()
         early = len(net.open)
         for b in range(group):
@@ -705,8 +742,7 @@
             return pltpu.make_async_copy(nrm.at[:, :, place(j)], nbuf.at[j % 2], loads.at[0, j % 2])
 
         normed_of(0).start()
-        for i in range(3):
-            arrivals[out_base + (i + 1) * tall] = []
+        grown = {out_base + (i + 1) * tall: [] for i in range(3)}
         for j in range(group):
             if j + 1 < group:
                 normed_of(j + 1).start()
@@ -718,9 +754,12 @@
                 src = dw.at[j, :, pl.ds(i * width, width)]
                 base = out_base + (i + 1) * tall
                 dst = own_all.at[pl.ds(base, tall), place(0)]
-                copy = net.to("shard", j, src, dst) if j else net.own(src, dst)
-                arrivals[base].insert(len(arrivals[base]) if j == 0 else 0, copy)
+                if j:
+                    grown[base].append(net.to("shard", j, src, dst))
+                else:
+                    kept_here[base] = [net.own(src, dst)]
             yield 0
+        arrivals.update(grown)
 
         def weight_of(a):
             return [
@@ -728,6 +767,7 @@
                 for i, w in enumerate((wq, wk, wv))
             ]
 
+        net.settle(early)
         for copy in weight_of(0):
             copy.start()
         for a in range(group):
@@ -744,19 +784,25 @@
             yield 0
         red = Reduce(net, part, work[:2], masks)
         red.begin()
-        net.settle(early)
-        own = net.own(dpart, branch)
-        yield 62
-        own.wait()
+        yield 0
+        down_of = stream(lambda a: wd.at[:, pl.ds(a * width, width)], dbuf, 4)
+        down_of.begin()
+        for a in range(group):
+            block = down_of.take(a)
+            branch[:, :, pl.ds(a * width, width)] = (
+                dot(active[...], block).astype(BF).reshape(group, rows, width)
+            )
+            if a % 2:
+                yield 0
         late = Reduce(net, branch, work[2:4], masks)
         late.begin()
-        yield 66
+        yield 69
         red.prepare()
         for s in range(red.steps - 1):
-            yield 74 + 4 * s
+            yield 75 + 4 * s
             for n in range(2):
                 red.advance(n, s)
-        yield 79
+        yield 80
         for n in range(2):
             red.advance(n, red.steps - 1)
 
@@ -770,9 +816,9 @@
             by_rows(n, rows, first)
         tiny = [net.to("shard", j, sums.at[:, place(j)], land.at[me]) for j in range(1, group)]
         own = net.own(sums.at[:, place(0)], land.at[me])
-        yield 81
+        yield 83
         late.prepare()
-        yield 83
+        yield 85
         for copy in tiny:
             copy.wait_recv()
         own.wait()
@@ -783,10 +829,10 @@
         tiny = [net.to("rep", h, both, zland.at[rep]) for h in range(1, reps)]
         own = net.own(both, zland.at[rep])
         for s in range(late.steps - 1):
-            yield 89 + 4 * s
+            yield 90 + 4 * s
             for n in range(2):
                 late.advance(n, s)
-        yield 93
+        yield 94
         for n in range(2):
             late.advance(n, late.steps - 1)
 
@@ -795,7 +841,7 @@
                 out[at] = (m * live_rows(length, start, 16)).astype(BF)
 
             by_rows(n, rows, close)
-        yield 96
+        yield 97
         for copy in tiny:
             copy.wait_recv()
         own.wait()
@@ -811,11 +857,10 @@
         if t < line.count and t % line.each == 0 and (base == up_base or base >= out_base):
             while base not in arrivals:
                 resume = next(todo, None)
-            for copy in arrivals.get(base, []):
-                if copy is arrivals[base][-1]:
-                    copy.wait()
-                else:
-                    copy.wait_recv()
+            for copy in arrivals[base]:
+                copy.wait_recv()
+            for copy in kept_here.pop(base, []):
+                copy.wait()
         line.step(t)
         if resume is not None and t >= resume:
             resume = next(todo, None)
@@ -948,10 +993,7 @@
     pdf = jnp.exp(-0.5 * upper * upper) * (1.0 / math.sqrt(2.0 * math.pi))
     active = (upper * cdf).astype(BF)
     gup = (dot_nt(mixed, down_weight) * (cdf + upper * pdf)).astype(BF)
-    gpart = dot_nt(gup, wu).astype(BF).reshape(blocks)
-    dpart = dot(active, down_weight).astype(BF).reshape(blocks)
     down_grad = dot_tn(active, mixed).astype(BF)
-    up_part = dot_tn(second, gup).astype(BF).reshape(group, g, f)
     cols = jnp.concatenate(
         [jnp.sum(gup.astype(F32), axis=0).reshape(4, g), jnp.zeros((2, g), F32)]
     )
@@ -976,7 +1018,9 @@
             pltpu.VMEM((group, g, 3 * g), BF),
             pltpu.VMEM((2, group, rows, g), BF),
             pltpu.VMEM((2, 3, g, g), BF),
-            pltpu.SemaphoreType.DMA((4, 2)),
+            pltpu.VMEM((2, g, f), BF),
+            pltpu.VMEM((2, f, g), BF),
+            pltpu.SemaphoreType.DMA((5, 2)),
         ]
         + [pltpu.SemaphoreType.DMA((4 * count,))] * 2
         + [pltpu.SemaphoreType.DMA((2 * count,))]
@@ -994,9 +1038,11 @@
         scratch,
         320,
         (
-            gpart,
-            dpart,
-            up_part,
+            gup,
+            active,
+            second.reshape(blocks),
+            wu.reshape(group, g, f),
+            down_weight,
             down_grad,
             mid,
             cot,
@@ -1014,12 +1060,12 @@
             out_weight,
             cols,
         ),
-        (0, 1, 2, 3, 13, 14, 15, 16),
+        (2, 3, 4, 5, 15, 16, 17, 18),
         (3,),
     )
     dd = whole[:f].astype(F32)
-    du = whole[f : f + blocks_up * g].reshape(blocks_up, g, width).transpose(1, 0, 2)
-    du = du.reshape(g, hidden).astype(F32)
+    ups = [whole[f + i * g : f + (i + 1) * g] for i in range(blocks_up)]
+    du = jnp.concatenate(ups, axis=1).astype(F32)
     skip = f + blocks_up * g
     do, dq, dk, dv = (whole[skip + i * g : skip + (i + 1) * g].astype(F32) for i in range(4))
     return (

time: 558 us -> 537 us (0.962)
  matrix products: 43.8 us -> 21.6 us
    dot_general x2 -> x1, matrix products: 15.9 us -> 6.22 us  [dot_tn(): return jnp.einsum('tr,tc->rc', a, b, preferred_element_type=F32)]
    dot_general x2 -> x1, matrix products: 14.8 us -> 8.29 us  [dot(): return jnp.dot(a, b, preferred_element_type=F32)]
    dot_general x2 -> x1, matrix products: 13.1 us -> 7.05 us  [dot_nt(): return jnp.einsum('tc,rc->tr', a, b, preferred_element_type=F32)]
where the time goes in v5:
time: 537 us; the launch traced here: 529 us
  Pallas kernels  477 us (89%)
  matrix products  21.6 us (4%)
  other arithmetic  15.8 us (3%)
  local copies, waits for them, and re-layouts  13.5 us (3%)
    pallas_call x2, Pallas kernels, call(): pl.pallas_call(functools.partial(body, *sizes), out_shape=[jax.ShapeDtype...  477 us

profile of v5, /device:TPU:0, one launch (start us, length us, event | category | flops | bytes accessed | tf_op | source)
XLA Modules:
  0.0 529.4 jit_solution(12049063634264060273)
XLA Ops:
  1.3 0.7 convert_element_type.40
  2.0 0.8 dynamic-update-slice
  2.8 0.8 dynamic-update-slice.1
  3.7 0.8 dynamic-update-slice.2
  4.5 0.8 dynamic-update-slice.3
  5.3 0.8 dynamic-update-slice.4
  6.2 0.8 dynamic-update-slice.5
  7.0 0.8 dynamic-update-slice.6
  7.8 0.8 dynamic-update-slice.7
  8.6 0.6 reshape.58.refs_3_
  9.2 156.9 %forward_kernel.1 = (bf16[8,128,2048]{2,1,0:T(8,128)(2,1)}, f32[8,2048]{1,0:T(8,128)}, bf16[8,256,256]{2,1,0:T(8,128)(2,1)}, bf16[8,256,256]{2,1,0:T(8,128)(2,1)...) custom-call(s32[1]{0:T(128)S(6)} %copy.46.refs_0_, ...), custom_call_target="tpu_custom_call" | custom-call | tf_op jit(solution)/shard_map/forward_kernel/pallas_call | solution.py:874
  166.1 8.3 %multiply_convert_fusion = (bf16[1024,1024]{1,0:T(8,128)(2,1)S(1)}, f32[1024,1024]{1,0:T(8,128)S(1)}) fusion(f32[1024]{0:T(1024)S(1)} %convert_element_type.40, bf16[1024,2048]{1,0:T(8,128)(2,1)} %bitcast.25, bf16[2048,1024]{1,0:T(8,128)(2,1)} %bitcast.24), kind=kOutput, calls=%fused_computation.10 | convolution fusion | flops 4301258752 | bytes 14684160 | tf_op jit(solution)/shard_map/dot_general | solution.py:891
  174.5 7.0 %convert_reduce_fusion = (f32[1024]{0:T(1024)S(1)}, bf16[1024,1024]{1,0:T(8,128)(2,1)}) fusion(f32[1024,1024]{1,0:T(8,128)S(1)} %get-tuple-element.70, f32[1024]{0:T(1024)S(1)} %convert_element_type.40, bf16[1024,2048]{1,0:T(8,128)(2,1)S(1)} %bitcast.41, bf16[1024,2048]{1,0:T(8,128)(2,1)S(1)} %copy-done.1), kind=kOutput, calls=%fused_computation.9 | convolution fusion | flops 4308597760 | bytes 14688256 | tf_op jit(solution)/shard_map/tc,rc->tr/dot_general | solution.py:895
  181.5 6.2 %convolution_convert_fusion.refs_5_ = bf16[1024,2048]{1,0:T(8,128)(2,1)} fusion(bf16[1024,1024]{1,0:T(8,128)(2,1)S(1)} %get-tuple-element.69.refs_1_, bf16[1024,2048]{1,0:T(8,128)(2,1)S(1)} %bitcast.42), kind=kOutput, calls=%fused_computation.12 | convolution fusion | flops 4297064448 | bytes 10485760 | tf_op jit(solution)/shard_map/tr,tc->rc/dot_general | solution.py:899
  187.7 0.6 concatenate.10.refs_20_
  188.3 319.8 %final_kernel.1 = (bf16[128,2048]{1,0:T(8,128)(2,1)}, bf16[128,2048]{1,0:T(8,128)(2,1)}, f32[16,256]{1,0:T(8,128)}, bf16[3072,2048]{1,0:T(8,128)(2,1)}) custom-call(bf16[1024,1024]{1,0:T(8,128)(2,1)} %get-tuple-element.72.refs_0_, bf16[1024,1024]{1,0:T(8,128)(2,1)} %copy-done.2, bf16[8,128,2048]{2,1,0:T(8,128)(2,1)} %get-tuple-element.36.refs_2_, ...), custom_call_target="tpu_custom_call" | custom-call | tf_op jit(solution)/shard_map/final_kernel/pallas_call | solution.py:874
  508.2 0.7 slice_bitcast_fusion
  508.9 1.5 fusion.7
  511.0 7.7 %slice_convert_fusion = f32[1024,2048]{1,0:T(8,128)} fusion(bf16[3072,2048]{1,0:T(8,128)(2,1)} %get-tuple-element.52), kind=kLoop, calls=%fused_computation.8 | loop fusion | flops 2097152 | bytes 12582912 | tf_op jit(solution)/shard_map/convert_element_type | solution.py:1066
  518.7 1.2 copy-done
  519.9 3.6 fusion.6
  523.5 3.8 maximum_convert_fusion
  527.3 0.8 copy.47
  528.1 0.8 copy.48
  (14 shorter events, 0.6 us)
Async XLA Ops:
  166.1 8.3 %copy-start.1 = (bf16[1024,2048]{1,0:T(8,128)(2,1)S(1)}, bf16[1024,2048]{1,0:T(8,128)(2,1)}, u32[]{:S(2)}) copy-start(bf16[1024,2048]{1,0:T(8,128)(2,1)} %refs_4_.3) | copy-start | bytes 12582916
  166.1 8.3 %copy-start.5 = (bf16[8,128,2048]{2,1,0:T(8,128)(2,1)S(1)}, bf16[8,128,2048]{2,1,0:T(8,128)(2,1)}, u32[]{:S(2)}) copy-start(bf16[8,128,2048]{2,1,0:T(8,128)(2,1)} %get-tuple-element.35) | copy-start | bytes 12582916
  174.4 7.1 %copy-start.2 = (bf16[1024,1024]{1,0:T(8,128)(2,1)}, bf16[1024,1024]{1,0:T(8,128)(2,1)S(1)}, u32[]{:S(2)}) copy-start(bf16[1024,1024]{1,0:T(8,128)(2,1)S(1)} %get-tuple-element.69.refs_1_) | copy-start | bytes 6291460
  511.0 8.9 %copy-start = (bf16[3072,2048]{1,0:T(8,128)(2,1)S(1)}, bf16[3072,2048]{1,0:T(8,128)(2,1)}, u32[]{:S(2)}) copy-start(bf16[3072,2048]{1,0:T(8,128)(2,1)} %get-tuple-element.52) | copy-start | bytes 37748740
  523.5 3.9 copy-start.4
  523.5 4.6 copy-start.3

commit v6 on v5

--- a/solution.py
+++ b/solution.py
@@ -316,11 +316,14 @@
 
 def forward_kernel(sizes, head, *refs):
     group, reps = sizes
-    length_ref, x_ref, cot_ref, vectors, q_ref, k_ref, v_ref, u_ref, wo = refs[:9]
-    nrm, small_all, wq, wk, wv, wu, queries, keys, values, p_ref, ctx, mid, second, mix = refs[9:23]
-    work = refs[23:]
+    length_ref, x_ref, cot_ref, q_ref, k_ref, v_ref, u_ref, wo, vectors = refs[:9]
+    refs = refs[9:]
+    (nrm_out, small_all, wq_out, wk_out, wv_out, wu, queries, keys, values, p_ref, ctx) = refs[:11]
+    mid, second, mix = refs[11:14]
+    work = refs[14:]
     part, small_ref = work[2:4]
     spread_sems = work[4:6]
+    nrm, wq, wk, wv = work[6:10]
     me, rep = lax.axis_index("shard"), lax.axis_index("rep")
     net = Net(*work[-2:])
     masks = shard_masks(group)
@@ -388,6 +391,10 @@
             if row is not None:
                 res = res + vectors[row : row + 1]
             low[pl.ds(b * rows, 2 * rows)] = res.astype(BF)
+    leaving = [
+        net.own(a, b)
+        for a, b in ((nrm, nrm_out), (wq, wq_out), (wk, wk_out), (wv, wv_out))
+    ]
     gmix = Gather(net, mix, masks)
     red = Reduce(net, part, work[:2], masks)
     order = [h ^ 1 for h in red.sequence] + red.sequence
@@ -459,6 +466,8 @@
     gather.end()
     if spread.reps > 1:
         spread.finish()
+    for copy in leaving:
+        copy.wait()
     net.finish()
 
 
@@ -927,19 +936,20 @@
     head = width // HEADS
     scale = 1.0 / math.sqrt(head)
     me = lax.axis_index("shard")
-    vectors = jnp.concatenate(
-        [
-            first_gain,
-            first_shift,
-            out_bias,
-            second_gain,
-            second_shift,
-            down_bias,
-            query_bias,
-            value_bias,
-        ]
+    vectors = (
+        first_gain,
+        first_shift,
+        out_bias,
+        second_gain,
+        second_shift,
+        down_bias,
+        query_bias,
+        value_bias,
     )
-    vectors = vectors.reshape(8, g).astype(F32)
+    at = lax.broadcasted_iota(jnp.int32, (8, g), 0)
+    stacked = jnp.zeros((8, g), F32)
+    for i, a in enumerate(vectors):
+        stacked = jnp.where(at == i, a.astype(F32)[None], stacked)
     x, cot = block_input[0], cotangent[0]
     blocks = (group, rows, width)
     masks = shard_masks(group)
@@ -967,21 +977,23 @@
         ],
         work
         + [pltpu.VMEM(blocks, BF), pltpu.VMEM((8, g), F32)]
-        + [pltpu.SemaphoreType.DMA((2 * reps,))] * 2,
+        + [pltpu.SemaphoreType.DMA((2 * reps,))] * 2
+        + [pltpu.VMEM(blocks, BF)]
+        + [pltpu.VMEM((group, g, g), BF)] * 3,
         320,
         (
             lengths,
             x,
             cot,
-            vectors,
             query_weight,
             key_weight,
             value_weight,
             up_weight,
             out_weight,
+            stacked,
         ),
-        (4, 5, 6, 7),
-        (),
+        (3, 4, 5, 6),
+        (0, 2, 3, 4),
         (0,),
     )
     flat = lambda a: a.reshape(-1, a.shape[-1])

time: 537 us -> 534 us (level)
  local copies, waits for them, and re-layouts: 13.5 us -> 6.23 us
  other arithmetic: 15.8 us -> 21.8 us
    unnamed x23 -> x16, local copies, waits for them, and re-layouts: 9.92 us -> 4.11 us
where the time goes in v6:
time: 534 us; the launch traced here: 526 us
  Pallas kernels  474 us (89%)
  other arithmetic  21.8 us (4%)
  matrix products  21.6 us (4%)
  local copies, waits for them, and re-layouts  6.23 us (1%)
    pallas_call x2, Pallas kernels, call(): pl.pallas_call(functools.partial(body, *sizes), out_shape=[jax.ShapeDtype...  474 us

profile of v6, /device:TPU:0, one launch (start us, length us, event | category | flops | bytes accessed | tf_op | source)
XLA Modules:
  0.0 525.7 jit_solution(3530719543676662627)
XLA Ops:
  1.3 0.7 convert_element_type.64
  2.0 0.7 convert_element_type.63
  2.6 0.7 convert_element_type.58
  3.3 0.7 convert_element_type.57
  3.9 0.7 convert_element_type.62
  4.6 0.7 convert_element_type.61
  5.2 0.7 convert_element_type.60
  5.9 0.7 convert_element_type.59
  6.6 0.7 select_select_fusion.refs_8_
  7.3 0.7 convert_element_type.65
  8.0 154.6 %forward_kernel.1 = (bf16[8,128,2048]{2,1,0:T(8,128)(2,1)}, f32[8,2048]{1,0:T(8,128)}, bf16[8,256,256]{2,1,0:T(8,128)(2,1)}, bf16[8,256,256]{2,1,0:T(8,128)(2,1)...) custom-call(s32[1]{0:T(128)S(6)} %copy.38.refs_0_, ...), custom_call_target="tpu_custom_call" | custom-call | tf_op jit(solution)/shard_map/forward_kernel/pallas_call | solution.py:883
  162.6 8.1 %multiply_convert_fusion = (bf16[1024,1024]{1,0:T(8,128)(2,1)S(1)}, f32[1024,1024]{1,0:T(8,128)S(1)}) fusion(f32[1024]{0:T(1024)S(1)} %convert_element_type.65, bf16[1024,2048]{1,0:T(8,128)(2,1)} %bitcast.25, bf16[2048,1024]{1,0:T(8,128)(2,1)} %bitcast.24), kind=kOutput, calls=%fused_computation.10 | convolution fusion | flops 4301258752 | bytes 14684160 | tf_op jit(solution)/shard_map/dot_general | solution.py:900
  170.7 7.3 %convert_reduce_fusion = (f32[1024]{0:T(1024)S(1)}, bf16[1024,1024]{1,0:T(8,128)(2,1)}) fusion(f32[1024,1024]{1,0:T(8,128)S(1)} %get-tuple-element.70, f32[1024]{0:T(1024)S(1)} %convert_element_type.65, bf16[1024,2048]{1,0:T(8,128)(2,1)S(1)} %bitcast.41, bf16[1024,2048]{1,0:T(8,128)(2,1)S(1)} %copy-done.1), kind=kOutput, calls=%fused_computation.9 | convolution fusion | flops 4308597760 | bytes 14688256 | tf_op jit(solution)/shard_map/tc,rc->tr/dot_general | solution.py:904
  178.0 6.2 %convolution_convert_fusion.refs_5_ = bf16[1024,2048]{1,0:T(8,128)(2,1)} fusion(bf16[1024,1024]{1,0:T(8,128)(2,1)S(1)} %get-tuple-element.69.refs_1_, bf16[1024,2048]{1,0:T(8,128)(2,1)S(1)} %bitcast.42), kind=kOutput, calls=%fused_computation.12 | convolution fusion | flops 4297064448 | bytes 10485760 | tf_op jit(solution)/shard_map/tr,tc->rc/dot_general | solution.py:908
  184.2 0.6 concatenate.6.refs_20_
  184.8 319.7 %final_kernel.1 = (bf16[128,2048]{1,0:T(8,128)(2,1)}, bf16[128,2048]{1,0:T(8,128)(2,1)}, f32[16,256]{1,0:T(8,128)}, bf16[3072,2048]{1,0:T(8,128)(2,1)}) custom-call(bf16[1024,1024]{1,0:T(8,128)(2,1)} %get-tuple-element.72.refs_0_, bf16[1024,1024]{1,0:T(8,128)(2,1)} %copy-done.2, bf16[8,128,2048]{2,1,0:T(8,128)(2,1)} %get-tuple-element.36.refs_2_, ...), custom_call_target="tpu_custom_call" | custom-call | tf_op jit(solution)/shard_map/final_kernel/pallas_call | solution.py:883
  504.6 0.7 slice_bitcast_fusion
  505.3 1.5 fusion.7
  507.4 7.7 %slice_convert_fusion = f32[1024,2048]{1,0:T(8,128)} fusion(bf16[3072,2048]{1,0:T(8,128)(2,1)} %get-tuple-element.52), kind=kLoop, calls=%fused_computation.8 | loop fusion | flops 2097152 | bytes 12582912 | tf_op jit(solution)/shard_map/convert_element_type | solution.py:1078
  515.0 1.2 copy-done
  516.2 3.6 fusion.6
  519.9 3.8 maximum_convert_fusion
  523.7 0.8 copy.39
  524.5 0.8 copy.40
  (17 shorter events, 0.7 us)
Async XLA Ops:
  162.6 8.1 %copy-start.1 = (bf16[1024,2048]{1,0:T(8,128)(2,1)S(1)}, bf16[1024,2048]{1,0:T(8,128)(2,1)}, u32[]{:S(2)}) copy-start(bf16[1024,2048]{1,0:T(8,128)(2,1)} %refs_4_.3) | copy-start | bytes 12582916
  162.6 8.1 %copy-start.5 = (bf16[8,128,2048]{2,1,0:T(8,128)(2,1)S(1)}, bf16[8,128,2048]{2,1,0:T(8,128)(2,1)}, u32[]{:S(2)}) copy-start(bf16[8,128,2048]{2,1,0:T(8,128)(2,1)} %get-tuple-element.35) | copy-start | bytes 12582916
  170.7 7.3 %copy-start.2 = (bf16[1024,1024]{1,0:T(8,128)(2,1)}, bf16[1024,1024]{1,0:T(8,128)(2,1)S(1)}, u32[]{:S(2)}) copy-start(bf16[1024,1024]{1,0:T(8,128)(2,1)S(1)} %get-tuple-element.69.refs_1_) | copy-start | bytes 6291460
  507.4 8.9 %copy-start = (bf16[3072,2048]{1,0:T(8,128)(2,1)S(1)}, bf16[3072,2048]{1,0:T(8,128)(2,1)}, u32[]{:S(2)}) copy-start(bf16[3072,2048]{1,0:T(8,128)(2,1)} %get-tuple-element.52) | copy-start | bytes 37748740
  519.9 3.9 copy-start.4
  519.9 4.6 copy-start.3
